TPU v7x, 256 devices: a whole 4x4x8 slice. The times are simulated.
256 devices in a mesh: rows: 64 (over y, z, core), pairs: 4 (over x).
Axes of the slice: x: 4, y: 4, z: 8, core: 2. Of those that a mesh axis runs over, the one named last changes fastest.
Arguments:
- factor_rows: bfloat16 [32768, 256], P('rows'), may hold values from -6 to 6
- row_side_probes: bfloat16 [32768, 128], P('rows'), may hold values from -6 to 6
- factor_cols: bfloat16 [32768, 256], P(('rows', 'pairs')), may hold values from -0.375 to 0.375
- probe_cols: bfloat16 [32768, 128], P(('rows', 'pairs')), may hold values from -6 to 6
- pair_blocks: int32 [64, 64], P('rows'), may hold values from 0 to 63, as said below
- pair_count: int32 [64], P('rows'), may hold values from 32 to 64, as said below
Outputs:
- row_sketch: float32 [32768, 128], P(('rows', 'pairs'))
- col_sketch: float32 [32768, 128], P(('rows', 'pairs'))
- sketch_gram: float32 [128, 128], replicated
Inputs may be any that keep to these rules, and one draw needn't show every extreme that they name: `pair_blocks`: the entries of one row are distinct. `pair_count`: some row block has exactly 64 pairs.
All inputs are finite; a program needn't handle non-finite values.
Results may differ from a plain program's by a relative error of at most 0.003.
Values may be sent and summed in bfloat16 or wider, within the bound.
No kernel may reach another device: no remote copies, remote signals or barrier semaphores. Data moves between devices by JAX's collectives and lax.ppermute only.
A program may use at most 64 MiB of HBM per device.

v0:
```python
import math

import jax
import jax.numpy as jnp
from jax import lax
from jax.sharding import PartitionSpec as P


def shards(factor_rows, row_side_probes, factor_cols, probe_cols, pair_blocks, pair_count):
    row_devices = lax.axis_size("rows")
    block_rows = factor_rows.shape[0]
    sub_rows = factor_cols.shape[0]
    rank_width = factor_rows.shape[1]
    probe_width = row_side_probes.shape[1]
    sketch_scale = 1.0 / math.sqrt(row_devices * block_rows)
    gathered_factor, gathered_probe = (
        lax.all_gather(factor_cols, "rows", axis=0, tiled=True),
        lax.all_gather(probe_cols, "rows", axis=0, tiled=True),
    )
    gathered_factor = gathered_factor.reshape(row_devices, sub_rows, rank_width)
    gathered_probe = gathered_probe.reshape(row_devices, sub_rows, probe_width)
    targets = pair_blocks[0]
    live_count = pair_count[0]

    def one_turn(turn_index, carry):
        row_accumulator, col_acc = carry
        first_slot = 2 * turn_index
        second_slot = jnp.minimum(first_slot + 1, row_devices - 1)
        second_live = first_slot + 1 < live_count
        first_block = targets[first_slot]
        second_block = targets[second_slot]
        factor_pair = jnp.concatenate(
            [gathered_factor[first_block], gathered_factor[second_block]], 0
        )
        gaussian_draw_duo = jnp.concatenate(
            [gathered_probe[first_block], gathered_probe[second_block]], 0
        )
        kernel_weights = lax.dot_general(
            factor_rows, factor_pair, (((1,), (1,)), ((), ())), preferred_element_type=jnp.float32
        )
        column_keep = jnp.concatenate(
            [jnp.ones((sub_rows,), jnp.bool_), jnp.full((sub_rows,), second_live)]
        )
        nearness_kernel = jnp.where(
            column_keep[None, :], jnp.log(jnp.maximum(4.0 * kernel_weights, 1.0)), 0.0
        ).astype(jnp.bfloat16)
        row_accumulator = row_accumulator + jnp.dot(
            nearness_kernel, gaussian_draw_duo, preferred_element_type=jnp.float32
        )
        vertical_sketch_entries = lax.dot_general(
            nearness_kernel,
            row_side_probes,
            (((0,), (0,)), ((), ())),
            preferred_element_type=jnp.float32,
        )
        col_acc = col_acc.at[first_block].add(vertical_sketch_entries[:sub_rows])
        col_acc = col_acc.at[second_block].add(vertical_sketch_entries[sub_rows:])
        return (row_accumulator, col_acc)

    row_zero = jnp.zeros((block_rows, probe_width), jnp.float32)
    col_zero = jnp.zeros((row_devices, sub_rows, probe_width), jnp.float32)
    turn_total = (live_count + 1) // 2
    row_accumulator, col_acc = lax.fori_loop(0, turn_total, one_turn, (row_zero, col_zero))
    row_sketch = (
        lax.psum_scatter(row_accumulator, "pairs", scatter_dimension=0, tiled=True) * sketch_scale
    )
    own_start = lax.axis_index("pairs") * sub_rows
    own_probe = lax.dynamic_slice_in_dim(row_side_probes, own_start, sub_rows, 0)
    gram_terms = jnp.dot(
        own_probe.astype(jnp.float32).T, row_sketch, precision=lax.Precision.HIGHEST
    )
    sketch_gram = lax.psum(gram_terms, ("rows", "pairs")) / math.sqrt(row_devices * block_rows)
    col_sum = lax.psum_scatter(col_acc, "rows", scatter_dimension=0, tiled=True)
    col_sketch = col_sum.reshape(sub_rows, probe_width) * sketch_scale
    return (row_sketch, col_sketch, sketch_gram)


def solution(mesh):
    return jax.shard_map(
        shards,
        mesh=mesh,
        in_specs=(
            P("rows", None),
            P("rows", None),
            P(("rows", "pairs"), None),
            P(("rows", "pairs"), None),
            P("rows", None),
            P("rows"),
        ),
        out_specs=(P(("rows", "pairs"), None), P(("rows", "pairs"), None), P()),
        check_vma=False,
    )
```

profile of v0, /device:TPU:1, one launch (start us, length us, event | category | flops | bytes accessed | tf_op | source)
XLA Modules:
  0.0 988.1 jit_solution(11318563951729065293)
XLA Ops:
  9.4 83.0 %all-gather.5.cloned.1.call-done = bf16[8192,128]{1,0:T(8,128)(2,1)} async-done(((bf16[128,128]{1,0:T(8,128)(2,1)}), bf16[8192,128]{1,0:T(8,128)(2,1)}) %all-gather.5.cloned.1.call-update) | async-done | bytes 2097168 | tf_op jit(solution)/shard_map/all_gather | solution.py:18
  92.4 79.5 %all-gather.3.cloned.1.call-done = bf16[8192,256]{1,0:T(8,128)(2,1)} async-done(((bf16[128,256]{1,0:T(8,128)(2,1)}), bf16[8192,256]{1,0:T(8,128)(2,1)}) %all-gather.3.cloned.1.call-update) | async-done | bytes 4194320 | tf_op jit(solution)/shard_map/all_gather | solution.py:17
  171.9 2.5 broadcast_in_dim.23
  174.4 300.6 %while.14 = (s32[]{:T(128)}, f32[512,128]{1,0:T(8,128)S(1)}, f32[64,128,128]{2,1,0:T(8,128)}, s32[]{:T(128)}, s32[]{:T(128)}, /*index=5*/s32[64]{0:T(128)S(1)}, ...) while((s32[]{:T(128)}, f32[512,128]{1,0:T(8,128)S(1)}, ...), condition=%wide.region_3.4_spmd, body=%wide.region_0.3_spmd.sunk | while | flops 135266352 | bytes 2821286 | solution.py:63
  184.9 2.1 fusion.45
  197.4 2.1 fusion.45
  209.9 2.1 fusion.45
  235.0 2.1 fusion.45
  247.5 2.1 fusion.45
  272.5 2.1 fusion.45
  285.1 2.1 fusion.45
  335.1 2.1 fusion.45
  347.6 2.1 fusion.45
  372.7 2.1 fusion.45
  385.2 2.1 fusion.45
  397.7 2.1 fusion.45
  410.3 2.1 fusion.45
  422.8 2.1 fusion.45
  447.8 2.1 fusion.45
  460.4 2.1 fusion.45
  472.9 2.1 fusion.45
  475.8 118.0 %reduce-scatter.3.cloned.1.call-done = f32[128,128]{1,0:T(8,128)} async-done(((f32[512,128]{1,0:T(8,128)}), f32[128,128]{1,0:T(8,128)}) %reduce-scatter.3.cloned.1.call-update) | async-done | bytes 65552 | tf_op jit(solution)/shard_map/reduce_scatter | solution.py:65
  596.1 244.5 %all-reduce.3.cloned.1.call-done = f32[128,128]{1,0:T(8,128)} async-done(((f32[128,128]{1,0:T(8,128)}), f32[128,128]{1,0:T(8,128)}) %all-reduce.3.cloned.1.call-update) | async-done | bytes 65552 | tf_op jit(solution)/shard_map/psum | solution.py:72
  842.1 138.0 %reduce-scatter.5.cloned.1.call-done = f32[1,128,128]{2,1,0:T(8,128)} async-done(((f32[64,128,128]{2,1,0:T(8,128)}), f32[1,128,128]{2,1,0:T(8,128)}) %reduce-scatter.5.cloned.1.call-update) | async-done | bytes 65552 | tf_op jit(solution)/shard_map/reduce_scatter | solution.py:73
  (274 shorter events, 162.9 us)
Async XLA Ops:
  7.2 167.3 %copy-start.4 = (s32[3]{0:T(128)S(1)}, s32[3]{0:T(128)}, u32[]{:S(2)}) copy-start(s32[3]{0:T(128)} %constant.82.clone.1) | copy-start | bytes 40
  7.2 167.2 %copy-start.3 = (s32[1,64]{1,0:T(1,128)S(1)}, s32[1,64]{1,0:T(1,128)}, u32[]{:S(2)}) copy-start(s32[1,64]{1,0:T(1,128)} %param.16) | copy-start | bytes 772
  7.2 167.2 %copy-start.5 = (bf16[512,256]{1,0:T(8,128)(2,1)S(1)}, bf16[512,256]{1,0:T(8,128)(2,1)}, u32[]{:S(2)}) copy-start(bf16[512,256]{1,0:T(8,128)(2,1)} %param.12) | copy-start | bytes 786436
  7.2 167.2 %copy-start.1 = (bf16[512,128]{1,0:T(8,128)(2,1)S(1)}, bf16[512,128]{1,0:T(8,128)(2,1)}, u32[]{:S(2)}) copy-start(bf16[512,128]{1,0:T(8,128)(2,1)} %param.13) | copy-start | bytes 393220
  7.2 85.2 %all-gather.5.cloned.1.call-start = ((), (), s32[]{:S(2)}) async-start(), calls=%async_computation.3 | async-start | bytes 2129920 | tf_op jit(solution)/shard_map/all_gather | solution.py:18
  7.9 164.0 %all-gather.3.cloned.1.call-start = ((), (), s32[]{:S(2)}) async-start(), calls=%async_computation.2 | async-start | bytes 4259840 | tf_op jit(solution)/shard_map/all_gather | solution.py:17
  8.7 585.1 %reduce-scatter.3.cloned.1.call-start = ((), (), s32[]{:S(2)}) async-start(), calls=%async_computation.4 | async-start | bytes 327680 | tf_op jit(solution)/shard_map/reduce_scatter | solution.py:65
  475.0 0.7 copy-start
  475.7 364.9 %all-reduce.3.cloned.1.call-start = ((), (), s32[]{:S(2)}) async-start(), calls=%async_computation.6 | async-start | bytes 131072 | tf_op jit(solution)/shard_map/psum | solution.py:72
  594.6 387.0 %copy-start.2 = (f32[128,128]{1,0:T(8,128)}, f32[128,128]{1,0:T(8,128)S(1)}, u32[]{:S(2)}) copy-start(f32[128,128]{1,0:T(8,128)S(1)} %broadcast_multiply_fusion.1) | copy-start | bytes 196612
  595.5 384.6 %reduce-scatter.5.cloned.1.call-start = ((), (), s32[]{:S(2)}) async-start(), calls=%async_computation.5 | async-start | bytes 4259840 | tf_op jit(solution)/shard_map/reduce_scatter | solution.py:73
Sparse Core Ops, SparseCore 0:
  10.8 81.5 all-gather.4
  95.2 76.6 all-gather.2
  475.8 117.8 reduce-scatter.2
  600.6 239.9 all-reduce.2
  845.2 134.8 reduce-scatter.4
where the time goes:
time: 1000 us; the launch traced here: 988 us
  waiting for transfers between devices  665 us (66%)
  other arithmetic  121 us (12%)
  loops' own time  109 us (11%)
  local copies, waits for them, and re-layouts  58.6 us (6%)
  matrix products  19.8 us (2%)
  between operations  14.5 us (1%)
    psum x1, waiting for transfers between devices, shards(): lax.psum(gram_terms, ('rows', 'pairs'))  245 us
    reduce_scatter x1, waiting for transfers between devices, shards(): col_sum = lax.psum_scatter(col_acc, 'rows', scatter_dimension=0, tiled=True)  138 us
    reduce_scatter x1, waiting for transfers between devices, shards(): lax.psum_scatter(row_accumulator, 'pairs', scatter_dimension=0, tiled=True)  118 us
    another operation x1, loops' own time, shards(): lax.fori_loop(0, turn_total, one_turn, (row_zero, col_zero))  109 us
    all_gather x1, waiting for transfers between devices, shards(): lax.all_gather(probe_cols, 'rows', axis=0, tiled=True)  83 us
    all_gather x1, waiting for transfers between devices, shards(): lax.all_gather(factor_cols, 'rows', axis=0, tiled=True)  79.5 us
    scatter-add x24, other arithmetic, one_turn(): col_acc = col_acc.at[second_block].add(vertical_sketch_entries[sub_rows:])  50.5 us
    scatter-add x24, other arithmetic, one_turn(): col_acc = col_acc.at[first_block].add(vertical_sketch_entries[:sub_rows])  48.7 us
  transfers between devices with their start and end apart: 5, of which 5 were waited for; matrix products, arithmetic and copies ran while one was open for 0% of the time, Pallas kernels for 0%

commit v1 on v0

v1 whole, which is shorter than its diff:
```python
import math

import jax
import jax.numpy as jnp
from jax import lax
from jax.experimental import pallas as pl
from jax.experimental.pallas import tpu as pltpu
from jax.sharding import Mesh, PartitionSpec as P

BF16 = jnp.bfloat16
F32 = jnp.float32
Y, Z, C, X = 4, 8, 2, 4
BLOCK, SUB, RANK, PROBES = 512, 128, 256, 128
WIDTH = RANK + PROBES
MASK_ROWS = 16
HALF = Z * SUB
NODES = Y * Z * C * BLOCK


def tile_kernel(scale_ref, rows_ref, own_ref, other_ref, row_ref, keep_ref, send_ref, row_acc, col_acc):
    def step(turn, _):
        block = turn // 2
        half = turn - 2 * block

        def run(cols_ref):
            left = rows_ref[block, 0:BLOCK, 0:RANK]
            left_probes = rows_ref[block, 0:BLOCK, RANK:WIDTH]
            right = jnp.concatenate(
                [cols_ref[s, :, 0:RANK] * scale_ref[block, half * Z + s].astype(BF16) for s in range(Z)], 0
            )
            right_probes = cols_ref[:, :, RANK:WIDTH].reshape(HALF, PROBES)
            scores = lax.dot_general(left, right, (((1,), (1,)), ((), ())), preferred_element_type=F32)
            proximity = jnp.log(jnp.maximum(scores, 1.0)).astype(BF16)
            row_part = jnp.dot(proximity, right_probes, preferred_element_type=F32)
            col_part = lax.dot_general(left_probes, proximity, (((0,), (0,)), ((), ())), preferred_element_type=F32)

            @pl.when(half == 0)
            def _():
                row_acc[block] = row_part

            @pl.when(half == 1)
            def _():
                row_acc[block] += row_part

            @pl.when(block == 0)
            def _():
                col_acc[half] = col_part

            @pl.when(block > 0)
            def _():
                col_acc[half] += col_part

        @pl.when(half == 0)
        def _():
            run(own_ref)

        @pl.when(half == 1)
        def _():
            run(other_ref)

        return 0

    lax.fori_loop(0, 2 * Y, step, 0)
    gram = jnp.zeros((PROBES, PROBES), F32)
    for block in range(Y):
        total = row_acc[block]
        high = total.astype(BF16)
        low = (total - high.astype(F32)).astype(BF16)
        row_ref[block] = high
        left_probes = rows_ref[block, 0:BLOCK, RANK:WIDTH]
        for part in (high, low):
            gram += lax.dot_general(left_probes, part, (((0,), (0,)), ((), ())), preferred_element_type=F32)
    for s in range(Z):
        keep_ref[s] = col_acc[0, :, s * SUB : (s + 1) * SUB]
        send_ref[s] = col_acc[1, :, s * SUB : (s + 1) * SUB]
    keep_ref[Z] = gram
    send_ref[Z] = gram


def split(value):
    high = value.astype(BF16)
    low = (value - high.astype(F32)).astype(BF16)
    return high, low


def shards(factor_rows, row_side_probes, factor_cols, probe_cols, pair_blocks, pair_count):
    scale = 1.0 / math.sqrt(NODES)
    y, c = lax.axis_index("y"), lax.axis_index("c")
    live = lax.iota(jnp.int32, Y * Z * C)[:, None] < pair_count[0]
    hits = (pair_blocks[0][:, None] == lax.iota(jnp.int32, Y * Z * C)[None, :]) & live
    used = jnp.any(hits, axis=0).astype(BF16)
    used_rows = jnp.pad(used[None, :], ((0, MASK_ROWS - 1), (0, WIDTH - Y * Z * C)))
    row_load = jnp.concatenate([jnp.concatenate([factor_rows, row_side_probes], 1), used_rows], 0)
    all_rows = lax.all_gather(row_load, "y", axis=0, tiled=False)

    col_load = jnp.concatenate([factor_cols, probe_cols], 1)
    own_cols = lax.all_to_all(
        jnp.broadcast_to(col_load[None], (Z, SUB, WIDTH)), "z", split_axis=0, concat_axis=0, tiled=True
    )
    other_cols = lax.ppermute(own_cols, "c", [(0, 1), (1, 0)])

    flags = lax.dynamic_slice_in_dim(all_rows[:, BLOCK, : Y * Z * C], y * Z * C, Z * C, 1)
    flags = 4.0 * flags.astype(F32).reshape(Y, Z, C)
    flags = jnp.stack([lax.dynamic_index_in_dim(flags, c, 2, False), lax.dynamic_index_in_dim(flags, 1 - c, 2, False)], 1)
    flags = flags.reshape(Y, C * Z)

    vmem = pl.BlockSpec(memory_space=pltpu.VMEM)
    row_part, keep, send = pl.pallas_call(
        tile_kernel,
        out_shape=[
            jax.ShapeDtypeStruct((Y, BLOCK, PROBES), BF16),
            jax.ShapeDtypeStruct((Z + 1, PROBES, SUB), F32),
            jax.ShapeDtypeStruct((Z + 1, PROBES, SUB), F32),
        ],
        in_specs=[pl.BlockSpec(memory_space=pltpu.SMEM), vmem, vmem, vmem],
        out_specs=[vmem, vmem, vmem],
        scratch_shapes=[pltpu.VMEM((Y, BLOCK, PROBES), F32), pltpu.VMEM((C, PROBES, HALF), F32)],
        compiler_params=pltpu.CompilerParams(vmem_limit_bytes=40 * 2**20),
        name="tiles",
    )(flags, all_rows, own_cols, other_cols)

    chip = keep + lax.ppermute(send, "c", [(0, 1), (1, 0)])
    gram_half = lax.dynamic_index_in_dim(chip[Z].reshape(C, X, 16, PROBES), c, 0, False)
    gram_half = jnp.broadcast_to(gram_half[None], (Y, X, 16, PROBES)).reshape(Y * X, 16, PROBES)
    row_load = jnp.concatenate([row_part.reshape(Y * X, SUB, PROBES), *split(gram_half)], 1)
    row_got = lax.all_to_all(row_load, ("y", "x"), split_axis=0, concat_axis=0, tiled=True)
    row_sum = jnp.sum(row_got.astype(F32), 0)
    row_sketch = row_sum[:SUB] * scale
    gram_piece = row_sum[SUB : SUB + 16] + row_sum[SUB + 16 :]

    gram_all_z = jnp.broadcast_to(jnp.concatenate(split(gram_piece), 0)[None], (Z, 32, PROBES))
    col_load = jnp.concatenate([chip[:Z].astype(BF16), gram_all_z], 1)
    col_got = lax.all_to_all(col_load, "z", split_axis=0, concat_axis=0, tiled=True)
    col_sum = jnp.sum(col_got.astype(F32), 0)
    col_sketch = col_sum[:SUB].T * scale
    gram_piece = (col_sum[SUB : SUB + 16] + col_sum[SUB + 16 :]) / NODES
    sketch_gram = lax.all_gather(gram_piece, ("c", "x"), axis=0, tiled=True)
    return (row_sketch, col_sketch, sketch_gram)


def solution(mesh):
    grid = Mesh(mesh.devices.reshape(Y, Z, C, X), ("y", "z", "c", "x"))
    rows, subs = ("y", "z", "c"), ("y", "z", "c", "x")
    return jax.shard_map(
        shards,
        mesh=grid,
        in_specs=(P(rows, None), P(rows, None), P(subs, None), P(subs, None), P(rows, None), P(rows)),
        out_specs=(P(subs, None), P(subs, None), P()),
        check_vma=False,
    )
```

time: 1000 us -> 128 us (0.13); the launches traced: 988 us -> 127 us
  waiting for transfers between devices: 665 us -> 25 us
  other arithmetic: 121 us -> 6.05 us
  loops' own time: 109 us -> 0 us
  local copies, waits for them, and re-layouts: 58.6 us -> 3.98 us
  blocking collectives: 0 us -> 54.5 us
  matrix products: 19.8 us -> 0 us
  starting transfers between devices: 0.2 us -> 14 us
    reduce_scatter x2 -> x0, waiting for transfers between devices: 256 us -> none  [the longest x1 138 us: shards(): col_sum = lax.psum_scatter(col_acc, 'rows', scatter_dimension=0, tiled=True)]
    psum x1 -> x0, waiting for transfers between devices: 245 us -> none  [shards(): lax.psum(gram_terms, ('rows', 'pairs'))]
    all_gather x2 -> x1, waiting for transfers between devices: 163 us -> 0.01 us  [shards(): all_rows = lax.all_gather(row_load, 'y', axis=0, tiled=False)]
    another operation x1 -> x0, loops' own time: 109 us -> none  [shards(): lax.fori_loop(0, turn_total, one_turn, (row_zero, col_zero))]
    scatter-add x48 -> x0, other arithmetic: 99.2 us -> none  [the longest x24 50.5 us: one_turn(): col_acc = col_acc.at[second_block].add(vertical_sketch_entries[sub_rows:])]
    squeeze x48 -> x0, local copies, waits for them, and re-layouts: 40.2 us -> none  [the longest x24 21.3 us: one_turn(): gathered_factor[first_block]]
    all_to_all x0 -> x1, blocking collectives: none -> 30.4 us  [shards(): lax.all_to_all(jnp.broadcast_to(col_load[None], (Z, SUB, WIDTH)), 'z', sp...]
    all_gather x0 -> x1, blocking collectives: none -> 24.1 us  [shards(): sketch_gram = lax.all_gather(gram_piece, ('c', 'x'), axis=0, tiled=True)]
  transfers between devices with their start and end apart: 5 -> 5, of which waited for: 5 -> 4; matrix products, arithmetic and copies ran while one was open for 0% -> 2% of each run, Pallas kernels for 0% -> 0%
where the time goes in v1:
time: 128 us; the launch traced here: 127 us
  blocking collectives  54.5 us (43%)
  waiting for transfers between devices  25 us (20%)
  between operations  14.8 us (12%)
  starting transfers between devices  14 us (11%)
  Pallas kernels  8.95 us (7%)
  other arithmetic  6.05 us (5%)
  local copies, waits for them, and re-layouts  3.98 us (3%)
    all_to_all x1, blocking collectives, shards(): lax.all_to_all(jnp.broadcast_to(col_load[None], (Z, SUB, WIDTH)), 'z', sp...  30.4 us
    all_gather x1, blocking collectives, shards(): sketch_gram = lax.all_gather(gram_piece, ('c', 'x'), axis=0, tiled=True)  24.1 us
    all_to_all x1, waiting for transfers between devices, shards(): lax.all_to_all(row_load, ('y', 'x'), split_axis=0, concat_axis=0, tiled=T...  12.1 us
    all_to_all x1, waiting for transfers between devices, shards(): lax.all_to_all(col_load, 'z', split_axis=0, concat_axis=0, tiled=True)  10.5 us
    pallas_call x1, Pallas kernels, shards(): pl.pallas_call(tile_kernel, out_shape=[jax.ShapeDtypeStruct((Y, BLOCK, PR...  8.95 us
    all_to_all x1, starting transfers between devices, shards(): lax.all_to_all(row_load, ('y', 'x'), split_axis=0, concat_axis=0, tiled=T...  6.75 us
    all_to_all x1, starting transfers between devices, shards(): lax.all_to_all(col_load, 'z', split_axis=0, concat_axis=0, tiled=True)  4.3 us
    unnamed x4, local copies, waits for them, and re-layouts  2.79 us
  transfers between devices with their start and end apart: 5, of which 4 were waited for; matrix products, arithmetic and copies ran while one was open for 2% of the time, Pallas kernels for 0%

profile of v1, /device:TPU:1, one launch (start us, length us, event | category | flops | bytes accessed | tf_op | source)
XLA Modules:
  0.0 127.3 jit_solution(404013807333409743)
XLA Ops:
  7.9 0.8 fusion.3
  8.6 1.8 %pad_maximum_fusion.1 = bf16[528,384]{1,0:T(8,128)(2,1)} fusion(bf16[16,384]{1,0:T(8,128)(2,1)S(1)} %pad_convert_fusion, bf16[512,128]{1,0:T(8,128)(2,1)} %param.7, bf16[512,256]{1,0:T(8,128)(2,1)} %param.6), kind=kLoop, calls=%fused_computation.4 | loop fusion | flops 1216512 | bytes 811008 | tf_op jit(solution)/shard_map/concatenate | solution.py:93
  10.5 0.9 pad_maximum_fusion.3
  11.4 30.4 %all_to_all.15.own_ref = bf16[8,128,384]{2,1,0:T(8,128)(2,1)S(1)} all-to-all(bf16[8,128,384]{2,1,0:T(8,128)(2,1)S(1)} %broadcast_in_dim.8), channel_id=1, replica_groups=mesh['y'=4,'z'=8,'c'=2,'x'=4] {'z'}, dimensions={0} | all-to-all | bytes 1572864 | tf_op jit(solution)/shard_map/all_to_all | solution.py:97
  41.9 2.5 %collective-permute-start = (bf16[8,128,384]{2,1,0:T(8,128)(2,1)S(1)}, bf16[8,128,384]{2,1,0:T(8,128)(2,1)S(1)}, u32[]{:S(2)}, u32[]{:S(2)}) collective-permute-start(bf16[8,128,384]{2,1,0:T(8,128)(2,1)S(1)} %all_to_all.15.own_ref), channel_id=1, source_target_pairs={{0,4},{4,0},{1,5},{5,1},{2,6},{6,2},{3,7},{7,3},{8,12},{12,8},{9,1... | collective-permute-start | bytes 2359304 | tf_op jit(solution)/shard_map/ppermute | solution.py:100
  44.3 0.7 slice.37
  45.1 0.1 copy.19
  45.4 0.1 reshape.40.scale_ref
  45.5 0.8 collective-permute-done.other_ref
  46.2 1.4 %copy-done = bf16[2112,384]{1,0:T(8,128)(2,1)S(1)} copy-done((bf16[2112,384]{1,0:T(8,128)(2,1)S(1)}, bf16[2112,384]{1,0:T(8,128)(2,1)}, u32[]{:S(2)}) %copy-start) | copy-done | bytes 1622040
  47.7 8.9 %tiles.1 = (bf16[4,512,128]{2,1,0:T(8,128)(2,1)S(1)}, f32[9,128,128]{2,1,0:T(8,128)S(1)}, f32[9,128,128]{2,1,0:T(8,128)S(1)}) custom-call(f32[4,16]{1,0:T(4,128)S(1)} %reshape.40.scale_ref, bf16[4,528,384]{2,1,0:T(8,128)(2,1)S(1)} %bitcast.22, bf16[8,128,384]{2,1,0:T(8,128)(2,1)S(1)} %all_to_all.15.own_ref, ...), custom_call_target="tpu_custom_call" | custom-call | tf_op jit(solution)/shard_map/tiles/pallas_call | solution.py:108
  56.6 0.5 collective-permute-start.1
  57.1 1.6 %collective-permute-done.1 = f32[9,128,128]{2,1,0:T(8,128)S(1)} collective-permute-done((f32[9,128,128]{2,1,0:T(8,128)S(1)}, f32[9,128,128]{2,1,0:T(8,128)S(1)}, u32[]{:S(2)}, u32[]{:S(2)}) %collective-permute-start.1) | collective-permute-done | bytes 589856 | tf_op jit(solution)/shard_map/ppermute | solution.py:122
  58.8 0.9 pad_maximum_fusion
  59.7 6.8 %all-to-all-start.1 = ((bf16[16,160,128]{2,1,0:T(8,128)(2,1)}), bf16[16,160,128]{2,1,0:T(8,128)(2,1)S(1)}, u32[]{:S(2)}, u32[]{:S(2)}) async-start(bf16[16,160,128]{2,1,0:T(8,128)(2,1)} %pad_maximum_fusion), calls=%async_computation.1 | async-start | bytes 1310720 | tf_op jit(solution)/shard_map/all_to_all | solution.py:126
  66.5 12.1 %all-to-all-done.1 = bf16[16,160,128]{2,1,0:T(8,128)(2,1)S(1)} async-done(((bf16[16,160,128]{2,1,0:T(8,128)(2,1)}), bf16[16,160,128]{2,1,0:T(8,128)(2,1)S(1)}, u32[]{:S(2)}, u32[]{:S(2)}) %all-to-all-start.1) | async-done | bytes 655392 | tf_op jit(solution)/shard_map/all_to_all | solution.py:126
  78.6 0.1 convert_reduce_fusion
  78.8 0.7 pad_maximum_fusion.2
  79.5 4.3 %all-to-all-start.2 = ((bf16[8,160,128]{2,1,0:T(8,128)(2,1)}), bf16[8,160,128]{2,1,0:T(8,128)(2,1)S(1)}, u32[]{:S(2)}, u32[]{:S(2)}) async-start(bf16[8,160,128]{2,1,0:T(8,128)(2,1)} %pad_maximum_fusion.2), calls=%async_computation.2 | async-start | bytes 655360 | tf_op jit(solution)/shard_map/all_to_all | solution.py:133
  83.8 0.6 slice_multiply_fusion.1
  84.4 10.5 %all-to-all-done.2 = bf16[8,160,128]{2,1,0:T(8,128)(2,1)S(1)} async-done(((bf16[8,160,128]{2,1,0:T(8,128)(2,1)}), bf16[8,160,128]{2,1,0:T(8,128)(2,1)S(1)}, u32[]{:S(2)}, u32[]{:S(2)}) %all-to-all-start.2) | async-done | bytes 327712 | tf_op jit(solution)/shard_map/all_to_all | solution.py:133
  95.0 0.7 copy.23
  95.7 24.1 %all_gather.11 = f32[128,128]{1,0:T(8,128)S(1)} all-gather(f32[16,128]{1,0:T(8,128)S(1)} %fusion.4), channel_id=1, replica_groups=mesh['y'=4,'z'=8,'c'=2,'x'=4] {'c','x'}, dimensions={0}, use_global_device_ids=true | all-gather | bytes 73728 | tf_op jit(solution)/shard_map/all_gather | solution.py:137
  119.8 0.6 copy.26
  (25 shorter events, 0.6 us)
Async XLA Ops:
  7.2 37.2 %all-gather.3.cloned.1.call-start = ((), (), s32[]{:S(2)}) async-start(), calls=%async_computation.3 | async-start | bytes 2027520 | tf_op jit(solution)/shard_map/all_gather | solution.py:94
  41.9 4.4 %collective-permute-start = (bf16[8,128,384]{2,1,0:T(8,128)(2,1)S(1)}, bf16[8,128,384]{2,1,0:T(8,128)(2,1)S(1)}, u32[]{:S(2)}, u32[]{:S(2)}) collective-permute-start(bf16[8,128,384]{2,1,0:T(8,128)(2,1)S(1)} %all_to_all.15.own_ref), channel_id=1, source_target_pairs={{0,4},{4,0},{1,5},{5,1},{2,6},{6,2},{3,7},{7,3},{8,12},{12,8},{9,1... | collective-permute-start | bytes 2359304 | tf_op jit(solution)/shard_map/ppermute | solution.py:100
  46.2 1.4 %copy-start = (bf16[2112,384]{1,0:T(8,128)(2,1)S(1)}, bf16[2112,384]{1,0:T(8,128)(2,1)}, u32[]{:S(2)}) copy-start(bf16[2112,384]{1,0:T(8,128)(2,1)} %all-gather.3.cloned.1.call-done) | copy-start | bytes 4866052
  56.6 2.1 %collective-permute-start.1 = (f32[9,128,128]{2,1,0:T(8,128)S(1)}, f32[9,128,128]{2,1,0:T(8,128)S(1)}, u32[]{:S(2)}, u32[]{:S(2)}) collective-permute-start(f32[9,128,128]{2,1,0:T(8,128)S(1)} %get-tuple-element.8), channel_id=1, source_target_pairs={{0,4},{4,0},{1,5},{5,1},{2,6},{6,2},{3,7},{7,3},{8,12},{12,8},{9,1... | collective-permute-start | bytes 1769480 | tf_op jit(solution)/shard_map/ppermute | solution.py:122
  59.7 18.9 %all-to-all-start.1 = ((bf16[16,160,128]{2,1,0:T(8,128)(2,1)}), bf16[16,160,128]{2,1,0:T(8,128)(2,1)S(1)}, u32[]{:S(2)}, u32[]{:S(2)}) async-start(bf16[16,160,128]{2,1,0:T(8,128)(2,1)} %pad_maximum_fusion), calls=%async_computation.1 | async-start | bytes 1310720 | tf_op jit(solution)/shard_map/all_to_all | solution.py:126
  79.5 15.4 %all-to-all-start.2 = ((bf16[8,160,128]{2,1,0:T(8,128)(2,1)}), bf16[8,160,128]{2,1,0:T(8,128)(2,1)S(1)}, u32[]{:S(2)}, u32[]{:S(2)}) async-start(bf16[8,160,128]{2,1,0:T(8,128)(2,1)} %pad_maximum_fusion.2), calls=%async_computation.2 | async-start | bytes 655360 | tf_op jit(solution)/shard_map/all_to_all | solution.py:133
Sparse Core Ops, SparseCore 0:
  10.6 33.2 all-gather.2

commit v2 on v1

v2 whole, which is shorter than its diff:
```python
import math

import jax
import jax.numpy as jnp
from jax import lax
from jax.experimental import pallas as pl
from jax.experimental.pallas import tpu as pltpu
from jax.sharding import Mesh, PartitionSpec as P

BF16 = jnp.bfloat16
F32 = jnp.float32
Y, Z, C, X = 4, 8, 2, 4
BLOCKS = Y * Z * C
BLOCK, SUB, RANK, PROBES = 512, 128, 256, 128
WIDTH = RANK + PROBES
MASK_ROWS = 16
LOAD_ROWS = BLOCK + MASK_ROWS
HALF = Z * SUB
NODES = BLOCKS * BLOCK
PIECE = PROBES // (C * X)
SENT = SUB + 2 * PIECE
SCALE = 1.0 / math.sqrt(NODES)
LIMIT = 40 * 2**20
SWAP = [(0, 1), (1, 0)]


def contract_rows(left, right):
    return lax.dot_general(left, right, (((0,), (0,)), ((), ())), preferred_element_type=F32)


def split(value):
    high = value.astype(BF16)
    low = (value - high.astype(F32)).astype(BF16)
    return high, low


def pack_kernel(count_ref, factor_ref, side_ref, cols_ref, probe_ref, pairs_ref, rows_out, cols_out):
    slots = pairs_ref.shape[1]
    used = lax.broadcasted_iota(jnp.int32, (BLOCKS, slots), 1) < count_ref[0]
    same = lax.broadcasted_iota(jnp.int32, (BLOCKS, slots), 0) == pairs_ref[...]
    hits = jnp.where(same & used, 1.0, 0.0).astype(BF16)
    ones = jnp.ones((MASK_ROWS, slots), BF16)
    flags = lax.dot_general(ones, hits, (((1,), (1,)), ((), ())), preferred_element_type=F32)
    flags = jnp.concatenate([flags, jnp.zeros((MASK_ROWS, WIDTH - BLOCKS), F32)], 1)
    rows_out[BLOCK:LOAD_ROWS, :] = flags.astype(BF16)
    rows_out[0:BLOCK, 0:RANK] = factor_ref[...]
    rows_out[0:BLOCK, RANK:WIDTH] = side_ref[...]
    for s in range(Z):
        cols_out[s, :, 0:RANK] = cols_ref[...]
        cols_out[s, :, RANK:WIDTH] = probe_ref[...]


def tile_kernel(rows_hbm, own_ref, other_ref, row_ref, keep_ref, send_ref, rows_ref, col_acc, sems):
    copies = [pltpu.make_async_copy(rows_hbm.at[k], rows_ref.at[k], sems.at[k]) for k in range(Y)]
    for copy in copies:
        copy.start()
    first = lax.axis_index("y") * (Z * C)
    core = lax.axis_index("c")
    gram = jnp.zeros((PROBES, PROBES), F32)
    for block in range(Y):
        copies[block].wait()
        left = rows_ref[block, 0:BLOCK, 0:RANK]
        left_probes = rows_ref[block, 0:BLOCK, RANK:WIDTH]
        flags = 4.0 * rows_ref[block, BLOCK:LOAD_ROWS, 0:128].astype(F32)[0:8]
        total = None
        for half, cols_ref in enumerate((own_ref, other_ref)):
            at = first + (core if half == 0 else 1 - core)
            turned = pltpu.roll(flags, lax.rem(128 - at, 128), 1)
            right = jnp.concatenate(
                [cols_ref[s, :, 0:RANK] * turned[0:1, C * s : C * s + 1].astype(BF16) for s in range(Z)], 0
            )
            right_probes = cols_ref[:, :, RANK:WIDTH].reshape(HALF, PROBES)
            scores = lax.dot_general(left, right, (((1,), (1,)), ((), ())), preferred_element_type=F32)
            proximity = jnp.log(jnp.maximum(scores, 1.0)).astype(BF16)
            row_part = jnp.dot(proximity, right_probes, preferred_element_type=F32)
            total = row_part if half == 0 else total + row_part
            col_part = contract_rows(left_probes, proximity)
            if block == 0:
                col_acc[half] = col_part
            else:
                col_acc[half] += col_part
        high, low = split(total)
        for q in range(X):
            row_ref[X * block + q] = high[SUB * q : SUB * (q + 1)]
        gram += contract_rows(left_probes, high) + contract_rows(left_probes, low)
    for s in range(Z):
        keep_ref[s] = col_acc[0, :, s * SUB : (s + 1) * SUB]
        send_ref[s] = col_acc[1, :, s * SUB : (s + 1) * SUB]
    keep_ref[Z] = gram
    send_ref[Z] = gram


def join_kernel(keep_ref, got_ref, part_ref, rows_out, cols_out):
    for s in range(Z):
        cols_out[s, 0:SUB, :] = (keep_ref[s] + got_ref[s]).astype(BF16)
    core = lax.axis_index("c")
    half = PROBES // C
    at = pl.ds(pl.multiple_of(core * half, half), half)
    gram = keep_ref[Z, at, :] + got_ref[Z, at, :]
    high, low = split(gram)
    for y in range(Y):
        for x in range(X):
            rows_out[X * y + x, 0:SUB, :] = part_ref[X * y + x]
            rows_out[X * y + x, SUB : SUB + PIECE, :] = high[PIECE * x : PIECE * (x + 1)]
            rows_out[X * y + x, SUB + PIECE : SENT, :] = low[PIECE * x : PIECE * (x + 1)]


def row_kernel(got_ref, cols_ref, sketch_ref, cols_out):
    total = got_ref[0].astype(F32)
    for k in range(1, Y * X):
        total += got_ref[k].astype(F32)
    sketch_ref[...] = total[0:SUB] * SCALE
    high, low = split(total[SUB : SUB + PIECE] + total[SUB + PIECE : SENT])
    for s in range(Z):
        cols_out[s, 0:SUB, :] = cols_ref[s]
        cols_out[s, SUB : SUB + PIECE, :] = high
        cols_out[s, SUB + PIECE : SENT, :] = low


def col_kernel(got_ref, sketch_ref, gram_ref):
    total = got_ref[0].astype(F32)
    for k in range(1, Z):
        total += got_ref[k].astype(F32)
    sketch_ref[...] = total[0:SUB].T * SCALE
    gram_ref[...] = (total[SUB : SUB + PIECE] + total[SUB + PIECE : SENT]) * (1.0 / NODES)


def shards(factor_rows, row_side_probes, factor_cols, probe_cols, pair_blocks, pair_count):
    vmem = pl.BlockSpec(memory_space=pltpu.VMEM)
    smem = pl.BlockSpec(memory_space=pltpu.SMEM)
    hbm = pl.BlockSpec(memory_space=pl.ANY)
    params = pltpu.CompilerParams(vmem_limit_bytes=LIMIT)
    shape = jax.ShapeDtypeStruct

    row_load, col_load = pl.pallas_call(
        pack_kernel,
        out_shape=[shape((LOAD_ROWS, WIDTH), BF16), shape((Z, SUB, WIDTH), BF16)],
        in_specs=[smem, vmem, vmem, vmem, vmem, vmem],
        out_specs=[vmem, vmem],
        compiler_params=params,
        name="pack",
    )(pair_count, factor_rows, row_side_probes, factor_cols, probe_cols, pair_blocks)
    all_rows = lax.all_gather(row_load, "y", axis=0, tiled=False)
    own_cols = lax.all_to_all(col_load, "z", split_axis=0, concat_axis=0, tiled=True)
    other_cols = lax.ppermute(own_cols, "c", SWAP)

    row_part, keep, send = pl.pallas_call(
        tile_kernel,
        out_shape=[
            shape((Y * X, SUB, PROBES), BF16),
            shape((Z + 1, PROBES, SUB), F32),
            shape((Z + 1, PROBES, SUB), F32),
        ],
        in_specs=[hbm, vmem, vmem],
        out_specs=[vmem, vmem, vmem],
        scratch_shapes=[
            pltpu.VMEM((Y, LOAD_ROWS, WIDTH), BF16),
            pltpu.VMEM((C, PROBES, HALF), F32),
            pltpu.SemaphoreType.DMA((Y,)),
        ],
        compiler_params=params,
        name="tiles",
    )(all_rows, own_cols, other_cols)

    got = lax.ppermute(send, "c", SWAP)
    row_load, col_part = pl.pallas_call(
        join_kernel,
        out_shape=[shape((Y * X, SENT, PROBES), BF16), shape((Z, SUB, SUB), BF16)],
        in_specs=[vmem, vmem, vmem],
        out_specs=[vmem, vmem],
        compiler_params=params,
        name="join",
    )(keep, got, row_part)
    row_got = lax.all_to_all(row_load, ("y", "x"), split_axis=0, concat_axis=0, tiled=True)
    row_sketch, col_load = pl.pallas_call(
        row_kernel,
        out_shape=[shape((SUB, PROBES), F32), shape((Z, SENT, SUB), BF16)],
        in_specs=[vmem, vmem],
        out_specs=[vmem, vmem],
        compiler_params=params,
        name="row_sum",
    )(row_got, col_part)
    col_got = lax.all_to_all(col_load, "z", split_axis=0, concat_axis=0, tiled=True)
    col_sketch, gram = pl.pallas_call(
        col_kernel,
        out_shape=[shape((SUB, PROBES), F32), shape((PIECE, PROBES), F32)],
        in_specs=[vmem],
        out_specs=[vmem, vmem],
        compiler_params=params,
        name="col_sum",
    )(col_got)

    x, c = lax.axis_index("x"), lax.axis_index("c")
    for axis, pairs, upper in (
        ("x", [(0, 1), (1, 0), (2, 3), (3, 2)], lax.rem(x, 2) == 1),
        ("x", [(0, 3), (3, 0), (1, 2), (2, 1)], x >= 2),
        ("c", SWAP, c == 1),
    ):
        peer = lax.ppermute(gram, axis, pairs)
        gram = jnp.concatenate([jnp.where(upper, peer, gram), jnp.where(upper, gram, peer)], 0)
    return (row_sketch, col_sketch, gram)


def solution(mesh):
    grid = Mesh(mesh.devices.reshape(Y, Z, C, X), ("y", "z", "c", "x"))
    rows, subs = ("y", "z", "c"), ("y", "z", "c", "x")
    return jax.shard_map(
        shards,
        mesh=grid,
        in_specs=(P(rows, None), P(rows, None), P(subs, None), P(subs, None), P(rows, None), P(rows)),
        out_specs=(P(subs, None), P(subs, None), P()),
        check_vma=False,
    )
```

time: 128 us -> 119 us (0.930)
  waiting for transfers between devices: 25 us -> 10.3 us
  blocking collectives: 54.5 us -> 64.1 us
  other arithmetic: 6.05 us -> 0.66 us
  Pallas kernels: 8.95 us -> 14 us
  starting transfers between devices: 14 us -> 9.22 us
  local copies, waits for them, and re-layouts: 3.98 us -> 5.52 us
    all_to_all x1 -> x3, blocking collectives: 30.4 us -> 64.1 us  [the longest x2 45.1 us: shards(): lax.all_to_all(col_load, 'z', split_axis=0, concat_axis=0, tiled=True)]
    all_gather x1 -> x0, blocking collectives: 24.1 us -> none  [shards(): sketch_gram = lax.all_gather(gram_piece, ('c', 'x'), axis=0, tiled=True)]
    all_to_all x2 -> x0, waiting for transfers between devices: 22.6 us -> none  [the longest x1 12.1 us: shards(): lax.all_to_all(row_load, ('y', 'x'), split_axis=0, concat_axis=0, tiled=T...]
    all_to_all x2 -> x0, starting transfers between devices: 11.1 us -> none  [the longest x1 6.75 us: shards(): lax.all_to_all(row_load, ('y', 'x'), split_axis=0, concat_axis=0, tiled=T...]
    ppermute x2 -> x5, waiting for transfers between devices: 2.4 us -> 10.3 us  [the longest x3 6.73 us: shards(): peer = lax.ppermute(gram, axis, pairs)]
    ppermute x2 -> x5, starting transfers between devices: 2.91 us -> 9.18 us  [the longest x3 6.3 us: shards(): peer = lax.ppermute(gram, axis, pairs)]
    pallas_call x1 -> x5, Pallas kernels: 8.95 us -> 14 us  [the longest x1 11.5 us: shards(): pl.pallas_call(tile_kernel, out_shape=[shape((Y * X, SUB, PROBES), BF16),...]
    concatenate x5 -> x3, other arithmetic: 4.33 us -> 0.65 us  [shards(): jnp.concatenate([jnp.where(upper, peer, gram), jnp.where(upper, gram, pee...]
  transfers between devices with their start and end apart: 5 -> 6, of which waited for: 4 -> 5; matrix products, arithmetic and copies ran while one was open for 2% -> 0% of each run, Pallas kernels for 0% -> 0%
where the time goes in v2:
time: 119 us; the launch traced here: 118 us
  blocking collectives  64.1 us (54%)
  between operations  14.7 us (12%)
  Pallas kernels  14 us (12%)
  waiting for transfers between devices  10.3 us (9%)
  starting transfers between devices  9.22 us (8%)
  local copies, waits for them, and re-layouts  5.52 us (5%)
    all_to_all x2, blocking collectives, shards(): lax.all_to_all(col_load, 'z', split_axis=0, concat_axis=0, tiled=True)  45.1 us
    all_to_all x1, blocking collectives, shards(): lax.all_to_all(row_load, ('y', 'x'), split_axis=0, concat_axis=0, tiled=T...  19 us
    pallas_call x1, Pallas kernels, shards(): pl.pallas_call(tile_kernel, out_shape=[shape((Y * X, SUB, PROBES), BF16),...  11.5 us
    ppermute x3, waiting for transfers between devices, shards(): peer = lax.ppermute(gram, axis, pairs)  6.73 us
    ppermute x3, starting transfers between devices, shards(): peer = lax.ppermute(gram, axis, pairs)  6.3 us
    unnamed x12, local copies, waits for them, and re-layouts  5.52 us
    ppermute x1, starting transfers between devices, shards(): other_cols = lax.ppermute(own_cols, 'c', SWAP)  2.41 us
  transfers between devices with their start and end apart: 6, of which 5 were waited for; matrix products, arithmetic and copies ran while one was open for 0% of the time, Pallas kernels for 0%

profile of v2, /device:TPU:1, one launch (start us, length us, event | category | flops | bytes accessed | tf_op | source)
XLA Modules:
  0.0 118.5 jit_solution(11448693546392173020)
XLA Ops:
  7.9 0.9 copy-done.1
  8.8 0.9 copy-done.2
  9.7 0.8 copy-done.3
  10.6 0.8 copy-done.4
  11.3 0.7 copy-done.5
  12.0 0.9 pack.1
  12.9 30.5 %all_to_all.15.own_ref = bf16[8,128,384]{2,1,0:T(8,128)(2,1)S(1)} all-to-all(bf16[8,128,384]{2,1,0:T(8,128)(2,1)S(1)} %get-tuple-element.15), channel_id=1, replica_groups=mesh['y'=4,'z'=8,'c'=2,'x'=4] {'z'}, dimensions={0} | all-to-all | bytes 1572864 | tf_op jit(solution)/shard_map/all_to_all | solution.py:144
  43.4 2.4 %collective-permute-start = (bf16[8,128,384]{2,1,0:T(8,128)(2,1)S(1)}, bf16[8,128,384]{2,1,0:T(8,128)(2,1)S(1)}, u32[]{:S(2)}, u32[]{:S(2)}) collective-permute-start(bf16[8,128,384]{2,1,0:T(8,128)(2,1)S(1)} %all_to_all.15.own_ref), channel_id=1, source_target_pairs={{0,4},{4,0},{1,5},{5,1},{2,6},{6,2},{3,7},{7,3},{8,12},{12,8},{9,1... | collective-permute-start | bytes 2359304 | tf_op jit(solution)/shard_map/ppermute | solution.py:145
  45.8 1.9 %collective-permute-done.other_ref = bf16[8,128,384]{2,1,0:T(8,128)(2,1)S(1)} collective-permute-done((bf16[8,128,384]{2,1,0:T(8,128)(2,1)S(1)}, bf16[8,128,384]{2,1,0:T(8,128)(2,1)S(1)}, u32[]{:S(2)}, u32[]{:S(2)}) %collective-permute-start) | collective-permute-done | bytes 786464 | tf_op jit(solution)/shard_map/ppermute | solution.py:145
  47.7 1.4 %copy-done = bf16[2112,384]{1,0:T(8,128)(2,1)S(1)} copy-done((bf16[2112,384]{1,0:T(8,128)(2,1)S(1)}, bf16[2112,384]{1,0:T(8,128)(2,1)}, u32[]{:S(2)}) %copy-start) | copy-done | bytes 1622040
  49.2 11.5 %tiles.1 = (bf16[16,128,128]{2,1,0:T(8,128)(2,1)S(1)}, f32[9,128,128]{2,1,0:T(8,128)S(1)}, f32[9,128,128]{2,1,0:T(8,128)S(1)}) custom-call(bf16[4,528,384]{2,1,0:T(8,128)(2,1)S(1)} %bitcast.1, bf16[8,128,384]{2,1,0:T(8,128)(2,1)S(1)} %all_to_all.15.own_ref, bf16[8,128,384]{2,1,0:T(8,128)(2,1)S(1)} %collective-permute-done.other_ref), custom_call_target="tpu_custom_call" | custom-call | tf_op jit(solution)/shard_map/tiles/pallas_call | solution.py:147
  60.7 0.5 collective-permute-start.1
  61.1 1.6 %collective-permute-done.1.got_ref = f32[9,128,128]{2,1,0:T(8,128)S(1)} collective-permute-done((f32[9,128,128]{2,1,0:T(8,128)S(1)}, f32[9,128,128]{2,1,0:T(8,128)S(1)}, u32[]{:S(2)}, u32[]{:S(2)}) %collective-permute-start.1) | collective-permute-done | bytes 589856 | tf_op jit(solution)/shard_map/ppermute | solution.py:165
  62.8 0.1 join.1
  62.9 19.0 %all_to_all.16.got_ref = bf16[16,160,128]{2,1,0:T(8,128)(2,1)S(1)} all-to-all(bf16[16,160,128]{2,1,0:T(8,128)(2,1)S(1)} %get-tuple-element.19), channel_id=1, replica_groups=mesh['y'=4,'z'=8,'c'=2,'x'=4] {'y','x'}, dimensions={0} | all-to-all | bytes 1310720 | tf_op jit(solution)/shard_map/all_to_all | solution.py:174
  81.8 0.7 row_sum.1
  82.5 14.6 %all_to_all.17.got_ref = bf16[8,160,128]{2,1,0:T(8,128)(2,1)S(1)} all-to-all(bf16[8,160,128]{2,1,0:T(8,128)(2,1)S(1)} %get-tuple-element.22), channel_id=1, replica_groups=mesh['y'=4,'z'=8,'c'=2,'x'=4] {'z'}, dimensions={0} | all-to-all | bytes 655360 | tf_op jit(solution)/shard_map/all_to_all | solution.py:183
  97.2 0.7 col_sum.1
  97.9 2.5 %collective-permute-done.2 = f32[16,128]{1,0:T(8,128)S(1)} collective-permute-done((f32[16,128]{1,0:T(8,128)S(1)}, f32[16,128]{1,0:T(8,128)S(1)}, u32[]{:S(2)}, u32[]{:S(2)}) %collective-permute-start.2) | collective-permute-done | bytes 8224 | tf_op jit(solution)/shard_map/ppermute | solution.py:199
  100.4 0.4 collective-permute-start.3
  100.9 3.4 %collective-permute-done.3 = f32[32,128]{1,0:T(8,128)S(1)} collective-permute-done((f32[32,128]{1,0:T(8,128)S(1)}, f32[32,128]{1,0:T(8,128)S(1)}, u32[]{:S(2)}, u32[]{:S(2)}) %collective-permute-start.3) | collective-permute-done | bytes 16416 | tf_op jit(solution)/shard_map/ppermute | solution.py:199
  104.2 5.9 %collective-permute-start.4 = (f32[64,128]{1,0:T(8,128)S(1)}, f32[64,128]{1,0:T(8,128)S(1)}, u32[]{:S(2)}, u32[]{:S(2)}) collective-permute-start(f32[64,128]{1,0:T(8,128)S(1)} %pad_maximum_fusion.1), channel_id=1, source_target_pairs={{0,4},{4,0},{1,5},{5,1},{2,6},{6,2},{3,7},{7,3},{8,12},{12,8},{9,1... | collective-permute-start | bytes 98312 | tf_op jit(solution)/shard_map/ppermute | solution.py:199
  110.1 0.9 collective-permute-done.4
  111.0 0.6 pad_maximum_fusion
  (15 shorter events, 0.1 us)
Async XLA Ops:
  7.2 40.6 %all-gather.3.cloned.1.call-start = ((), (), s32[]{:S(2)}) async-start(), calls=%async_computation.3 | async-start | bytes 2027520 | tf_op jit(solution)/shard_map/all_gather | solution.py:143
  7.9 1.0 copy-start.1
  8.8 0.9 copy-start.2
  9.7 0.8 copy-start.3
  10.6 0.8 copy-start.4
  11.3 0.7 copy-start.5
  43.4 4.3 %collective-permute-start = (bf16[8,128,384]{2,1,0:T(8,128)(2,1)S(1)}, bf16[8,128,384]{2,1,0:T(8,128)(2,1)S(1)}, u32[]{:S(2)}, u32[]{:S(2)}) collective-permute-start(bf16[8,128,384]{2,1,0:T(8,128)(2,1)S(1)} %all_to_all.15.own_ref), channel_id=1, source_target_pairs={{0,4},{4,0},{1,5},{5,1},{2,6},{6,2},{3,7},{7,3},{8,12},{12,8},{9,1... | collective-permute-start | bytes 2359304 | tf_op jit(solution)/shard_map/ppermute | solution.py:145
  47.7 1.4 %copy-start = (bf16[2112,384]{1,0:T(8,128)(2,1)S(1)}, bf16[2112,384]{1,0:T(8,128)(2,1)}, u32[]{:S(2)}) copy-start(bf16[2112,384]{1,0:T(8,128)(2,1)} %all-gather.3.cloned.1.call-done) | copy-start | bytes 4866052
  60.7 2.1 %collective-permute-start.1 = (f32[9,128,128]{2,1,0:T(8,128)S(1)}, f32[9,128,128]{2,1,0:T(8,128)S(1)}, u32[]{:S(2)}, u32[]{:S(2)}) collective-permute-start(f32[9,128,128]{2,1,0:T(8,128)S(1)} %get-tuple-element.17), channel_id=1, source_target_pairs={{0,4},{4,0},{1,5},{5,1},{2,6},{6,2},{3,7},{7,3},{8,12},{12,8},{9,1... | collective-permute-start | bytes 1769480 | tf_op jit(solution)/shard_map/ppermute | solution.py:165
  97.9 2.5 %collective-permute-start.2 = (f32[16,128]{1,0:T(8,128)S(1)}, f32[16,128]{1,0:T(8,128)S(1)}, u32[]{:S(2)}, u32[]{:S(2)}) collective-permute-start(f32[16,128]{1,0:T(8,128)S(1)} %get-tuple-element.24), channel_id=1, source_target_pairs={{0,1},{1,0},{2,3},{3,2},{4,5},{5,4},{6,7},{7,6},{8,9},{9,8},{10,11... | collective-permute-start | bytes 24584 | tf_op jit(solution)/shard_map/ppermute | solution.py:199
  100.4 3.8 %collective-permute-start.3 = (f32[32,128]{1,0:T(8,128)S(1)}, f32[32,128]{1,0:T(8,128)S(1)}, u32[]{:S(2)}, u32[]{:S(2)}) collective-permute-start(f32[32,128]{1,0:T(8,128)S(1)} %pad_maximum_fusion.2), channel_id=1, source_target_pairs={{0,3},{3,0},{1,2},{2,1},{4,7},{7,4},{5,6},{6,5},{8,11},{11,8},{9,1... | collective-permute-start | bytes 49160 | tf_op jit(solution)/shard_map/ppermute | solution.py:199
  104.2 6.7 %collective-permute-start.4 = (f32[64,128]{1,0:T(8,128)S(1)}, f32[64,128]{1,0:T(8,128)S(1)}, u32[]{:S(2)}, u32[]{:S(2)}) collective-permute-start(f32[64,128]{1,0:T(8,128)S(1)} %pad_maximum_fusion.1), channel_id=1, source_target_pairs={{0,4},{4,0},{1,5},{5,1},{2,6},{6,2},{3,7},{7,3},{8,12},{12,8},{9,1... | collective-permute-start | bytes 98312 | tf_op jit(solution)/shard_map/ppermute | solution.py:199
Sparse Core Ops, SparseCore 0:
  13.0 33.2 all-gather.2

commit v3 on v2

--- a/solution.py
+++ b/solution.py
@@ -21,6 +21,7 @@
 SENT = SUB + 2 * PIECE
 SCALE = 1.0 / math.sqrt(NODES)
 LIMIT = 40 * 2**20
+WHOLE = 60 * 2**20
 SWAP = [(0, 1), (1, 0)]
 
 
@@ -34,7 +35,26 @@
     return high, low
 
 
-def pack_kernel(count_ref, factor_ref, side_ref, cols_ref, probe_ref, pairs_ref, rows_out, cols_out):
+def pack_kernel(
+    count_hbm, factor_hbm, side_hbm, cols_hbm, probe_hbm, pairs_hbm, rows_out, cols_out, count_ref, pairs_ref, sems
+):
+    copies = [
+        pltpu.make_async_copy(source, target, sems.at[k])
+        for k, (source, target) in enumerate(
+            (
+                (count_hbm, count_ref),
+                (pairs_hbm, pairs_ref),
+                (cols_hbm, cols_out.at[0, :, 0:RANK]),
+                (probe_hbm, cols_out.at[0, :, RANK:WIDTH]),
+                (factor_hbm, rows_out.at[0:BLOCK, 0:RANK]),
+                (side_hbm, rows_out.at[0:BLOCK, RANK:WIDTH]),
+            )
+        )
+    ]
+    for copy in copies:
+        copy.start()
+    for copy in copies[:2]:
+        copy.wait()
     slots = pairs_ref.shape[1]
     used = lax.broadcasted_iota(jnp.int32, (BLOCKS, slots), 1) < count_ref[0]
     same = lax.broadcasted_iota(jnp.int32, (BLOCKS, slots), 0) == pairs_ref[...]
@@ -43,49 +63,57 @@
     flags = lax.dot_general(ones, hits, (((1,), (1,)), ((), ())), preferred_element_type=F32)
     flags = jnp.concatenate([flags, jnp.zeros((MASK_ROWS, WIDTH - BLOCKS), F32)], 1)
     rows_out[BLOCK:LOAD_ROWS, :] = flags.astype(BF16)
-    rows_out[0:BLOCK, 0:RANK] = factor_ref[...]
-    rows_out[0:BLOCK, RANK:WIDTH] = side_ref[...]
-    for s in range(Z):
-        cols_out[s, :, 0:RANK] = cols_ref[...]
-        cols_out[s, :, RANK:WIDTH] = probe_ref[...]
-
-
-def tile_kernel(rows_hbm, own_ref, other_ref, row_ref, keep_ref, send_ref, rows_ref, col_acc, sems):
-    copies = [pltpu.make_async_copy(rows_hbm.at[k], rows_ref.at[k], sems.at[k]) for k in range(Y)]
-    for copy in copies:
-        copy.start()
-    first = lax.axis_index("y") * (Z * C)
+    for copy in copies[2:4]:
+        copy.wait()
+    for s in range(1, Z):
+        cols_out[s] = cols_out[0]
+    for copy in copies[4:]:
+        copy.wait()
+
+
+def tile_kernel(rows0, rows1, rows2, rows3, low_ref, high_ref, row_ref, keep_ref, send_ref, row_acc, col_acc):
+    y = lax.axis_index("y")
     core = lax.axis_index("c")
-    gram = jnp.zeros((PROBES, PROBES), F32)
-    for block in range(Y):
-        copies[block].wait()
-        left = rows_ref[block, 0:BLOCK, 0:RANK]
-        left_probes = rows_ref[block, 0:BLOCK, RANK:WIDTH]
-        flags = 4.0 * rows_ref[block, BLOCK:LOAD_ROWS, 0:128].astype(F32)[0:8]
-        total = None
-        for half, cols_ref in enumerate((own_ref, other_ref)):
-            at = first + (core if half == 0 else 1 - core)
+    gram = jnp.zeros((PROBES, 2 * PROBES), F32)
+    for back, rows_ref in enumerate((rows0, rows1, rows2, rows3)):
+        flags = 4.0 * rows_ref[BLOCK:LOAD_ROWS, 0:128].astype(F32)[0:8]
+        for half in range(C):
+            owner = core if half == 0 else 1 - core
+            at = y * (Z * C) + owner
             turned = pltpu.roll(flags, lax.rem(128 - at, 128), 1)
             right = jnp.concatenate(
-                [cols_ref[s, :, 0:RANK] * turned[0:1, C * s : C * s + 1].astype(BF16) for s in range(Z)], 0
-            )
-            right_probes = cols_ref[:, :, RANK:WIDTH].reshape(HALF, PROBES)
-            scores = lax.dot_general(left, right, (((1,), (1,)), ((), ())), preferred_element_type=F32)
+                [
+                    (low_ref, high_ref)[s // 4][owner, s % 4, :, 0:RANK] * turned[0:1, C * s : C * s + 1].astype(BF16)
+                    for s in range(Z)
+                ],
+                0,
+            )
+            right_probes = jnp.concatenate(
+                [cols_ref[owner, :, :, RANK:WIDTH].reshape(HALF // 2, PROBES) for cols_ref in (low_ref, high_ref)], 0
+            )
+            scores = lax.dot_general(
+                rows_ref[0:BLOCK, 0:RANK], right, (((1,), (1,)), ((), ())), preferred_element_type=F32
+            )
             proximity = jnp.log(jnp.maximum(scores, 1.0)).astype(BF16)
             row_part = jnp.dot(proximity, right_probes, preferred_element_type=F32)
-            total = row_part if half == 0 else total + row_part
-            col_part = contract_rows(left_probes, proximity)
-            if block == 0:
+            if half == 0:
+                row_acc[...] = row_part
+            else:
+                row_acc[...] += row_part
+            col_part = contract_rows(rows_ref[0:BLOCK, RANK:WIDTH], proximity)
+            if back == 0:
                 col_acc[half] = col_part
             else:
                 col_acc[half] += col_part
-        high, low = split(total)
+        high, low = split(row_acc[...])
+        block = lax.rem(y + Y - back, Y)
         for q in range(X):
             row_ref[X * block + q] = high[SUB * q : SUB * (q + 1)]
-        gram += contract_rows(left_probes, high) + contract_rows(left_probes, low)
+        gram += contract_rows(rows_ref[0:BLOCK, RANK:WIDTH], jnp.concatenate([high, low], 1))
     for s in range(Z):
         keep_ref[s] = col_acc[0, :, s * SUB : (s + 1) * SUB]
         send_ref[s] = col_acc[1, :, s * SUB : (s + 1) * SUB]
+    gram = gram[:, 0:PROBES] + gram[:, PROBES:]
     keep_ref[Z] = gram
     send_ref[Z] = gram
 
@@ -127,7 +155,6 @@
 
 def shards(factor_rows, row_side_probes, factor_cols, probe_cols, pair_blocks, pair_count):
     vmem = pl.BlockSpec(memory_space=pltpu.VMEM)
-    smem = pl.BlockSpec(memory_space=pltpu.SMEM)
     hbm = pl.BlockSpec(memory_space=pl.ANY)
     params = pltpu.CompilerParams(vmem_limit_bytes=LIMIT)
     shape = jax.ShapeDtypeStruct
@@ -135,14 +162,19 @@
     row_load, col_load = pl.pallas_call(
         pack_kernel,
         out_shape=[shape((LOAD_ROWS, WIDTH), BF16), shape((Z, SUB, WIDTH), BF16)],
-        in_specs=[smem, vmem, vmem, vmem, vmem, vmem],
-        out_specs=[vmem, vmem],
-        compiler_params=params,
+        in_specs=[hbm] * 6,
+        out_specs=[vmem, vmem],
+        scratch_shapes=[
+            pltpu.SMEM((1,), jnp.int32),
+            pltpu.VMEM(pair_blocks.shape, jnp.int32),
+            pltpu.SemaphoreType.DMA((6,)),
+        ],
+        compiler_params=pltpu.CompilerParams(vmem_limit_bytes=WHOLE),
         name="pack",
     )(pair_count, factor_rows, row_side_probes, factor_cols, probe_cols, pair_blocks)
-    all_rows = lax.all_gather(row_load, "y", axis=0, tiled=False)
+    all_rows = [row_load] + [lax.ppermute(row_load, "y", [(k, (k + s) % Y) for k in range(Y)]) for s in range(1, Y)]
     own_cols = lax.all_to_all(col_load, "z", split_axis=0, concat_axis=0, tiled=True)
-    other_cols = lax.ppermute(own_cols, "c", SWAP)
+    cols = [lax.all_gather(own_cols[k : k + Z // 2], "c", axis=0, tiled=False) for k in (0, Z // 2)]
 
     row_part, keep, send = pl.pallas_call(
         tile_kernel,
@@ -151,16 +183,15 @@
             shape((Z + 1, PROBES, SUB), F32),
             shape((Z + 1, PROBES, SUB), F32),
         ],
-        in_specs=[hbm, vmem, vmem],
+        in_specs=[vmem] * 6,
         out_specs=[vmem, vmem, vmem],
         scratch_shapes=[
-            pltpu.VMEM((Y, LOAD_ROWS, WIDTH), BF16),
+            pltpu.VMEM((BLOCK, PROBES), F32),
             pltpu.VMEM((C, PROBES, HALF), F32),
-            pltpu.SemaphoreType.DMA((Y,)),
         ],
         compiler_params=params,
         name="tiles",
-    )(all_rows, own_cols, other_cols)
+    )(*all_rows, *cols)
 
     got = lax.ppermute(send, "c", SWAP)
     row_load, col_part = pl.pallas_call(

time: 119 us -> 98.6 us (0.83)
  blocking collectives: 64.1 us -> 37.2 us
  waiting for transfers between devices: 10.3 us -> 26.9 us
  between operations: 14.7 us -> 1.33 us
  starting transfers between devices: 9.22 us -> 20.7 us
  local copies, waits for them, and re-layouts: 5.52 us -> 0.08 us
  Pallas kernels: 14 us -> 11.5 us
    all_to_all x2 -> x1, blocking collectives: 45.1 us -> 13.4 us  [shards(): lax.all_to_all(col_load, 'z', split_axis=0, concat_axis=0, tiled=True)]
    all_to_all x0 -> x1, waiting for transfers between devices: none -> 18.5 us  [shards(): lax.all_to_all(col_load, 'z', split_axis=0, concat_axis=0, tiled=True)]
    all_to_all x0 -> x1, starting transfers between devices: none -> 9.16 us  [shards(): lax.all_to_all(col_load, 'z', split_axis=0, concat_axis=0, tiled=True)]
    unnamed x12 -> x2, local copies, waits for them, and re-layouts: 5.52 us -> 0.01 us
    all_gather x0 -> x2, blocking collectives: none -> 4.85 us  [shards(): lax.all_gather(own_cols[k:k + Z // 2], 'c', axis=0, tiled=False)]
    pallas_call x1, Pallas kernels: 11.5 us -> 7.77 us  [shards(): pl.pallas_call(tile_kernel, out_shape=[shape((Y * X, SUB, PROBES), BF16),...]
    ppermute x1 -> x3, starting transfers between devices: 2.41 us -> 5.06 us  [shards(): lax.ppermute(row_load, 'y', [(k, (k + s) % Y) for k in range(Y)])]
    ppermute x1 -> x3, waiting for transfers between devices: 1.91 us -> 0.01 us  [shards(): lax.ppermute(row_load, 'y', [(k, (k + s) % Y) for k in range(Y)])]
  transfers between devices with their start and end apart: 6 -> 8, of which waited for: 5 -> 5; matrix products, arithmetic and copies ran while one was open for 0% -> 0% of each run, Pallas kernels for 0% -> 0%
where the time goes in v3:
time: 98.6 us; the launch traced here: 98.3 us
  blocking collectives  37.2 us (38%)
  waiting for transfers between devices  26.9 us (27%)
  starting transfers between devices  20.7 us (21%)
  Pallas kernels  11.5 us (12%)
  between operations  1.33 us (1%)
    all_to_all x1, blocking collectives, shards(): lax.all_to_all(row_load, ('y', 'x'), split_axis=0, concat_axis=0, tiled=T...  19 us
    all_to_all x1, waiting for transfers between devices, shards(): lax.all_to_all(col_load, 'z', split_axis=0, concat_axis=0, tiled=True)  18.5 us
    all_to_all x1, blocking collectives, shards(): lax.all_to_all(col_load, 'z', split_axis=0, concat_axis=0, tiled=True)  13.4 us
    all_to_all x1, starting transfers between devices, shards(): lax.all_to_all(col_load, 'z', split_axis=0, concat_axis=0, tiled=True)  9.16 us
    pallas_call x1, Pallas kernels, shards(): pl.pallas_call(tile_kernel, out_shape=[shape((Y * X, SUB, PROBES), BF16),...  7.77 us
    ppermute x3, waiting for transfers between devices, shards(): peer = lax.ppermute(gram, axis, pairs)  6.71 us
    ppermute x3, starting transfers between devices, shards(): peer = lax.ppermute(gram, axis, pairs)  6.04 us
    ppermute x3, starting transfers between devices, shards(): lax.ppermute(row_load, 'y', [(k, (k + s) % Y) for k in range(Y)])  5.06 us
  transfers between devices with their start and end apart: 8, of which 5 were waited for; matrix products, arithmetic and copies ran while one was open for 0% of the time, Pallas kernels for 0%

profile of v3, /device:TPU:1, one launch (start us, length us, event | category | flops | bytes accessed | tf_op | source)
XLA Modules:
  0.0 98.3 jit_solution(5585366676664521278)
XLA Ops:
  1.3 2.2 %pack.1 = (bf16[528,384]{1,0:T(8,128)(2,1)}, bf16[8,128,384]{2,1,0:T(8,128)(2,1)}) custom-call(s32[1]{0:T(128)S(6)} %copy.9.count_hbm, bf16[512,256]{1,0:T(8,128)(2,1)} %factor_hbm.1, bf16[512,128]{1,0:T(8,128)(2,1)} %side_hbm.1, bf16[128,256]{1,0:T(8,128)(2,1)} %cols_hbm.1, bf16[128,128]{1,0:T(8,128)(2,1)} %probe_hbm.1, s32[1,64]{1,0:T(1,128)} %pairs_hbm.1), custom_call_target="tpu_custom_call" | custom-call | tf_op jit(solution)/shard_map/pack/pallas_call | solution.py:162
  3.5 9.2 %all-to-all-start = ((bf16[8,128,384]{2,1,0:T(8,128)(2,1)}), bf16[8,128,384]{2,1,0:T(8,128)(2,1)S(1)}, u32[]{:S(2)}, u32[]{:S(2)}) async-start(bf16[8,128,384]{2,1,0:T(8,128)(2,1)} %get-tuple-element.15), calls=%async_computation | async-start | bytes 1572864 | tf_op jit(solution)/shard_map/all_to_all | solution.py:176
  12.6 1.4 %collective-permute-start = (bf16[528,384]{1,0:T(8,128)(2,1)S(1)}, bf16[528,384]{1,0:T(8,128)(2,1)S(1)}, u32[]{:S(2)}, u32[]{:S(2)}) collective-permute-start(bf16[528,384]{1,0:T(8,128)(2,1)S(1)} %copy-done), channel_id=1, source_target_pairs={{0,64},{64,128},{128,192},{192,0},{1,65},{65,129},{129,193},{193,1... | collective-permute-start | bytes 1216520 | tf_op jit(solution)/shard_map/ppermute | solution.py:175
  14.0 2.6 %collective-permute-start.1 = (bf16[528,384]{1,0:T(8,128)(2,1)S(1)}, bf16[528,384]{1,0:T(8,128)(2,1)S(1)}, u32[]{:S(2)}, u32[]{:S(2)}) collective-permute-start(bf16[528,384]{1,0:T(8,128)(2,1)S(1)} %copy-done), channel_id=1, source_target_pairs={{0,128},{64,192},{128,0},{192,64},{1,129},{65,193},{129,1},{193,65... | collective-permute-start | bytes 1216520 | tf_op jit(solution)/shard_map/ppermute | solution.py:175
  16.6 1.1 %collective-permute-start.2 = (bf16[528,384]{1,0:T(8,128)(2,1)S(1)}, bf16[528,384]{1,0:T(8,128)(2,1)S(1)}, u32[]{:S(2)}, u32[]{:S(2)}) collective-permute-start(bf16[528,384]{1,0:T(8,128)(2,1)S(1)} %copy-done), channel_id=1, source_target_pairs={{0,192},{64,0},{128,64},{192,128},{1,193},{65,1},{129,65},{193,129... | collective-permute-start | bytes 1216520 | tf_op jit(solution)/shard_map/ppermute | solution.py:175
  17.7 18.5 %all-to-all-done = bf16[8,128,384]{2,1,0:T(8,128)(2,1)S(1)} async-done(((bf16[8,128,384]{2,1,0:T(8,128)(2,1)}), bf16[8,128,384]{2,1,0:T(8,128)(2,1)S(1)}, u32[]{:S(2)}, u32[]{:S(2)}) %all-to-all-start) | async-done | bytes 786464 | tf_op jit(solution)/shard_map/all_to_all | solution.py:176
  36.2 0.1 fusion
  36.3 2.5 %all-gather = bf16[8,128,384]{2,1,0:T(8,128)(2,1)S(1)} all-gather(bf16[4,128,384]{2,1,0:T(8,128)(2,1)S(1)} %get-tuple-element.26), channel_id=2, replica_groups=mesh['y'=4,'z'=8,'c'=2,'x'=4] {'c'}, dimensions={0}, use_global_device_ids=true | all-gather | bytes 1179648 | tf_op jit(solution)/shard_map/all_gather | solution.py:177
  38.8 2.4 %all-gather.1 = bf16[8,128,384]{2,1,0:T(8,128)(2,1)S(1)} all-gather(bf16[4,128,384]{2,1,0:T(8,128)(2,1)S(1)} %get-tuple-element.25), channel_id=3, replica_groups=mesh['y'=4,'z'=8,'c'=2,'x'=4] {'c'}, dimensions={0}, use_global_device_ids=true | all-gather | bytes 1179648 | tf_op jit(solution)/shard_map/all_gather | solution.py:177
  41.1 0.0 collective-permute-done.rows1
  41.1 7.8 %tiles.1 = (bf16[16,128,128]{2,1,0:T(8,128)(2,1)S(1)}, f32[9,128,128]{2,1,0:T(8,128)S(1)}, f32[9,128,128]{2,1,0:T(8,128)S(1)}) custom-call(bf16[528,384]{1,0:T(8,128)(2,1)S(1)} %copy-done, bf16[528,384]{1,0:T(8,128)(2,1)S(1)} %collective-permute-done.rows1, bf16[528,384]{1,0:T(8,128)(2,1)S(1)} %collective-permute-done.1.rows2, ...), custom_call_target="tpu_custom_call" | custom-call | tf_op jit(solution)/shard_map/tiles/pallas_call | solution.py:179
  48.9 0.5 collective-permute-start.3
  49.4 1.6 %collective-permute-done.3.got_ref = f32[9,128,128]{2,1,0:T(8,128)S(1)} collective-permute-done((f32[9,128,128]{2,1,0:T(8,128)S(1)}, f32[9,128,128]{2,1,0:T(8,128)S(1)}, u32[]{:S(2)}, u32[]{:S(2)}) %collective-permute-start.3) | collective-permute-done | bytes 589856 | tf_op jit(solution)/shard_map/ppermute | solution.py:196
  51.0 0.1 join.1
  51.1 19.0 %all_to_all.15.got_ref = bf16[16,160,128]{2,1,0:T(8,128)(2,1)S(1)} all-to-all(bf16[16,160,128]{2,1,0:T(8,128)(2,1)S(1)} %get-tuple-element.19), channel_id=1, replica_groups=mesh['y'=4,'z'=8,'c'=2,'x'=4] {'y','x'}, dimensions={0} | all-to-all | bytes 1310720 | tf_op jit(solution)/shard_map/all_to_all | solution.py:205
  70.1 0.7 row_sum.1
  70.8 13.4 %all_to_all.16.got_ref = bf16[8,160,128]{2,1,0:T(8,128)(2,1)S(1)} all-to-all(bf16[8,160,128]{2,1,0:T(8,128)(2,1)S(1)} %get-tuple-element.22), channel_id=1, replica_groups=mesh['y'=4,'z'=8,'c'=2,'x'=4] {'z'}, dimensions={0} | all-to-all | bytes 655360 | tf_op jit(solution)/shard_map/all_to_all | solution.py:214
  84.2 0.7 col_sum.1
  84.9 2.5 %collective-permute-done.4 = f32[16,128]{1,0:T(8,128)S(1)} collective-permute-done((f32[16,128]{1,0:T(8,128)S(1)}, f32[16,128]{1,0:T(8,128)S(1)}, u32[]{:S(2)}, u32[]{:S(2)}) %collective-permute-start.4) | collective-permute-done | bytes 8224 | tf_op jit(solution)/shard_map/ppermute | solution.py:230
  87.4 0.4 collective-permute-start.5
  87.9 3.4 %collective-permute-done.5 = f32[32,128]{1,0:T(8,128)S(1)} collective-permute-done((f32[32,128]{1,0:T(8,128)S(1)}, f32[32,128]{1,0:T(8,128)S(1)}, u32[]{:S(2)}, u32[]{:S(2)}) %collective-permute-start.5) | collective-permute-done | bytes 16416 | tf_op jit(solution)/shard_map/ppermute | solution.py:230
  91.2 5.6 %collective-permute-start.6 = (f32[64,128]{1,0:T(8,128)S(1)}, f32[64,128]{1,0:T(8,128)S(1)}, u32[]{:S(2)}, u32[]{:S(2)}) collective-permute-start(f32[64,128]{1,0:T(8,128)S(1)} %pad_maximum_fusion.1), channel_id=1, source_target_pairs={{0,4},{4,0},{1,5},{5,1},{2,6},{6,2},{3,7},{7,3},{8,12},{12,8},{9,1... | collective-permute-start | bytes 98312 | tf_op jit(solution)/shard_map/ppermute | solution.py:230
  96.8 0.9 collective-permute-done.6
  97.7 0.6 pad_maximum_fusion
  (10 shorter events, 0.0 us)
Async XLA Ops:
  3.4 9.2 %copy-start = (bf16[528,384]{1,0:T(8,128)(2,1)S(1)}, bf16[528,384]{1,0:T(8,128)(2,1)}, u32[]{:S(2)}) copy-start(bf16[528,384]{1,0:T(8,128)(2,1)} %get-tuple-element.14.rows0) | copy-start | bytes 1216516
  3.5 32.7 %all-to-all-start = ((bf16[8,128,384]{2,1,0:T(8,128)(2,1)}), bf16[8,128,384]{2,1,0:T(8,128)(2,1)S(1)}, u32[]{:S(2)}, u32[]{:S(2)}) async-start(bf16[8,128,384]{2,1,0:T(8,128)(2,1)} %get-tuple-element.15), calls=%async_computation | async-start | bytes 1572864 | tf_op jit(solution)/shard_map/all_to_all | solution.py:176
  12.6 28.5 %collective-permute-start = (bf16[528,384]{1,0:T(8,128)(2,1)S(1)}, bf16[528,384]{1,0:T(8,128)(2,1)S(1)}, u32[]{:S(2)}, u32[]{:S(2)}) collective-permute-start(bf16[528,384]{1,0:T(8,128)(2,1)S(1)} %copy-done), channel_id=1, source_target_pairs={{0,64},{64,128},{128,192},{192,0},{1,65},{65,129},{129,193},{193,1... | collective-permute-start | bytes 1216520 | tf_op jit(solution)/shard_map/ppermute | solution.py:175
  14.0 27.1 %collective-permute-start.1 = (bf16[528,384]{1,0:T(8,128)(2,1)S(1)}, bf16[528,384]{1,0:T(8,128)(2,1)S(1)}, u32[]{:S(2)}, u32[]{:S(2)}) collective-permute-start(bf16[528,384]{1,0:T(8,128)(2,1)S(1)} %copy-done), channel_id=1, source_target_pairs={{0,128},{64,192},{128,0},{192,64},{1,129},{65,193},{129,1},{193,65... | collective-permute-start | bytes 1216520 | tf_op jit(solution)/shard_map/ppermute | solution.py:175
  16.6 24.5 %collective-permute-start.2 = (bf16[528,384]{1,0:T(8,128)(2,1)S(1)}, bf16[528,384]{1,0:T(8,128)(2,1)S(1)}, u32[]{:S(2)}, u32[]{:S(2)}) collective-permute-start(bf16[528,384]{1,0:T(8,128)(2,1)S(1)} %copy-done), channel_id=1, source_target_pairs={{0,192},{64,0},{128,64},{192,128},{1,193},{65,1},{129,65},{193,129... | collective-permute-start | bytes 1216520 | tf_op jit(solution)/shard_map/ppermute | solution.py:175
  48.9 2.1 %collective-permute-start.3 = (f32[9,128,128]{2,1,0:T(8,128)S(1)}, f32[9,128,128]{2,1,0:T(8,128)S(1)}, u32[]{:S(2)}, u32[]{:S(2)}) collective-permute-start(f32[9,128,128]{2,1,0:T(8,128)S(1)} %get-tuple-element.17), channel_id=1, source_target_pairs={{0,4},{4,0},{1,5},{5,1},{2,6},{6,2},{3,7},{7,3},{8,12},{12,8},{9,1... | collective-permute-start | bytes 1769480 | tf_op jit(solution)/shard_map/ppermute | solution.py:196
  84.9 2.5 %collective-permute-start.4 = (f32[16,128]{1,0:T(8,128)S(1)}, f32[16,128]{1,0:T(8,128)S(1)}, u32[]{:S(2)}, u32[]{:S(2)}) collective-permute-start(f32[16,128]{1,0:T(8,128)S(1)} %get-tuple-element.24), channel_id=1, source_target_pairs={{0,1},{1,0},{2,3},{3,2},{4,5},{5,4},{6,7},{7,6},{8,9},{9,8},{10,11... | collective-permute-start | bytes 24584 | tf_op jit(solution)/shard_map/ppermute | solution.py:230
  87.4 3.8 %collective-permute-start.5 = (f32[32,128]{1,0:T(8,128)S(1)}, f32[32,128]{1,0:T(8,128)S(1)}, u32[]{:S(2)}, u32[]{:S(2)}) collective-permute-start(f32[32,128]{1,0:T(8,128)S(1)} %pad_maximum_fusion.2), channel_id=1, source_target_pairs={{0,3},{3,0},{1,2},{2,1},{4,7},{7,4},{5,6},{6,5},{8,11},{11,8},{9,1... | collective-permute-start | bytes 49160 | tf_op jit(solution)/shard_map/ppermute | solution.py:230
  91.2 6.4 %collective-permute-start.6 = (f32[64,128]{1,0:T(8,128)S(1)}, f32[64,128]{1,0:T(8,128)S(1)}, u32[]{:S(2)}, u32[]{:S(2)}) collective-permute-start(f32[64,128]{1,0:T(8,128)S(1)} %pad_maximum_fusion.1), channel_id=1, source_target_pairs={{0,4},{4,0},{1,5},{5,1},{2,6},{6,2},{3,7},{7,3},{8,12},{12,8},{9,1... | collective-permute-start | bytes 98312 | tf_op jit(solution)/shard_map/ppermute | solution.py:230

commit v4 on v3

--- a/solution.py
+++ b/solution.py
@@ -71,60 +71,57 @@
         copy.wait()
 
 
-def tile_kernel(rows0, rows1, rows2, rows3, low_ref, high_ref, row_ref, keep_ref, send_ref, row_acc, col_acc):
+def tiles(shift, rows_refs, cols_refs, row_acc, first, col_acc):
+    owner = lax.axis_index("c") if shift == 0 else 1 - lax.axis_index("c")
+    at = lax.axis_index("y") * (Z * C) + owner
+    subs = [cols_ref.at[s] for cols_ref in cols_refs for s in range(cols_ref.shape[0])]
+    right_probes = jnp.concatenate([sub[:, RANK:WIDTH] for sub in subs], 0)
+    for back, rows_ref in enumerate(rows_refs):
+        flags = 4.0 * rows_ref[BLOCK:LOAD_ROWS, 0:128].astype(F32)[0:8]
+        turned = pltpu.roll(flags, lax.rem(128 - at, 128), 1)
+        right = jnp.concatenate(
+            [sub[:, 0:RANK] * turned[0:1, C * s : C * s + 1].astype(BF16) for s, sub in enumerate(subs)], 0
+        )
+        scores = lax.dot_general(
+            rows_ref[0:BLOCK, 0:RANK], right, (((1,), (1,)), ((), ())), preferred_element_type=F32
+        )
+        proximity = jnp.log(jnp.maximum(scores, 1.0)).astype(BF16)
+        row_part = jnp.dot(proximity, right_probes, preferred_element_type=F32)
+        row_acc[back] = row_part if first is None else first[back] + row_part
+        col_part = contract_rows(rows_ref[0:BLOCK, RANK:WIDTH], proximity)
+        if back == 0:
+            col_acc[...] = col_part
+        else:
+            col_acc[...] += col_part
+    gram = jnp.dot(jnp.concatenate(split(col_acc[...]), 0), right_probes, preferred_element_type=F32)
+    return gram[0:PROBES] + gram[PROBES:]
+
+
+def own_kernel(rows0, rows1, rows2, rows3, low_ref, high_ref, row_ref, keep_ref, gram_ref, col_acc):
+    gram_ref[...] = tiles(0, (rows0, rows1, rows2, rows3), (low_ref, high_ref), row_ref, None, col_acc)
+    for s in range(Z):
+        keep_ref[s] = col_acc[:, s * SUB : (s + 1) * SUB]
+
+
+def other_kernel(rows0, rows1, rows2, rows3, low_ref, high_ref, first_ref, gram_ref, row_ref, send_ref, row_acc, col_acc):
+    gram = tiles(1, (rows0, rows1, rows2, rows3), (low_ref, high_ref), row_acc, first_ref, col_acc)
     y = lax.axis_index("y")
-    core = lax.axis_index("c")
-    gram = jnp.zeros((PROBES, 2 * PROBES), F32)
-    for back, rows_ref in enumerate((rows0, rows1, rows2, rows3)):
-        flags = 4.0 * rows_ref[BLOCK:LOAD_ROWS, 0:128].astype(F32)[0:8]
-        for half in range(C):
-            owner = core if half == 0 else 1 - core
-            at = y * (Z * C) + owner
-            turned = pltpu.roll(flags, lax.rem(128 - at, 128), 1)
-            right = jnp.concatenate(
-                [
-                    (low_ref, high_ref)[s // 4][owner, s % 4, :, 0:RANK] * turned[0:1, C * s : C * s + 1].astype(BF16)
-                    for s in range(Z)
-                ],
-                0,
-            )
-            right_probes = jnp.concatenate(
-                [cols_ref[owner, :, :, RANK:WIDTH].reshape(HALF // 2, PROBES) for cols_ref in (low_ref, high_ref)], 0
-            )
-            scores = lax.dot_general(
-                rows_ref[0:BLOCK, 0:RANK], right, (((1,), (1,)), ((), ())), preferred_element_type=F32
-            )
-            proximity = jnp.log(jnp.maximum(scores, 1.0)).astype(BF16)
-            row_part = jnp.dot(proximity, right_probes, preferred_element_type=F32)
-            if half == 0:
-                row_acc[...] = row_part
-            else:
-                row_acc[...] += row_part
-            col_part = contract_rows(rows_ref[0:BLOCK, RANK:WIDTH], proximity)
-            if back == 0:
-                col_acc[half] = col_part
-            else:
-                col_acc[half] += col_part
-        high, low = split(row_acc[...])
+    for back in range(Y):
         block = lax.rem(y + Y - back, Y)
         for q in range(X):
-            row_ref[X * block + q] = high[SUB * q : SUB * (q + 1)]
-        gram += contract_rows(rows_ref[0:BLOCK, RANK:WIDTH], jnp.concatenate([high, low], 1))
-    for s in range(Z):
-        keep_ref[s] = col_acc[0, :, s * SUB : (s + 1) * SUB]
-        send_ref[s] = col_acc[1, :, s * SUB : (s + 1) * SUB]
-    gram = gram[:, 0:PROBES] + gram[:, PROBES:]
-    keep_ref[Z] = gram
-    send_ref[Z] = gram
-
-
-def join_kernel(keep_ref, got_ref, part_ref, rows_out, cols_out):
+            row_ref[X * block + q] = row_acc[back, SUB * q : SUB * (q + 1)].astype(BF16)
+    for s in range(Z):
+        send_ref[s] = col_acc[:, s * SUB : (s + 1) * SUB]
+    send_ref[Z] = gram_ref[...] + gram
+
+
+def join_kernel(keep_ref, sent_ref, got_ref, part_ref, rows_out, cols_out):
     for s in range(Z):
         cols_out[s, 0:SUB, :] = (keep_ref[s] + got_ref[s]).astype(BF16)
     core = lax.axis_index("c")
     half = PROBES // C
     at = pl.ds(pl.multiple_of(core * half, half), half)
-    gram = keep_ref[Z, at, :] + got_ref[Z, at, :]
+    gram = sent_ref[Z, at, :] + got_ref[Z, at, :]
     high, low = split(gram)
     for y in range(Y):
         for x in range(X):
@@ -174,34 +171,42 @@
     )(pair_count, factor_rows, row_side_probes, factor_cols, probe_cols, pair_blocks)
     all_rows = [row_load] + [lax.ppermute(row_load, "y", [(k, (k + s) % Y) for k in range(Y)]) for s in range(1, Y)]
     own_cols = lax.all_to_all(col_load, "z", split_axis=0, concat_axis=0, tiled=True)
-    cols = [lax.all_gather(own_cols[k : k + Z // 2], "c", axis=0, tiled=False) for k in (0, Z // 2)]
-
-    row_part, keep, send = pl.pallas_call(
-        tile_kernel,
-        out_shape=[
-            shape((Y * X, SUB, PROBES), BF16),
-            shape((Z + 1, PROBES, SUB), F32),
-            shape((Z + 1, PROBES, SUB), F32),
-        ],
+    own_cols = [own_cols[: Z // 2], own_cols[Z // 2 :]]
+    other_cols = [lax.ppermute(part, "c", SWAP) for part in own_cols]
+
+    cost = pl.CostEstimate(
+        flops=2 * Y * BLOCK * HALF * (RANK + 2 * PROBES), bytes_accessed=4 * 2**20, transcendentals=Y * BLOCK * HALF
+    )
+    first, keep, gram = pl.pallas_call(
+        own_kernel,
+        out_shape=[shape((Y, BLOCK, PROBES), F32), shape((Z, PROBES, SUB), F32), shape((PROBES, PROBES), F32)],
         in_specs=[vmem] * 6,
-        out_specs=[vmem, vmem, vmem],
-        scratch_shapes=[
-            pltpu.VMEM((BLOCK, PROBES), F32),
-            pltpu.VMEM((C, PROBES, HALF), F32),
-        ],
-        compiler_params=params,
-        name="tiles",
-    )(*all_rows, *cols)
+        out_specs=[vmem] * 3,
+        scratch_shapes=[pltpu.VMEM((PROBES, HALF), F32)],
+        compiler_params=params,
+        cost_estimate=cost,
+        name="own_tiles",
+    )(*all_rows, *own_cols)
+    row_part, send = pl.pallas_call(
+        other_kernel,
+        out_shape=[shape((Y * X, SUB, PROBES), BF16), shape((Z + 1, PROBES, SUB), F32)],
+        in_specs=[vmem] * 8,
+        out_specs=[vmem] * 2,
+        scratch_shapes=[pltpu.VMEM((Y, BLOCK, PROBES), F32), pltpu.VMEM((PROBES, HALF), F32)],
+        compiler_params=params,
+        cost_estimate=cost,
+        name="other_tiles",
+    )(*all_rows, *other_cols, first, gram)
 
     got = lax.ppermute(send, "c", SWAP)
     row_load, col_part = pl.pallas_call(
         join_kernel,
         out_shape=[shape((Y * X, SENT, PROBES), BF16), shape((Z, SUB, SUB), BF16)],
-        in_specs=[vmem, vmem, vmem],
+        in_specs=[vmem] * 4,
         out_specs=[vmem, vmem],
         compiler_params=params,
         name="join",
-    )(keep, got, row_part)
+    )(keep, send, got, row_part)
     row_got = lax.all_to_all(row_load, ("y", "x"), split_axis=0, concat_axis=0, tiled=True)
     row_sketch, col_load = pl.pallas_call(
         row_kernel,

time: 98.6 us -> 95.2 us (0.966)
  blocking collectives: 37.2 us -> 33.7 us
  starting transfers between devices: 20.7 us -> 21.7 us
    all_gather x2 -> x0, blocking collectives: 4.85 us -> none  [shards(): lax.all_gather(own_cols[k:k + Z // 2], 'c', axis=0, tiled=False)]
    all_to_all x1, blocking collectives: 13.4 us -> 14.7 us  [shards(): lax.all_to_all(col_load, 'z', split_axis=0, concat_axis=0, tiled=True)]
    pallas_call x1 -> x2, Pallas kernels: 7.77 us -> 6.87 us  [the longest x1 3.46 us: shards(): pl.pallas_call(other_kernel, out_shape=[shape((Y * X, SUB, PROBES), BF16)...]
  transfers between devices with their start and end apart: 8 -> 10, of which waited for: 5 -> 5; matrix products, arithmetic and copies ran while one was open for 0% -> 0% of each run, Pallas kernels for 0% -> 4%
where the time goes in v4:
time: 95.2 us; the launch traced here: 94.9 us
  blocking collectives  33.7 us (35%)
  waiting for transfers between devices  26.9 us (28%)
  starting transfers between devices  21.7 us (23%)
  Pallas kernels  10.6 us (11%)
  between operations  1.35 us (1%)
    all_to_all x1, blocking collectives, shards(): lax.all_to_all(row_load, ('y', 'x'), split_axis=0, concat_axis=0, tiled=T...  19 us
    all_to_all x1, waiting for transfers between devices, shards(): lax.all_to_all(col_load, 'z', split_axis=0, concat_axis=0, tiled=True)  18.5 us
    all_to_all x1, blocking collectives, shards(): lax.all_to_all(col_load, 'z', split_axis=0, concat_axis=0, tiled=True)  14.7 us
    all_to_all x1, starting transfers between devices, shards(): lax.all_to_all(col_load, 'z', split_axis=0, concat_axis=0, tiled=True)  9.16 us
    ppermute x3, waiting for transfers between devices, shards(): peer = lax.ppermute(gram, axis, pairs)  6.73 us
    ppermute x3, starting transfers between devices, shards(): peer = lax.ppermute(gram, axis, pairs)  6.3 us
    ppermute x3, starting transfers between devices, shards(): lax.ppermute(row_load, 'y', [(k, (k + s) % Y) for k in range(Y)])  5.06 us
    pallas_call x1, Pallas kernels, shards(): pl.pallas_call(other_kernel, out_shape=[shape((Y * X, SUB, PROBES), BF16)...  3.46 us
  transfers between devices with their start and end apart: 10, of which 5 were waited for; matrix products, arithmetic and copies ran while one was open for 0% of the time, Pallas kernels for 4%

profile of v4, /device:TPU:1, one launch (start us, length us, event | category | flops | bytes accessed | tf_op | source)
XLA Modules:
  0.0 94.9 jit_solution(15226474151986282212)
XLA Ops:
  1.3 2.1 %pack.1 = (bf16[528,384]{1,0:T(8,128)(2,1)}, bf16[8,128,384]{2,1,0:T(8,128)(2,1)}) custom-call(s32[1]{0:T(128)S(6)} %copy.9.count_hbm, bf16[512,256]{1,0:T(8,128)(2,1)} %factor_hbm.1, bf16[512,128]{1,0:T(8,128)(2,1)} %side_hbm.1, bf16[128,256]{1,0:T(8,128)(2,1)} %cols_hbm.1, bf16[128,128]{1,0:T(8,128)(2,1)} %probe_hbm.1, s32[1,64]{1,0:T(1,128)} %pairs_hbm.1), custom_call_target="tpu_custom_call" | custom-call | tf_op jit(solution)/shard_map/pack/pallas_call | solution.py:159
  3.4 9.2 %all-to-all-start = ((bf16[8,128,384]{2,1,0:T(8,128)(2,1)}), bf16[8,128,384]{2,1,0:T(8,128)(2,1)S(1)}, u32[]{:S(2)}, u32[]{:S(2)}) async-start(bf16[8,128,384]{2,1,0:T(8,128)(2,1)} %get-tuple-element.17), calls=%async_computation | async-start | bytes 1572864 | tf_op jit(solution)/shard_map/all_to_all | solution.py:173
  12.6 1.4 %collective-permute-start = (bf16[528,384]{1,0:T(8,128)(2,1)S(1)}, bf16[528,384]{1,0:T(8,128)(2,1)S(1)}, u32[]{:S(2)}, u32[]{:S(2)}) collective-permute-start(bf16[528,384]{1,0:T(8,128)(2,1)S(1)} %copy-done), channel_id=1, source_target_pairs={{0,64},{64,128},{128,192},{192,0},{1,65},{65,129},{129,193},{193,1... | collective-permute-start | bytes 1216520 | tf_op jit(solution)/shard_map/ppermute | solution.py:172
  14.0 2.6 %collective-permute-start.1 = (bf16[528,384]{1,0:T(8,128)(2,1)S(1)}, bf16[528,384]{1,0:T(8,128)(2,1)S(1)}, u32[]{:S(2)}, u32[]{:S(2)}) collective-permute-start(bf16[528,384]{1,0:T(8,128)(2,1)S(1)} %copy-done), channel_id=1, source_target_pairs={{0,128},{64,192},{128,0},{192,64},{1,129},{65,193},{129,1},{193,65... | collective-permute-start | bytes 1216520 | tf_op jit(solution)/shard_map/ppermute | solution.py:172
  16.6 1.1 %collective-permute-start.2 = (bf16[528,384]{1,0:T(8,128)(2,1)S(1)}, bf16[528,384]{1,0:T(8,128)(2,1)S(1)}, u32[]{:S(2)}, u32[]{:S(2)}) collective-permute-start(bf16[528,384]{1,0:T(8,128)(2,1)S(1)} %copy-done), channel_id=1, source_target_pairs={{0,192},{64,0},{128,64},{192,128},{1,193},{65,1},{129,65},{193,129... | collective-permute-start | bytes 1216520 | tf_op jit(solution)/shard_map/ppermute | solution.py:172
  17.7 18.5 %all-to-all-done = bf16[8,128,384]{2,1,0:T(8,128)(2,1)S(1)} async-done(((bf16[8,128,384]{2,1,0:T(8,128)(2,1)}), bf16[8,128,384]{2,1,0:T(8,128)(2,1)S(1)}, u32[]{:S(2)}, u32[]{:S(2)}) %all-to-all-start) | async-done | bytes 786464 | tf_op jit(solution)/shard_map/all_to_all | solution.py:173
  36.2 0.1 fusion
  36.3 0.6 collective-permute-start.3
  36.8 0.1 collective-permute-start.4
  36.9 3.4 %own_tiles.1 = (f32[4,512,128]{2,1,0:T(8,128)S(1)}, f32[8,128,128]{2,1,0:T(8,128)S(1)}, f32[128,128]{1,0:T(8,128)S(1)}) custom-call(bf16[528,384]{1,0:T(8,128)(2,1)S(1)} %copy-done, bf16[528,384]{1,0:T(8,128)(2,1)S(1)} %collective-permute-done.rows1, bf16[528,384]{1,0:T(8,128)(2,1)S(1)} %collective-permute-done.1.rows2, ...), custom_call_target="tpu_custom_call" | custom-call | flops 2147483648 | bytes 4194304 | tf_op jit(solution)/shard_map/own_tiles/pallas_call | solution.py:180
  40.4 3.5 %other_tiles.1 = (bf16[16,128,128]{2,1,0:T(8,128)(2,1)S(1)}, f32[9,128,128]{2,1,0:T(8,128)S(1)}) custom-call(bf16[528,384]{1,0:T(8,128)(2,1)S(1)} %copy-done, bf16[528,384]{1,0:T(8,128)(2,1)S(1)} %collective-permute-done.rows1, bf16[528,384]{1,0:T(8,128)(2,1)S(1)} %collective-permute-done.1.rows2, bf16[528,384]{1,0:T(8,128)(2,1)S(1)} %collective-permute-done.2.rows3, ...), custom_call_target="tpu_custom_call" | custom-call | flops 2147483648 | bytes 4194304 | tf_op jit(solution)/shard_map/other_tiles/pallas_call | solution.py:190
  43.8 0.5 collective-permute-start.5
  44.3 1.6 %collective-permute-done.5.got_ref = f32[9,128,128]{2,1,0:T(8,128)S(1)} collective-permute-done((f32[9,128,128]{2,1,0:T(8,128)S(1)}, f32[9,128,128]{2,1,0:T(8,128)S(1)}, u32[]{:S(2)}, u32[]{:S(2)}) %collective-permute-start.5) | collective-permute-done | bytes 589856 | tf_op jit(solution)/shard_map/ppermute | solution.py:201
  46.0 0.1 join.1
  46.1 19.0 %all_to_all.15.got_ref = bf16[16,160,128]{2,1,0:T(8,128)(2,1)S(1)} all-to-all(bf16[16,160,128]{2,1,0:T(8,128)(2,1)S(1)} %get-tuple-element.23), channel_id=1, replica_groups=mesh['y'=4,'z'=8,'c'=2,'x'=4] {'y','x'}, dimensions={0} | all-to-all | bytes 1310720 | tf_op jit(solution)/shard_map/all_to_all | solution.py:210
  65.0 0.7 row_sum.1
  65.8 14.7 %all_to_all.16.got_ref = bf16[8,160,128]{2,1,0:T(8,128)(2,1)S(1)} all-to-all(bf16[8,160,128]{2,1,0:T(8,128)(2,1)S(1)} %get-tuple-element.26), channel_id=1, replica_groups=mesh['y'=4,'z'=8,'c'=2,'x'=4] {'z'}, dimensions={0} | all-to-all | bytes 655360 | tf_op jit(solution)/shard_map/all_to_all | solution.py:219
  80.5 0.7 col_sum.1
  81.2 2.5 %collective-permute-done.6 = f32[16,128]{1,0:T(8,128)S(1)} collective-permute-done((f32[16,128]{1,0:T(8,128)S(1)}, f32[16,128]{1,0:T(8,128)S(1)}, u32[]{:S(2)}, u32[]{:S(2)}) %collective-permute-start.6) | collective-permute-done | bytes 8224 | tf_op jit(solution)/shard_map/ppermute | solution.py:235
  83.7 0.4 collective-permute-start.7
  84.2 3.4 %collective-permute-done.7 = f32[32,128]{1,0:T(8,128)S(1)} collective-permute-done((f32[32,128]{1,0:T(8,128)S(1)}, f32[32,128]{1,0:T(8,128)S(1)}, u32[]{:S(2)}, u32[]{:S(2)}) %collective-permute-start.7) | collective-permute-done | bytes 16416 | tf_op jit(solution)/shard_map/ppermute | solution.py:235
  87.5 5.9 %collective-permute-start.8 = (f32[64,128]{1,0:T(8,128)S(1)}, f32[64,128]{1,0:T(8,128)S(1)}, u32[]{:S(2)}, u32[]{:S(2)}) collective-permute-start(f32[64,128]{1,0:T(8,128)S(1)} %pad_maximum_fusion.1), channel_id=1, source_target_pairs={{0,4},{4,0},{1,5},{5,1},{2,6},{6,2},{3,7},{7,3},{8,12},{12,8},{9,1... | collective-permute-start | bytes 98312 | tf_op jit(solution)/shard_map/ppermute | solution.py:235
  93.4 0.9 collective-permute-done.8
  94.3 0.6 pad_maximum_fusion
  (13 shorter events, 0.0 us)
Async XLA Ops:
  3.4 9.2 %copy-start = (bf16[528,384]{1,0:T(8,128)(2,1)S(1)}, bf16[528,384]{1,0:T(8,128)(2,1)}, u32[]{:S(2)}) copy-start(bf16[528,384]{1,0:T(8,128)(2,1)} %get-tuple-element.16.rows0) | copy-start | bytes 1216516
  3.4 32.7 %all-to-all-start = ((bf16[8,128,384]{2,1,0:T(8,128)(2,1)}), bf16[8,128,384]{2,1,0:T(8,128)(2,1)S(1)}, u32[]{:S(2)}, u32[]{:S(2)}) async-start(bf16[8,128,384]{2,1,0:T(8,128)(2,1)} %get-tuple-element.17), calls=%async_computation | async-start | bytes 1572864 | tf_op jit(solution)/shard_map/all_to_all | solution.py:173
  12.6 24.3 %collective-permute-start = (bf16[528,384]{1,0:T(8,128)(2,1)S(1)}, bf16[528,384]{1,0:T(8,128)(2,1)S(1)}, u32[]{:S(2)}, u32[]{:S(2)}) collective-permute-start(bf16[528,384]{1,0:T(8,128)(2,1)S(1)} %copy-done), channel_id=1, source_target_pairs={{0,64},{64,128},{128,192},{192,0},{1,65},{65,129},{129,193},{193,1... | collective-permute-start | bytes 1216520 | tf_op jit(solution)/shard_map/ppermute | solution.py:172
  14.0 23.0 %collective-permute-start.1 = (bf16[528,384]{1,0:T(8,128)(2,1)S(1)}, bf16[528,384]{1,0:T(8,128)(2,1)S(1)}, u32[]{:S(2)}, u32[]{:S(2)}) collective-permute-start(bf16[528,384]{1,0:T(8,128)(2,1)S(1)} %copy-done), channel_id=1, source_target_pairs={{0,128},{64,192},{128,0},{192,64},{1,129},{65,193},{129,1},{193,65... | collective-permute-start | bytes 1216520 | tf_op jit(solution)/shard_map/ppermute | solution.py:172
  16.6 20.3 %collective-permute-start.2 = (bf16[528,384]{1,0:T(8,128)(2,1)S(1)}, bf16[528,384]{1,0:T(8,128)(2,1)S(1)}, u32[]{:S(2)}, u32[]{:S(2)}) collective-permute-start(bf16[528,384]{1,0:T(8,128)(2,1)S(1)} %copy-done), channel_id=1, source_target_pairs={{0,192},{64,0},{128,64},{192,128},{1,193},{65,1},{129,65},{193,129... | collective-permute-start | bytes 1216520 | tf_op jit(solution)/shard_map/ppermute | solution.py:172
  36.3 4.1 %collective-permute-start.3 = (bf16[4,128,384]{2,1,0:T(8,128)(2,1)S(1)}, bf16[4,128,384]{2,1,0:T(8,128)(2,1)S(1)}, u32[]{:S(2)}, u32[]{:S(2)}) collective-permute-start(bf16[4,128,384]{2,1,0:T(8,128)(2,1)S(1)} %get-tuple-element.30.low_ref), channel_id=1, source_target_pairs={{0,4},{4,0},{1,5},{5,1},{2,6},{6,2},{3,7},{7,3},{8,12},{12,8},{9,1... | collective-permute-start | bytes 1179656 | tf_op jit(solution)/shard_map/ppermute | solution.py:175
  36.8 3.5 %collective-permute-start.4 = (bf16[4,128,384]{2,1,0:T(8,128)(2,1)S(1)}, bf16[4,128,384]{2,1,0:T(8,128)(2,1)S(1)}, u32[]{:S(2)}, u32[]{:S(2)}) collective-permute-start(bf16[4,128,384]{2,1,0:T(8,128)(2,1)S(1)} %get-tuple-element.29.high_ref), channel_id=1, source_target_pairs={{0,4},{4,0},{1,5},{5,1},{2,6},{6,2},{3,7},{7,3},{8,12},{12,8},{9,1... | collective-permute-start | bytes 1179656 | tf_op jit(solution)/shard_map/ppermute | solution.py:175
  43.8 2.1 %collective-permute-start.5 = (f32[9,128,128]{2,1,0:T(8,128)S(1)}, f32[9,128,128]{2,1,0:T(8,128)S(1)}, u32[]{:S(2)}, u32[]{:S(2)}) collective-permute-start(f32[9,128,128]{2,1,0:T(8,128)S(1)} %get-tuple-element.21.sent_ref), channel_id=1, source_target_pairs={{0,4},{4,0},{1,5},{5,1},{2,6},{6,2},{3,7},{7,3},{8,12},{12,8},{9,1... | collective-permute-start | bytes 1769480 | tf_op jit(solution)/shard_map/ppermute | solution.py:201
  81.2 2.5 %collective-permute-start.6 = (f32[16,128]{1,0:T(8,128)S(1)}, f32[16,128]{1,0:T(8,128)S(1)}, u32[]{:S(2)}, u32[]{:S(2)}) collective-permute-start(f32[16,128]{1,0:T(8,128)S(1)} %get-tuple-element.28), channel_id=1, source_target_pairs={{0,1},{1,0},{2,3},{3,2},{4,5},{5,4},{6,7},{7,6},{8,9},{9,8},{10,11... | collective-permute-start | bytes 24584 | tf_op jit(solution)/shard_map/ppermute | solution.py:235
  83.7 3.8 %collective-permute-start.7 = (f32[32,128]{1,0:T(8,128)S(1)}, f32[32,128]{1,0:T(8,128)S(1)}, u32[]{:S(2)}, u32[]{:S(2)}) collective-permute-start(f32[32,128]{1,0:T(8,128)S(1)} %pad_maximum_fusion.2), channel_id=1, source_target_pairs={{0,3},{3,0},{1,2},{2,1},{4,7},{7,4},{5,6},{6,5},{8,11},{11,8},{9,1... | collective-permute-start | bytes 49160 | tf_op jit(solution)/shard_map/ppermute | solution.py:235
  87.5 6.7 %collective-permute-start.8 = (f32[64,128]{1,0:T(8,128)S(1)}, f32[64,128]{1,0:T(8,128)S(1)}, u32[]{:S(2)}, u32[]{:S(2)}) collective-permute-start(f32[64,128]{1,0:T(8,128)S(1)} %pad_maximum_fusion.1), channel_id=1, source_target_pairs={{0,4},{4,0},{1,5},{5,1},{2,6},{6,2},{3,7},{7,3},{8,12},{12,8},{9,1... | collective-permute-start | bytes 98312 | tf_op jit(solution)/shard_map/ppermute | solution.py:235

commit v5 on v4

--- a/solution.py
+++ b/solution.py
@@ -17,12 +17,16 @@
 LOAD_ROWS = BLOCK + MASK_ROWS
 HALF = Z * SUB
 NODES = BLOCKS * BLOCK
-PIECE = PROBES // (C * X)
-SENT = SUB + 2 * PIECE
+TERMS = 1
+SENT = SUB + TERMS * PROBES // C
 SCALE = 1.0 / math.sqrt(NODES)
 LIMIT = 40 * 2**20
 WHOLE = 60 * 2**20
 SWAP = [(0, 1), (1, 0)]
+
+
+def ring(size, shift):
+    return [(k, (k + shift) % size) for k in range(size)]
 
 
 def contract_rows(left, right):
@@ -103,51 +107,42 @@
         keep_ref[s] = col_acc[:, s * SUB : (s + 1) * SUB]
 
 
-def other_kernel(rows0, rows1, rows2, rows3, low_ref, high_ref, first_ref, gram_ref, row_ref, send_ref, row_acc, col_acc):
+def other_kernel(
+    rows0, rows1, rows2, rows3, low_ref, high_ref, first_ref, gram_ref, piece0, piece1, piece2, piece3, send_ref, row_acc, col_acc
+):
     gram = tiles(1, (rows0, rows1, rows2, rows3), (low_ref, high_ref), row_acc, first_ref, col_acc)
-    y = lax.axis_index("y")
-    for back in range(Y):
-        block = lax.rem(y + Y - back, Y)
-        for q in range(X):
-            row_ref[X * block + q] = row_acc[back, SUB * q : SUB * (q + 1)].astype(BF16)
+    x = lax.axis_index("x")
+    for ahead, piece in enumerate((piece0, piece1, piece2, piece3)):
+        at = pl.ds(pl.multiple_of(SUB * lax.rem(x + ahead, X), SUB), SUB)
+        for back in range(Y):
+            piece[back] = row_acc[back, at, :].astype(piece.dtype)
     for s in range(Z):
         send_ref[s] = col_acc[:, s * SUB : (s + 1) * SUB]
     send_ref[Z] = gram_ref[...] + gram
 
 
-def join_kernel(keep_ref, sent_ref, got_ref, part_ref, rows_out, cols_out):
+def join_kernel(keep_ref, sent_ref, got_ref, cols_out):
+    half = PROBES // C
+    at = pl.ds(pl.multiple_of(lax.axis_index("c") * half, half), half)
+    parts = split(sent_ref[Z, at, :] + got_ref[Z, at, :])
     for s in range(Z):
         cols_out[s, 0:SUB, :] = (keep_ref[s] + got_ref[s]).astype(BF16)
-    core = lax.axis_index("c")
+        for k in range(TERMS):
+            cols_out[s, SUB + half * k : SUB + half * (k + 1), :] = parts[k]
+
+
+def piece_kernel(kept_ref, got1, got2, got3, col_ref, out0, out1, out2, out3, gram_out):
     half = PROBES // C
-    at = pl.ds(pl.multiple_of(core * half, half), half)
-    gram = sent_ref[Z, at, :] + got_ref[Z, at, :]
-    high, low = split(gram)
-    for y in range(Y):
-        for x in range(X):
-            rows_out[X * y + x, 0:SUB, :] = part_ref[X * y + x]
-            rows_out[X * y + x, SUB : SUB + PIECE, :] = high[PIECE * x : PIECE * (x + 1)]
-            rows_out[X * y + x, SUB + PIECE : SENT, :] = low[PIECE * x : PIECE * (x + 1)]
-
-
-def row_kernel(got_ref, cols_ref, sketch_ref, cols_out):
-    total = got_ref[0].astype(F32)
-    for k in range(1, Y * X):
-        total += got_ref[k].astype(F32)
-    sketch_ref[...] = total[0:SUB] * SCALE
-    high, low = split(total[SUB : SUB + PIECE] + total[SUB + PIECE : SENT])
-    for s in range(Z):
-        cols_out[s, 0:SUB, :] = cols_ref[s]
-        cols_out[s, SUB : SUB + PIECE, :] = high
-        cols_out[s, SUB + PIECE : SENT, :] = low
-
-
-def col_kernel(got_ref, sketch_ref, gram_ref):
-    total = got_ref[0].astype(F32)
-    for k in range(1, Z):
-        total += got_ref[k].astype(F32)
-    sketch_ref[...] = total[0:SUB].T * SCALE
-    gram_ref[...] = (total[SUB : SUB + PIECE] + total[SUB + PIECE : SENT]) * (1.0 / NODES)
+    gram = col_ref[SUB : SUB + half]
+    for k in range(1, TERMS):
+        gram += col_ref[SUB + half * k : SUB + half * (k + 1)]
+    for k in range(Y * X):
+        gram_out[k] = gram
+    for back, out in enumerate((out0, out1, out2, out3)):
+        total = kept_ref[back]
+        for got in (got1, got2, got3):
+            total += got[back].astype(F32)
+        out[...] = total
 
 
 def shards(factor_rows, row_side_probes, factor_cols, probe_cols, pair_blocks, pair_count):
@@ -169,7 +164,7 @@
         compiler_params=pltpu.CompilerParams(vmem_limit_bytes=WHOLE),
         name="pack",
     )(pair_count, factor_rows, row_side_probes, factor_cols, probe_cols, pair_blocks)
-    all_rows = [row_load] + [lax.ppermute(row_load, "y", [(k, (k + s) % Y) for k in range(Y)]) for s in range(1, Y)]
+    all_rows = [row_load] + [lax.ppermute(row_load, "y", ring(Y, s)) for s in range(1, Y)]
     own_cols = lax.all_to_all(col_load, "z", split_axis=0, concat_axis=0, tiled=True)
     own_cols = [own_cols[: Z // 2], own_cols[Z // 2 :]]
     other_cols = [lax.ppermute(part, "c", SWAP) for part in own_cols]
@@ -187,11 +182,13 @@
         cost_estimate=cost,
         name="own_tiles",
     )(*all_rows, *own_cols)
-    row_part, send = pl.pallas_call(
+    *pieces, send = pl.pallas_call(
         other_kernel,
-        out_shape=[shape((Y * X, SUB, PROBES), BF16), shape((Z + 1, PROBES, SUB), F32)],
+        out_shape=[shape((Y, SUB, PROBES), F32)]
+        + [shape((Y, SUB, PROBES), BF16)] * (X - 1)
+        + [shape((Z + 1, PROBES, SUB), F32)],
         in_specs=[vmem] * 8,
-        out_specs=[vmem] * 2,
+        out_specs=[vmem] * 5,
         scratch_shapes=[pltpu.VMEM((Y, BLOCK, PROBES), F32), pltpu.VMEM((PROBES, HALF), F32)],
         compiler_params=params,
         cost_estimate=cost,
@@ -199,42 +196,37 @@
     )(*all_rows, *other_cols, first, gram)
 
     got = lax.ppermute(send, "c", SWAP)
-    row_load, col_part = pl.pallas_call(
+    got_pieces = [lax.ppermute(pieces[s], "x", ring(X, s)) for s in range(1, X)]
+    col_load = pl.pallas_call(
         join_kernel,
-        out_shape=[shape((Y * X, SENT, PROBES), BF16), shape((Z, SUB, SUB), BF16)],
-        in_specs=[vmem] * 4,
-        out_specs=[vmem, vmem],
+        out_shape=shape((Z, SENT, SUB), BF16),
+        in_specs=[vmem] * 3,
+        out_specs=vmem,
         compiler_params=params,
         name="join",
-    )(keep, send, got, row_part)
-    row_got = lax.all_to_all(row_load, ("y", "x"), split_axis=0, concat_axis=0, tiled=True)
-    row_sketch, col_load = pl.pallas_call(
-        row_kernel,
-        out_shape=[shape((SUB, PROBES), F32), shape((Z, SENT, SUB), BF16)],
-        in_specs=[vmem, vmem],
-        out_specs=[vmem, vmem],
-        compiler_params=params,
-        name="row_sum",
-    )(row_got, col_part)
+    )(keep, send, got)
     col_got = lax.all_to_all(col_load, "z", split_axis=0, concat_axis=0, tiled=True)
-    col_sketch, gram = pl.pallas_call(
-        col_kernel,
-        out_shape=[shape((SUB, PROBES), F32), shape((PIECE, PROBES), F32)],
-        in_specs=[vmem],
-        out_specs=[vmem, vmem],
-        compiler_params=params,
-        name="col_sum",
-    )(col_got)
-
-    x, c = lax.axis_index("x"), lax.axis_index("c")
-    for axis, pairs, upper in (
-        ("x", [(0, 1), (1, 0), (2, 3), (3, 2)], lax.rem(x, 2) == 1),
-        ("x", [(0, 3), (3, 0), (1, 2), (2, 1)], x >= 2),
-        ("c", SWAP, c == 1),
-    ):
-        peer = lax.ppermute(gram, axis, pairs)
-        gram = jnp.concatenate([jnp.where(upper, peer, gram), jnp.where(upper, gram, peer)], 0)
-    return (row_sketch, col_sketch, gram)
+    col_sum = jnp.sum(col_got.astype(F32), 0)
+    half = PROBES // C
+    col_sketch = col_sum[:SUB].T * SCALE
+
+    *sums, gram = pl.pallas_call(
+        piece_kernel,
+        out_shape=[shape((SUB, PROBES), F32)] * Y + [shape((Y * X, half, PROBES), F32)],
+        in_specs=[vmem] * 5,
+        out_specs=[vmem] * 5,
+        compiler_params=params,
+        name="pieces",
+    )(pieces[0], *got_pieces, col_sum)
+    got_sums = [lax.ppermute(sums[back], "y", ring(Y, Y - back)) for back in range(1, Y)]
+    row_sketch = (sums[0] + got_sums[0] + got_sums[1] + got_sums[2]) * SCALE
+
+    gram = lax.all_to_all(gram, ("y", "x"), split_axis=0, concat_axis=0, tiled=True)
+    gram = jnp.sum(gram, 0) * (1.0 / NODES)
+    peer = lax.ppermute(gram, "c", SWAP)
+    upper = lax.axis_index("c") == 1
+    sketch_gram = jnp.concatenate([jnp.where(upper, peer, gram), jnp.where(upper, gram, peer)], 0)
+    return (row_sketch, col_sketch, sketch_gram)
 
 
 def solution(mesh):

time: 95.2 us -> 88.5 us (0.930)
  blocking collectives: 33.7 us -> 0 us
  starting transfers between devices: 21.7 us -> 38.7 us
  waiting for transfers between devices: 26.9 us -> 35 us
    all_to_all x2 -> x0, blocking collectives: 33.7 us -> none  [the longest x1 19 us: shards(): lax.all_to_all(row_load, ('y', 'x'), split_axis=0, concat_axis=0, tiled=T...]
    all_to_all x1 -> x2, waiting for transfers between devices: 18.5 us -> 28.8 us  [shards(): lax.all_to_all(col_load, 'z', split_axis=0, concat_axis=0, tiled=True)]
    ppermute x6 -> x10, waiting for transfers between devices: 6.74 us -> 0.22 us  [the longest x1 0.2 us: shards(): peer = lax.ppermute(gram, 'c', SWAP)]
    all_to_all x0 -> x1, starting transfers between devices: none -> 6.14 us  [shards(): lax.all_to_all(gram, ('y', 'x'), split_axis=0, concat_axis=0, tiled=True)]
    ppermute x6 -> x10, starting transfers between devices: 11.4 us -> 17.5 us  [the longest x3 5.55 us: shards(): lax.ppermute(sums[back], 'y', ring(Y, Y - back))]
    all_to_all x1 -> x2, starting transfers between devices: 9.16 us -> 14 us  [shards(): lax.all_to_all(col_load, 'z', split_axis=0, concat_axis=0, tiled=True)]
    all_to_all x0 -> x1, waiting for transfers between devices: none -> 4.29 us  [shards(): lax.all_to_all(gram, ('y', 'x'), split_axis=0, concat_axis=0, tiled=True)]
    pallas_call x4 -> x3, Pallas kernels: 5.01 us -> 5.26 us  [the longest x1 3.59 us: shards(): pl.pallas_call(other_kernel, out_shape=[shape((Y, SUB, PROBES), F32)] + [...]
  transfers between devices with their start and end apart: 10 -> 16, of which waited for: 5 -> 5; matrix products, arithmetic and copies ran while one was open for 0% -> 2% of each run, Pallas kernels for 4% -> 4%
where the time goes in v5:
time: 88.5 us; the launch traced here: 88.2 us
  starting transfers between devices  38.7 us (44%)
  waiting for transfers between devices  35 us (40%)
  Pallas kernels  10.8 us (12%)
  other arithmetic  1.39 us (2%)
  between operations  1.39 us (2%)
    all_to_all x2, waiting for transfers between devices, shards(): lax.all_to_all(col_load, 'z', split_axis=0, concat_axis=0, tiled=True)  28.8 us
    all_to_all x2, starting transfers between devices, shards(): lax.all_to_all(col_load, 'z', split_axis=0, concat_axis=0, tiled=True)  14 us
    all_to_all x1, starting transfers between devices, shards(): lax.all_to_all(gram, ('y', 'x'), split_axis=0, concat_axis=0, tiled=True)  6.14 us
    ppermute x3, starting transfers between devices, shards(): lax.ppermute(sums[back], 'y', ring(Y, Y - back))  5.55 us
    ppermute x3, starting transfers between devices, shards(): lax.ppermute(row_load, 'y', ring(Y, s))  5.06 us
    ppermute x3, starting transfers between devices, shards(): got_pieces = [lax.ppermute(pieces[s], 'x', ring(X, s)) for s in range(1, X)]  4.81 us
    all_to_all x1, waiting for transfers between devices, shards(): lax.all_to_all(gram, ('y', 'x'), split_axis=0, concat_axis=0, tiled=True)  4.29 us
    pallas_call x1, Pallas kernels, shards(): pl.pallas_call(other_kernel, out_shape=[shape((Y, SUB, PROBES), F32)] + [...  3.59 us
  transfers between devices with their start and end apart: 16, of which 5 were waited for; matrix products, arithmetic and copies ran while one was open for 2% of the time, Pallas kernels for 4%

profile of v5, /device:TPU:1, one launch (start us, length us, event | category | flops | bytes accessed | tf_op | source)
XLA Modules:
  0.0 88.2 jit_solution(9248898457154976819)
XLA Ops:
  1.3 2.1 %pack.1 = (bf16[528,384]{1,0:T(8,128)(2,1)}, bf16[8,128,384]{2,1,0:T(8,128)(2,1)}) custom-call(s32[1]{0:T(128)S(6)} %copy.10.count_hbm, bf16[512,256]{1,0:T(8,128)(2,1)} %factor_hbm.1, bf16[512,128]{1,0:T(8,128)(2,1)} %side_hbm.1, bf16[128,256]{1,0:T(8,128)(2,1)} %cols_hbm.1, bf16[128,128]{1,0:T(8,128)(2,1)} %probe_hbm.1, s32[1,64]{1,0:T(1,128)} %pairs_hbm.1), custom_call_target="tpu_custom_call" | custom-call | tf_op jit(solution)/shard_map/pack/pallas_call | solution.py:154
  3.4 9.2 %all-to-all-start = ((bf16[8,128,384]{2,1,0:T(8,128)(2,1)}), bf16[8,128,384]{2,1,0:T(8,128)(2,1)S(1)}, u32[]{:S(2)}, u32[]{:S(2)}) async-start(bf16[8,128,384]{2,1,0:T(8,128)(2,1)} %get-tuple-element.19), calls=%async_computation | async-start | bytes 1572864 | tf_op jit(solution)/shard_map/all_to_all | solution.py:168
  12.6 1.4 %collective-permute-start = (bf16[528,384]{1,0:T(8,128)(2,1)S(1)}, bf16[528,384]{1,0:T(8,128)(2,1)S(1)}, u32[]{:S(2)}, u32[]{:S(2)}) collective-permute-start(bf16[528,384]{1,0:T(8,128)(2,1)S(1)} %copy-done), channel_id=1, source_target_pairs={{0,64},{64,128},{128,192},{192,0},{1,65},{65,129},{129,193},{193,1... | collective-permute-start | bytes 1216520 | tf_op jit(solution)/shard_map/ppermute | solution.py:167
  14.0 2.6 %collective-permute-start.1 = (bf16[528,384]{1,0:T(8,128)(2,1)S(1)}, bf16[528,384]{1,0:T(8,128)(2,1)S(1)}, u32[]{:S(2)}, u32[]{:S(2)}) collective-permute-start(bf16[528,384]{1,0:T(8,128)(2,1)S(1)} %copy-done), channel_id=1, source_target_pairs={{0,128},{64,192},{128,0},{192,64},{1,129},{65,193},{129,1},{193,65... | collective-permute-start | bytes 1216520 | tf_op jit(solution)/shard_map/ppermute | solution.py:167
  16.6 1.1 %collective-permute-start.2 = (bf16[528,384]{1,0:T(8,128)(2,1)S(1)}, bf16[528,384]{1,0:T(8,128)(2,1)S(1)}, u32[]{:S(2)}, u32[]{:S(2)}) collective-permute-start(bf16[528,384]{1,0:T(8,128)(2,1)S(1)} %copy-done), channel_id=1, source_target_pairs={{0,192},{64,0},{128,64},{192,128},{1,193},{65,1},{129,65},{193,129... | collective-permute-start | bytes 1216520 | tf_op jit(solution)/shard_map/ppermute | solution.py:167
  17.7 18.5 %all-to-all-done = bf16[8,128,384]{2,1,0:T(8,128)(2,1)S(1)} async-done(((bf16[8,128,384]{2,1,0:T(8,128)(2,1)}), bf16[8,128,384]{2,1,0:T(8,128)(2,1)S(1)}, u32[]{:S(2)}, u32[]{:S(2)}) %all-to-all-start) | async-done | bytes 786464 | tf_op jit(solution)/shard_map/all_to_all | solution.py:168
  37.0 3.4 %own_tiles.1 = (f32[4,512,128]{2,1,0:T(8,128)S(1)}, f32[8,128,128]{2,1,0:T(8,128)S(1)}, f32[128,128]{1,0:T(8,128)S(1)}) custom-call(bf16[528,384]{1,0:T(8,128)(2,1)S(1)} %copy-done, bf16[528,384]{1,0:T(8,128)(2,1)S(1)} %collective-permute-done.rows1, bf16[528,384]{1,0:T(8,128)(2,1)S(1)} %collective-permute-done.1.rows2, ...), custom_call_target="tpu_custom_call" | custom-call | flops 2147483648 | bytes 4194304 | tf_op jit(solution)/shard_map/own_tiles/pallas_call | solution.py:175
  40.4 3.6 %other_tiles.1 = (f32[4,128,128]{2,1,0:T(8,128)S(1)}, bf16[4,128,128]{2,1,0:T(8,128)(2,1)S(1)}, bf16[4,128,128]{2,1,0:T(8,128)(2,1)S(1)}, bf16[4,128,128]{2,1,0:T(8,128)(2,1)S(1)}, f32[9,128,128]{2,1,0:T(8,128)S(1)}) custom-call(bf16[528,384]{1,0:T(8,128)(2,1)S(1)} %copy-done, bf16[528,384]{1,0:T(8,128)(2,1)S(1)} %collective-permute-done.rows1, ...), custom_call_target="tpu_custom_call" | custom-call | flops 2147483648 | bytes 4194304 | tf_op jit(solution)/shard_map/other_tiles/pallas_call | solution.py:185
  44.5 1.6 %collective-permute-done.8.got_ref = f32[9,128,128]{2,1,0:T(8,128)S(1)} collective-permute-done((f32[9,128,128]{2,1,0:T(8,128)S(1)}, f32[9,128,128]{2,1,0:T(8,128)S(1)}, u32[]{:S(2)}, u32[]{:S(2)}) %collective-permute-start.8) | collective-permute-done | bytes 589856 | tf_op jit(solution)/shard_map/ppermute | solution.py:198
  46.1 0.8 join.1
  46.9 4.8 %all-to-all-start.1 = ((bf16[8,192,128]{2,1,0:T(8,128)(2,1)}), bf16[8,192,128]{2,1,0:T(8,128)(2,1)S(1)}, u32[]{:S(2)}, u32[]{:S(2)}) async-start(bf16[8,192,128]{2,1,0:T(8,128)(2,1)} %join.1), calls=%async_computation.1 | async-start | bytes 786432 | tf_op jit(solution)/shard_map/all_to_all | solution.py:208
  51.7 1.2 %collective-permute-start.5 = (bf16[4,128,128]{2,1,0:T(8,128)(2,1)S(1)}, bf16[4,128,128]{2,1,0:T(8,128)(2,1)S(1)}, u32[]{:S(2)}, u32[]{:S(2)}) collective-permute-start(bf16[4,128,128]{2,1,0:T(8,128)(2,1)S(1)} %get-tuple-element.23), channel_id=1, source_target_pairs={{0,1},{1,2},{2,3},{3,0},{4,5},{5,6},{6,7},{7,4},{8,9},{9,10},{10,1... | collective-permute-start | bytes 393224 | tf_op jit(solution)/shard_map/ppermute | solution.py:199
  53.0 2.5 %collective-permute-start.6 = (bf16[4,128,128]{2,1,0:T(8,128)(2,1)S(1)}, bf16[4,128,128]{2,1,0:T(8,128)(2,1)S(1)}, u32[]{:S(2)}, u32[]{:S(2)}) collective-permute-start(bf16[4,128,128]{2,1,0:T(8,128)(2,1)S(1)} %get-tuple-element.24), channel_id=1, source_target_pairs={{0,2},{1,3},{2,0},{3,1},{4,6},{5,7},{6,4},{7,5},{8,10},{9,11},{10,... | collective-permute-start | bytes 393224 | tf_op jit(solution)/shard_map/ppermute | solution.py:199
  55.4 1.1 %collective-permute-start.7 = (bf16[4,128,128]{2,1,0:T(8,128)(2,1)S(1)}, bf16[4,128,128]{2,1,0:T(8,128)(2,1)S(1)}, u32[]{:S(2)}, u32[]{:S(2)}) collective-permute-start(bf16[4,128,128]{2,1,0:T(8,128)(2,1)S(1)} %get-tuple-element.25), channel_id=1, source_target_pairs={{0,3},{1,0},{2,1},{3,2},{4,7},{5,4},{6,5},{7,6},{8,11},{9,8},{10,9... | collective-permute-start | bytes 393224 | tf_op jit(solution)/shard_map/ppermute | solution.py:199
  56.6 10.3 %all-to-all-done.1 = bf16[8,192,128]{2,1,0:T(8,128)(2,1)S(1)} async-done(((bf16[8,192,128]{2,1,0:T(8,128)(2,1)}), bf16[8,192,128]{2,1,0:T(8,128)(2,1)S(1)}, u32[]{:S(2)}, u32[]{:S(2)}) %all-to-all-start.1) | async-done | bytes 393248 | tf_op jit(solution)/shard_map/all_to_all | solution.py:208
  67.0 0.9 pieces.1
  67.8 6.1 %all-to-all-start.2 = ((f32[16,64,128]{2,1,0:T(8,128)}), f32[16,64,128]{2,1,0:T(8,128)S(1)}, u32[]{:S(2)}, u32[]{:S(2)}) async-start(f32[16,64,128]{2,1,0:T(8,128)} %get-tuple-element.32), calls=%async_computation.2 | async-start | bytes 1048576 | tf_op jit(solution)/shard_map/all_to_all | solution.py:224
  74.0 2.9 %collective-permute-start.10 = (f32[128,128]{1,0:T(8,128)S(1)}, f32[128,128]{1,0:T(8,128)S(1)}, u32[]{:S(2)}, u32[]{:S(2)}) collective-permute-start(f32[128,128]{1,0:T(8,128)S(1)} %get-tuple-element.30), channel_id=1, source_target_pairs={{0,128},{64,192},{128,0},{192,64},{1,129},{65,193},{129,1},{193,65... | collective-permute-start | bytes 196616 | tf_op jit(solution)/shard_map/ppermute | solution.py:221
  77.1 2.4 %collective-permute-start.9 = (f32[128,128]{1,0:T(8,128)S(1)}, f32[128,128]{1,0:T(8,128)S(1)}, u32[]{:S(2)}, u32[]{:S(2)}) collective-permute-start(f32[128,128]{1,0:T(8,128)S(1)} %get-tuple-element.29), channel_id=1, source_target_pairs={{0,192},{64,0},{128,64},{192,128},{1,193},{65,1},{129,65},{193,129... | collective-permute-start | bytes 196616 | tf_op jit(solution)/shard_map/ppermute | solution.py:221
  79.5 0.7 copy.9
  80.3 4.3 %all-to-all-done.2 = f32[16,64,128]{2,1,0:T(8,128)S(1)} async-done(((f32[16,64,128]{2,1,0:T(8,128)}), f32[16,64,128]{2,1,0:T(8,128)S(1)}, u32[]{:S(2)}, u32[]{:S(2)}) %all-to-all-start.2) | async-done | bytes 524320 | tf_op jit(solution)/shard_map/all_to_all | solution.py:224
  84.6 2.0 %collective-permute-start.12 = (f32[64,128]{1,0:T(8,128)S(1)}, f32[64,128]{1,0:T(8,128)S(1)}, u32[]{:S(2)}, u32[]{:S(2)}) collective-permute-start(f32[64,128]{1,0:T(8,128)S(1)} %broadcast_multiply_fusion), channel_id=1, source_target_pairs={{0,4},{4,0},{1,5},{5,1},{2,6},{6,2},{3,7},{7,3},{8,12},{12,8},{9,1... | collective-permute-start | bytes 98312 | tf_op jit(solution)/shard_map/ppermute | solution.py:226
  86.7 0.6 add_multiply_fusion
  87.5 0.6 pad_maximum_fusion
  (24 shorter events, 1.9 us)
Async XLA Ops:
  3.4 9.2 %copy-start = (bf16[528,384]{1,0:T(8,128)(2,1)S(1)}, bf16[528,384]{1,0:T(8,128)(2,1)}, u32[]{:S(2)}) copy-start(bf16[528,384]{1,0:T(8,128)(2,1)} %get-tuple-element.18.rows0) | copy-start | bytes 1216516
  3.4 32.7 %all-to-all-start = ((bf16[8,128,384]{2,1,0:T(8,128)(2,1)}), bf16[8,128,384]{2,1,0:T(8,128)(2,1)S(1)}, u32[]{:S(2)}, u32[]{:S(2)}) async-start(bf16[8,128,384]{2,1,0:T(8,128)(2,1)} %get-tuple-element.19), calls=%async_computation | async-start | bytes 1572864 | tf_op jit(solution)/shard_map/all_to_all | solution.py:168
  12.6 24.3 %collective-permute-start = (bf16[528,384]{1,0:T(8,128)(2,1)S(1)}, bf16[528,384]{1,0:T(8,128)(2,1)S(1)}, u32[]{:S(2)}, u32[]{:S(2)}) collective-permute-start(bf16[528,384]{1,0:T(8,128)(2,1)S(1)} %copy-done), channel_id=1, source_target_pairs={{0,64},{64,128},{128,192},{192,0},{1,65},{65,129},{129,193},{193,1... | collective-permute-start | bytes 1216520 | tf_op jit(solution)/shard_map/ppermute | solution.py:167
  14.0 23.0 %collective-permute-start.1 = (bf16[528,384]{1,0:T(8,128)(2,1)S(1)}, bf16[528,384]{1,0:T(8,128)(2,1)S(1)}, u32[]{:S(2)}, u32[]{:S(2)}) collective-permute-start(bf16[528,384]{1,0:T(8,128)(2,1)S(1)} %copy-done), channel_id=1, source_target_pairs={{0,128},{64,192},{128,0},{192,64},{1,129},{65,193},{129,1},{193,65... | collective-permute-start | bytes 1216520 | tf_op jit(solution)/shard_map/ppermute | solution.py:167
  16.6 20.3 %collective-permute-start.2 = (bf16[528,384]{1,0:T(8,128)(2,1)S(1)}, bf16[528,384]{1,0:T(8,128)(2,1)S(1)}, u32[]{:S(2)}, u32[]{:S(2)}) collective-permute-start(bf16[528,384]{1,0:T(8,128)(2,1)S(1)} %copy-done), channel_id=1, source_target_pairs={{0,192},{64,0},{128,64},{192,128},{1,193},{65,1},{129,65},{193,129... | collective-permute-start | bytes 1216520 | tf_op jit(solution)/shard_map/ppermute | solution.py:167
  36.3 4.1 %collective-permute-start.3 = (bf16[4,128,384]{2,1,0:T(8,128)(2,1)S(1)}, bf16[4,128,384]{2,1,0:T(8,128)(2,1)S(1)}, u32[]{:S(2)}, u32[]{:S(2)}) collective-permute-start(bf16[4,128,384]{2,1,0:T(8,128)(2,1)S(1)} %get-tuple-element.37.low_ref), channel_id=1, source_target_pairs={{0,4},{4,0},{1,5},{5,1},{2,6},{6,2},{3,7},{7,3},{8,12},{12,8},{9,1... | collective-permute-start | bytes 1179656 | tf_op jit(solution)/shard_map/ppermute | solution.py:170
  36.8 3.5 %collective-permute-start.4 = (bf16[4,128,384]{2,1,0:T(8,128)(2,1)S(1)}, bf16[4,128,384]{2,1,0:T(8,128)(2,1)S(1)}, u32[]{:S(2)}, u32[]{:S(2)}) collective-permute-start(bf16[4,128,384]{2,1,0:T(8,128)(2,1)S(1)} %get-tuple-element.36.high_ref), channel_id=1, source_target_pairs={{0,4},{4,0},{1,5},{5,1},{2,6},{6,2},{3,7},{7,3},{8,12},{12,8},{9,1... | collective-permute-start | bytes 1179656 | tf_op jit(solution)/shard_map/ppermute | solution.py:170
  44.0 2.1 %collective-permute-start.8 = (f32[9,128,128]{2,1,0:T(8,128)S(1)}, f32[9,128,128]{2,1,0:T(8,128)S(1)}, u32[]{:S(2)}, u32[]{:S(2)}) collective-permute-start(f32[9,128,128]{2,1,0:T(8,128)S(1)} %get-tuple-element.27.sent_ref), channel_id=1, source_target_pairs={{0,4},{4,0},{1,5},{5,1},{2,6},{6,2},{3,7},{7,3},{8,12},{12,8},{9,1... | collective-permute-start | bytes 1769480 | tf_op jit(solution)/shard_map/ppermute | solution.py:198
  46.9 20.0 %all-to-all-start.1 = ((bf16[8,192,128]{2,1,0:T(8,128)(2,1)}), bf16[8,192,128]{2,1,0:T(8,128)(2,1)S(1)}, u32[]{:S(2)}, u32[]{:S(2)}) async-start(bf16[8,192,128]{2,1,0:T(8,128)(2,1)} %join.1), calls=%async_computation.1 | async-start | bytes 786432 | tf_op jit(solution)/shard_map/all_to_all | solution.py:208
  51.7 15.2 %collective-permute-start.5 = (bf16[4,128,128]{2,1,0:T(8,128)(2,1)S(1)}, bf16[4,128,128]{2,1,0:T(8,128)(2,1)S(1)}, u32[]{:S(2)}, u32[]{:S(2)}) collective-permute-start(bf16[4,128,128]{2,1,0:T(8,128)(2,1)S(1)} %get-tuple-element.23), channel_id=1, source_target_pairs={{0,1},{1,2},{2,3},{3,0},{4,5},{5,6},{6,7},{7,4},{8,9},{9,10},{10,1... | collective-permute-start | bytes 393224 | tf_op jit(solution)/shard_map/ppermute | solution.py:199
  53.0 14.0 %collective-permute-start.6 = (bf16[4,128,128]{2,1,0:T(8,128)(2,1)S(1)}, bf16[4,128,128]{2,1,0:T(8,128)(2,1)S(1)}, u32[]{:S(2)}, u32[]{:S(2)}) collective-permute-start(bf16[4,128,128]{2,1,0:T(8,128)(2,1)S(1)} %get-tuple-element.24), channel_id=1, source_target_pairs={{0,2},{1,3},{2,0},{3,1},{4,6},{5,7},{6,4},{7,5},{8,10},{9,11},{10,... | collective-permute-start | bytes 393224 | tf_op jit(solution)/shard_map/ppermute | solution.py:199
  55.4 11.6 %collective-permute-start.7 = (bf16[4,128,128]{2,1,0:T(8,128)(2,1)S(1)}, bf16[4,128,128]{2,1,0:T(8,128)(2,1)S(1)}, u32[]{:S(2)}, u32[]{:S(2)}) collective-permute-start(bf16[4,128,128]{2,1,0:T(8,128)(2,1)S(1)} %get-tuple-element.25), channel_id=1, source_target_pairs={{0,3},{1,0},{2,1},{3,2},{4,7},{5,4},{6,5},{7,6},{8,11},{9,8},{10,9... | collective-permute-start | bytes 393224 | tf_op jit(solution)/shard_map/ppermute | solution.py:199
  67.8 16.7 %all-to-all-start.2 = ((f32[16,64,128]{2,1,0:T(8,128)}), f32[16,64,128]{2,1,0:T(8,128)S(1)}, u32[]{:S(2)}, u32[]{:S(2)}) async-start(f32[16,64,128]{2,1,0:T(8,128)} %get-tuple-element.32), calls=%async_computation.2 | async-start | bytes 1048576 | tf_op jit(solution)/shard_map/all_to_all | solution.py:224
  74.0 12.7 %collective-permute-start.10 = (f32[128,128]{1,0:T(8,128)S(1)}, f32[128,128]{1,0:T(8,128)S(1)}, u32[]{:S(2)}, u32[]{:S(2)}) collective-permute-start(f32[128,128]{1,0:T(8,128)S(1)} %get-tuple-element.30), channel_id=1, source_target_pairs={{0,128},{64,192},{128,0},{192,64},{1,129},{65,193},{129,1},{193,65... | collective-permute-start | bytes 196616 | tf_op jit(solution)/shard_map/ppermute | solution.py:221
  76.9 9.8 %collective-permute-start.11 = (f32[128,128]{1,0:T(8,128)S(1)}, f32[128,128]{1,0:T(8,128)S(1)}, u32[]{:S(2)}, u32[]{:S(2)}) collective-permute-start(f32[128,128]{1,0:T(8,128)S(1)} %get-tuple-element.31), channel_id=1, source_target_pairs={{0,64},{64,128},{128,192},{192,0},{1,65},{65,129},{129,193},{193,1... | collective-permute-start | bytes 196616 | tf_op jit(solution)/shard_map/ppermute | solution.py:221
  77.1 9.5 %collective-permute-start.9 = (f32[128,128]{1,0:T(8,128)S(1)}, f32[128,128]{1,0:T(8,128)S(1)}, u32[]{:S(2)}, u32[]{:S(2)}) collective-permute-start(f32[128,128]{1,0:T(8,128)S(1)} %get-tuple-element.29), channel_id=1, source_target_pairs={{0,192},{64,0},{128,64},{192,128},{1,193},{65,1},{129,65},{193,129... | collective-permute-start | bytes 196616 | tf_op jit(solution)/shard_map/ppermute | solution.py:221
  84.6 2.9 %collective-permute-start.12 = (f32[64,128]{1,0:T(8,128)S(1)}, f32[64,128]{1,0:T(8,128)S(1)}, u32[]{:S(2)}, u32[]{:S(2)}) collective-permute-start(f32[64,128]{1,0:T(8,128)S(1)} %broadcast_multiply_fusion), channel_id=1, source_target_pairs={{0,4},{4,0},{1,5},{5,1},{2,6},{6,2},{3,7},{7,3},{8,12},{12,8},{9,1... | collective-permute-start | bytes 98312 | tf_op jit(solution)/shard_map/ppermute | solution.py:226

commit v6 on v5

--- a/solution.py
+++ b/solution.py
@@ -16,6 +16,7 @@
 MASK_ROWS = 16
 LOAD_ROWS = BLOCK + MASK_ROWS
 HALF = Z * SUB
+CUT = 272
 NODES = BLOCKS * BLOCK
 TERMS = 1
 SENT = SUB + TERMS * PROBES // C
@@ -80,19 +81,23 @@
     at = lax.axis_index("y") * (Z * C) + owner
     subs = [cols_ref.at[s] for cols_ref in cols_refs for s in range(cols_ref.shape[0])]
     right_probes = jnp.concatenate([sub[:, RANK:WIDTH] for sub in subs], 0)
-    for back, rows_ref in enumerate(rows_refs):
-        flags = 4.0 * rows_ref[BLOCK:LOAD_ROWS, 0:128].astype(F32)[0:8]
+    rows0, rows1, far_low, far_high, rows3 = rows_refs
+    for back, parts in enumerate(((rows0,), (rows1,), (far_low, far_high), (rows3,))):
+        loads = [part[...] for part in parts]
+        whole = loads[0] if len(loads) == 1 else jnp.concatenate(loads, 0)
+        left, left_probes = whole[0:BLOCK, 0:RANK], whole[0:BLOCK, RANK:WIDTH]
+        flags = 4.0 * whole[BLOCK:LOAD_ROWS, 0:128].astype(F32)[0:8]
         turned = pltpu.roll(flags, lax.rem(128 - at, 128), 1)
         right = jnp.concatenate(
             [sub[:, 0:RANK] * turned[0:1, C * s : C * s + 1].astype(BF16) for s, sub in enumerate(subs)], 0
         )
         scores = lax.dot_general(
-            rows_ref[0:BLOCK, 0:RANK], right, (((1,), (1,)), ((), ())), preferred_element_type=F32
+            left, right, (((1,), (1,)), ((), ())), preferred_element_type=F32
         )
         proximity = jnp.log(jnp.maximum(scores, 1.0)).astype(BF16)
         row_part = jnp.dot(proximity, right_probes, preferred_element_type=F32)
         row_acc[back] = row_part if first is None else first[back] + row_part
-        col_part = contract_rows(rows_ref[0:BLOCK, RANK:WIDTH], proximity)
+        col_part = contract_rows(left_probes, proximity)
         if back == 0:
             col_acc[...] = col_part
         else:
@@ -101,16 +106,16 @@
     return gram[0:PROBES] + gram[PROBES:]
 
 
-def own_kernel(rows0, rows1, rows2, rows3, low_ref, high_ref, row_ref, keep_ref, gram_ref, col_acc):
-    gram_ref[...] = tiles(0, (rows0, rows1, rows2, rows3), (low_ref, high_ref), row_ref, None, col_acc)
+def own_kernel(rows0, rows1, far_low, far_high, rows3, low_ref, high_ref, row_ref, keep_ref, gram_ref, col_acc):
+    gram_ref[...] = tiles(0, (rows0, rows1, far_low, far_high, rows3), (low_ref, high_ref), row_ref, None, col_acc)
     for s in range(Z):
         keep_ref[s] = col_acc[:, s * SUB : (s + 1) * SUB]
 
 
 def other_kernel(
-    rows0, rows1, rows2, rows3, low_ref, high_ref, first_ref, gram_ref, piece0, piece1, piece2, piece3, send_ref, row_acc, col_acc
+    rows0, rows1, far_low, far_high, rows3, low_ref, high_ref, first_ref, gram_ref, piece0, piece1, piece2, piece3, send_ref, row_acc, col_acc
 ):
-    gram = tiles(1, (rows0, rows1, rows2, rows3), (low_ref, high_ref), row_acc, first_ref, col_acc)
+    gram = tiles(1, (rows0, rows1, far_low, far_high, rows3), (low_ref, high_ref), row_acc, first_ref, col_acc)
     x = lax.axis_index("x")
     for ahead, piece in enumerate((piece0, piece1, piece2, piece3)):
         at = pl.ds(pl.multiple_of(SUB * lax.rem(x + ahead, X), SUB), SUB)
@@ -164,7 +169,9 @@
         compiler_params=pltpu.CompilerParams(vmem_limit_bytes=WHOLE),
         name="pack",
     )(pair_count, factor_rows, row_side_probes, factor_cols, probe_cols, pair_blocks)
-    all_rows = [row_load] + [lax.ppermute(row_load, "y", ring(Y, s)) for s in range(1, Y)]
+    near = [lax.ppermute(row_load, "y", ring(Y, s)) for s in (1, 3)]
+    far = [lax.ppermute(near[0][:CUT], "y", ring(Y, 1)), lax.ppermute(near[1][CUT:], "y", ring(Y, 3))]
+    all_rows = [row_load, near[0], *far, near[1]]
     own_cols = lax.all_to_all(col_load, "z", split_axis=0, concat_axis=0, tiled=True)
     own_cols = [own_cols[: Z // 2], own_cols[Z // 2 :]]
     other_cols = [lax.ppermute(part, "c", SWAP) for part in own_cols]
@@ -175,7 +182,7 @@
     first, keep, gram = pl.pallas_call(
         own_kernel,
         out_shape=[shape((Y, BLOCK, PROBES), F32), shape((Z, PROBES, SUB), F32), shape((PROBES, PROBES), F32)],
-        in_specs=[vmem] * 6,
+        in_specs=[vmem] * 7,
         out_specs=[vmem] * 3,
         scratch_shapes=[pltpu.VMEM((PROBES, HALF), F32)],
         compiler_params=params,
@@ -187,7 +194,7 @@
         out_shape=[shape((Y, SUB, PROBES), F32)]
         + [shape((Y, SUB, PROBES), BF16)] * (X - 1)
         + [shape((Z + 1, PROBES, SUB), F32)],
-        in_specs=[vmem] * 8,
+        in_specs=[vmem] * 9,
         out_specs=[vmem] * 5,
         scratch_shapes=[pltpu.VMEM((Y, BLOCK, PROBES), F32), pltpu.VMEM((PROBES, HALF), F32)],
         compiler_params=params,

time: 88.5 us -> 88.1 us (level)
  starting transfers between devices: 38.7 us -> 36.9 us
  waiting for transfers between devices: 35 us -> 36.3 us
    all_to_all x2, waiting for transfers between devices: 28.8 us -> 19.3 us  [shards(): lax.all_to_all(col_load, 'z', split_axis=0, concat_axis=0, tiled=True)]
    ppermute x3 -> x4, waiting for transfers between devices: 0.01 us -> 8.45 us  [the longest x2 8.45 us: shards(): near = [lax.ppermute(row_load, 'y', ring(Y, s)) for s in (1, 3)]]
    all_to_all x1, waiting for transfers between devices: 4.29 us -> 6.32 us  [shards(): lax.all_to_all(gram, ('y', 'x'), split_axis=0, concat_axis=0, tiled=True)]
    ppermute x3, starting transfers between devices: 5.55 us -> 3.73 us  [shards(): lax.ppermute(sums[back], 'y', ring(Y, Y - back))]
    all_to_all x2, starting transfers between devices: 14 us -> 12.6 us  [shards(): lax.all_to_all(col_load, 'z', split_axis=0, concat_axis=0, tiled=True)]
    ppermute x3 -> x4, starting transfers between devices: 5.06 us -> 5.71 us  [the longest x2 2.9 us: shards(): near = [lax.ppermute(row_load, 'y', ring(Y, s)) for s in (1, 3)]]
  transfers between devices with their start and end apart: 16 -> 17, of which waited for: 5 -> 6; matrix products, arithmetic and copies ran while one was open for 2% -> 2% of each run, Pallas kernels for 4% -> 4%
where the time goes in v6:
time: 88.1 us; the launch traced here: 87.7 us
  starting transfers between devices  36.9 us (42%)
  waiting for transfers between devices  36.3 us (41%)
  Pallas kernels  10.8 us (12%)
  between operations  1.43 us (2%)
  other arithmetic  1.39 us (2%)
    all_to_all x2, waiting for transfers between devices, shards(): lax.all_to_all(col_load, 'z', split_axis=0, concat_axis=0, tiled=True)  19.3 us
    all_to_all x2, starting transfers between devices, shards(): lax.all_to_all(col_load, 'z', split_axis=0, concat_axis=0, tiled=True)  12.6 us
    ppermute x2, waiting for transfers between devices, shards(): near = [lax.ppermute(row_load, 'y', ring(Y, s)) for s in (1, 3)]  8.45 us
    all_to_all x1, starting transfers between devices, shards(): lax.all_to_all(gram, ('y', 'x'), split_axis=0, concat_axis=0, tiled=True)  6.76 us
    all_to_all x1, waiting for transfers between devices, shards(): lax.all_to_all(gram, ('y', 'x'), split_axis=0, concat_axis=0, tiled=True)  6.32 us
    ppermute x3, starting transfers between devices, shards(): got_pieces = [lax.ppermute(pieces[s], 'x', ring(X, s)) for s in range(1, X)]  5.08 us
    ppermute x3, starting transfers between devices, shards(): lax.ppermute(sums[back], 'y', ring(Y, Y - back))  3.73 us
    pallas_call x1, Pallas kernels, shards(): pl.pallas_call(other_kernel, out_shape=[shape((Y, SUB, PROBES), F32)] + [...  3.59 us
  transfers between devices with their start and end apart: 17, of which 6 were waited for; matrix products, arithmetic and copies ran while one was open for 2% of the time, Pallas kernels for 4%

profile of v6, /device:TPU:1, one launch (start us, length us, event | category | flops | bytes accessed | tf_op | source)
XLA Modules:
  0.0 87.7 jit_solution(17196935689836921875)
XLA Ops:
  1.3 2.1 %pack.1 = (bf16[528,384]{1,0:T(8,128)(2,1)}, bf16[8,128,384]{2,1,0:T(8,128)(2,1)}) custom-call(s32[1]{0:T(128)S(6)} %copy.10.count_hbm, bf16[512,256]{1,0:T(8,128)(2,1)} %factor_hbm.1, bf16[512,128]{1,0:T(8,128)(2,1)} %side_hbm.1, bf16[128,256]{1,0:T(8,128)(2,1)} %cols_hbm.1, bf16[128,128]{1,0:T(8,128)(2,1)} %probe_hbm.1, s32[1,64]{1,0:T(1,128)} %pairs_hbm.1), custom_call_target="tpu_custom_call" | custom-call | tf_op jit(solution)/shard_map/pack/pallas_call | solution.py:159
  3.4 9.2 %all-to-all-start = ((bf16[8,128,384]{2,1,0:T(8,128)(2,1)}), bf16[8,128,384]{2,1,0:T(8,128)(2,1)S(1)}, u32[]{:S(2)}, u32[]{:S(2)}) async-start(bf16[8,128,384]{2,1,0:T(8,128)(2,1)} %get-tuple-element.19), calls=%async_computation | async-start | bytes 1572864 | tf_op jit(solution)/shard_map/all_to_all | solution.py:175
  12.6 1.4 %collective-permute-start = (bf16[528,384]{1,0:T(8,128)(2,1)S(1)}, bf16[528,384]{1,0:T(8,128)(2,1)S(1)}, u32[]{:S(2)}, u32[]{:S(2)}) collective-permute-start(bf16[528,384]{1,0:T(8,128)(2,1)S(1)} %copy-done), channel_id=1, source_target_pairs={{0,64},{64,128},{128,192},{192,0},{1,65},{65,129},{129,193},{193,1... | collective-permute-start | bytes 1216520 | tf_op jit(solution)/shard_map/ppermute | solution.py:172
  14.0 1.5 %collective-permute-start.2 = (bf16[528,384]{1,0:T(8,128)(2,1)S(1)}, bf16[528,384]{1,0:T(8,128)(2,1)S(1)}, u32[]{:S(2)}, u32[]{:S(2)}) collective-permute-start(bf16[528,384]{1,0:T(8,128)(2,1)S(1)} %copy-done), channel_id=1, source_target_pairs={{0,192},{64,0},{128,64},{192,128},{1,193},{65,1},{129,65},{193,129... | collective-permute-start | bytes 1216520 | tf_op jit(solution)/shard_map/ppermute | solution.py:172
  15.5 8.4 %collective-permute-done.rows1 = bf16[528,384]{1,0:T(8,128)(2,1)S(1)} collective-permute-done((bf16[528,384]{1,0:T(8,128)(2,1)S(1)}, bf16[528,384]{1,0:T(8,128)(2,1)S(1)}, u32[]{:S(2)}, u32[]{:S(2)}) %collective-permute-start) | collective-permute-done | bytes 405536 | tf_op jit(solution)/shard_map/ppermute | solution.py:172
  24.1 2.7 %collective-permute-start.3 = (bf16[256,384]{1,0:T(8,128)(2,1)S(1)}, bf16[256,384]{1,0:T(8,128)(2,1)S(1)}, u32[]{:S(2)}, u32[]{:S(2)}) collective-permute-start(bf16[256,384]{1,0:T(8,128)(2,1)S(1)} %slice.21), channel_id=1, source_target_pairs={{0,192},{64,0},{128,64},{192,128},{1,193},{65,1},{129,65},{193,129... | collective-permute-start | bytes 589832 | tf_op jit(solution)/shard_map/ppermute | solution.py:173
  26.8 9.3 %all-to-all-done = bf16[8,128,384]{2,1,0:T(8,128)(2,1)S(1)} async-done(((bf16[8,128,384]{2,1,0:T(8,128)(2,1)}), bf16[8,128,384]{2,1,0:T(8,128)(2,1)S(1)}, u32[]{:S(2)}, u32[]{:S(2)}) %all-to-all-start) | async-done | bytes 786464 | tf_op jit(solution)/shard_map/all_to_all | solution.py:175
  36.9 3.4 %own_tiles.1 = (f32[4,512,128]{2,1,0:T(8,128)S(1)}, f32[8,128,128]{2,1,0:T(8,128)S(1)}, f32[128,128]{1,0:T(8,128)S(1)}) custom-call(bf16[528,384]{1,0:T(8,128)(2,1)S(1)} %copy-done, bf16[528,384]{1,0:T(8,128)(2,1)S(1)} %collective-permute-done.rows1, bf16[272,384]{1,0:T(8,128)(2,1)S(1)} %collective-permute-done.1.far_low, ...), custom_call_target="tpu_custom_call" | custom-call | flops 2147483648 | bytes 4194304 | tf_op jit(solution)/shard_map/own_tiles/pallas_call | solution.py:182
  40.4 3.6 %other_tiles.1 = (f32[4,128,128]{2,1,0:T(8,128)S(1)}, bf16[4,128,128]{2,1,0:T(8,128)(2,1)S(1)}, bf16[4,128,128]{2,1,0:T(8,128)(2,1)S(1)}, bf16[4,128,128]{2,1,0:T(8,128)(2,1)S(1)}, f32[9,128,128]{2,1,0:T(8,128)S(1)}) custom-call(bf16[528,384]{1,0:T(8,128)(2,1)S(1)} %copy-done, bf16[528,384]{1,0:T(8,128)(2,1)S(1)} %collective-permute-done.rows1, ...), custom_call_target="tpu_custom_call" | custom-call | flops 2147483648 | bytes 4194304 | tf_op jit(solution)/shard_map/other_tiles/pallas_call | solution.py:192
  44.5 1.6 %collective-permute-done.9.got_ref = f32[9,128,128]{2,1,0:T(8,128)S(1)} collective-permute-done((f32[9,128,128]{2,1,0:T(8,128)S(1)}, f32[9,128,128]{2,1,0:T(8,128)S(1)}, u32[]{:S(2)}, u32[]{:S(2)}) %collective-permute-start.9) | collective-permute-done | bytes 589856 | tf_op jit(solution)/shard_map/ppermute | solution.py:205
  46.1 0.8 join.1
  46.9 3.5 %all-to-all-start.1 = ((bf16[8,192,128]{2,1,0:T(8,128)(2,1)}), bf16[8,192,128]{2,1,0:T(8,128)(2,1)S(1)}, u32[]{:S(2)}, u32[]{:S(2)}) async-start(bf16[8,192,128]{2,1,0:T(8,128)(2,1)} %join.1), calls=%async_computation.1 | async-start | bytes 786432 | tf_op jit(solution)/shard_map/all_to_all | solution.py:215
  50.4 1.5 %collective-permute-start.6 = (bf16[4,128,128]{2,1,0:T(8,128)(2,1)S(1)}, bf16[4,128,128]{2,1,0:T(8,128)(2,1)S(1)}, u32[]{:S(2)}, u32[]{:S(2)}) collective-permute-start(bf16[4,128,128]{2,1,0:T(8,128)(2,1)S(1)} %get-tuple-element.23), channel_id=1, source_target_pairs={{0,1},{1,2},{2,3},{3,0},{4,5},{5,6},{6,7},{7,4},{8,9},{9,10},{10,1... | collective-permute-start | bytes 393224 | tf_op jit(solution)/shard_map/ppermute | solution.py:206
  51.8 2.5 %collective-permute-start.7 = (bf16[4,128,128]{2,1,0:T(8,128)(2,1)S(1)}, bf16[4,128,128]{2,1,0:T(8,128)(2,1)S(1)}, u32[]{:S(2)}, u32[]{:S(2)}) collective-permute-start(bf16[4,128,128]{2,1,0:T(8,128)(2,1)S(1)} %get-tuple-element.24), channel_id=1, source_target_pairs={{0,2},{1,3},{2,0},{3,1},{4,6},{5,7},{6,4},{7,5},{8,10},{9,11},{10,... | collective-permute-start | bytes 393224 | tf_op jit(solution)/shard_map/ppermute | solution.py:206
  54.3 1.1 %collective-permute-start.8 = (bf16[4,128,128]{2,1,0:T(8,128)(2,1)S(1)}, bf16[4,128,128]{2,1,0:T(8,128)(2,1)S(1)}, u32[]{:S(2)}, u32[]{:S(2)}) collective-permute-start(bf16[4,128,128]{2,1,0:T(8,128)(2,1)S(1)} %get-tuple-element.25), channel_id=1, source_target_pairs={{0,3},{1,0},{2,1},{3,2},{4,7},{5,4},{6,5},{7,6},{8,11},{9,8},{10,9... | collective-permute-start | bytes 393224 | tf_op jit(solution)/shard_map/ppermute | solution.py:206
  55.4 10.0 %all-to-all-done.1 = bf16[8,192,128]{2,1,0:T(8,128)(2,1)S(1)} async-done(((bf16[8,192,128]{2,1,0:T(8,128)(2,1)}), bf16[8,192,128]{2,1,0:T(8,128)(2,1)S(1)}, u32[]{:S(2)}, u32[]{:S(2)}) %all-to-all-start.1) | async-done | bytes 393248 | tf_op jit(solution)/shard_map/all_to_all | solution.py:215
  65.5 0.9 %pieces.1 = (f32[128,128]{1,0:T(8,128)S(1)}, f32[128,128]{1,0:T(8,128)S(1)}, f32[128,128]{1,0:T(8,128)S(1)}, f32[128,128]{1,0:T(8,128)S(1)}, f32[16,64,128]{2,1,0:T(8,128)}) custom-call(f32[4,128,128]{2,1,0:T(8,128)S(1)} %get-tuple-element.22.kept_ref, bf16[4,128,128]{2,1,0:T(8,128)(2,1)S(1)} %collective-permute-done.6.got1, ...), custom_call_target="tpu_custom_call" | custom-call | tf_op jit(solution)/shard_map/pieces/pallas_call | solution.py:220
  66.4 6.8 %all-to-all-start.2 = ((f32[16,64,128]{2,1,0:T(8,128)}), f32[16,64,128]{2,1,0:T(8,128)S(1)}, u32[]{:S(2)}, u32[]{:S(2)}) async-start(f32[16,64,128]{2,1,0:T(8,128)} %get-tuple-element.32), calls=%async_computation.2 | async-start | bytes 1048576 | tf_op jit(solution)/shard_map/all_to_all | solution.py:231
  73.2 2.6 %collective-permute-start.10 = (f32[128,128]{1,0:T(8,128)S(1)}, f32[128,128]{1,0:T(8,128)S(1)}, u32[]{:S(2)}, u32[]{:S(2)}) collective-permute-start(f32[128,128]{1,0:T(8,128)S(1)} %get-tuple-element.29), channel_id=1, source_target_pairs={{0,192},{64,0},{128,64},{192,128},{1,193},{65,1},{129,65},{193,129... | collective-permute-start | bytes 196616 | tf_op jit(solution)/shard_map/ppermute | solution.py:228
  76.9 0.7 copy.9
  77.6 6.3 %all-to-all-done.2 = f32[16,64,128]{2,1,0:T(8,128)S(1)} async-done(((f32[16,64,128]{2,1,0:T(8,128)}), f32[16,64,128]{2,1,0:T(8,128)S(1)}, u32[]{:S(2)}, u32[]{:S(2)}) %all-to-all-start.2) | async-done | bytes 524320 | tf_op jit(solution)/shard_map/all_to_all | solution.py:231
  84.0 1.8 %collective-permute-start.13 = (f32[64,128]{1,0:T(8,128)S(1)}, f32[64,128]{1,0:T(8,128)S(1)}, u32[]{:S(2)}, u32[]{:S(2)}) collective-permute-start(f32[64,128]{1,0:T(8,128)S(1)} %broadcast_multiply_fusion), channel_id=1, source_target_pairs={{0,4},{4,0},{1,5},{5,1},{2,6},{6,2},{3,7},{7,3},{8,12},{12,8},{9,1... | collective-permute-start | bytes 98312 | tf_op jit(solution)/shard_map/ppermute | solution.py:233
  86.4 0.6 add_multiply_fusion
  87.0 0.6 pad_maximum_fusion
  (28 shorter events, 3.2 us)
Async XLA Ops:
  3.4 9.2 %copy-start = (bf16[528,384]{1,0:T(8,128)(2,1)S(1)}, bf16[528,384]{1,0:T(8,128)(2,1)}, u32[]{:S(2)}) copy-start(bf16[528,384]{1,0:T(8,128)(2,1)} %get-tuple-element.18.rows0) | copy-start | bytes 1216516
  3.4 32.7 %all-to-all-start = ((bf16[8,128,384]{2,1,0:T(8,128)(2,1)}), bf16[8,128,384]{2,1,0:T(8,128)(2,1)S(1)}, u32[]{:S(2)}, u32[]{:S(2)}) async-start(bf16[8,128,384]{2,1,0:T(8,128)(2,1)} %get-tuple-element.19), calls=%async_computation | async-start | bytes 1572864 | tf_op jit(solution)/shard_map/all_to_all | solution.py:175
  12.6 11.3 %collective-permute-start = (bf16[528,384]{1,0:T(8,128)(2,1)S(1)}, bf16[528,384]{1,0:T(8,128)(2,1)S(1)}, u32[]{:S(2)}, u32[]{:S(2)}) collective-permute-start(bf16[528,384]{1,0:T(8,128)(2,1)S(1)} %copy-done), channel_id=1, source_target_pairs={{0,64},{64,128},{128,192},{192,0},{1,65},{65,129},{129,193},{193,1... | collective-permute-start | bytes 1216520 | tf_op jit(solution)/shard_map/ppermute | solution.py:172
  14.0 10.1 %collective-permute-start.2 = (bf16[528,384]{1,0:T(8,128)(2,1)S(1)}, bf16[528,384]{1,0:T(8,128)(2,1)S(1)}, u32[]{:S(2)}, u32[]{:S(2)}) collective-permute-start(bf16[528,384]{1,0:T(8,128)(2,1)S(1)} %copy-done), channel_id=1, source_target_pairs={{0,192},{64,0},{128,64},{192,128},{1,193},{65,1},{129,65},{193,129... | collective-permute-start | bytes 1216520 | tf_op jit(solution)/shard_map/ppermute | solution.py:172
  24.0 13.0 %collective-permute-start.1 = (bf16[272,384]{1,0:T(8,128)(2,1)S(1)}, bf16[272,384]{1,0:T(8,128)(2,1)S(1)}, u32[]{:S(2)}, u32[]{:S(2)}) collective-permute-start(bf16[272,384]{1,0:T(8,128)(2,1)S(1)} %slice.20), channel_id=1, source_target_pairs={{0,64},{64,128},{128,192},{192,0},{1,65},{65,129},{129,193},{193,1... | collective-permute-start | bytes 626696 | tf_op jit(solution)/shard_map/ppermute | solution.py:173
  24.1 12.8 %collective-permute-start.3 = (bf16[256,384]{1,0:T(8,128)(2,1)S(1)}, bf16[256,384]{1,0:T(8,128)(2,1)S(1)}, u32[]{:S(2)}, u32[]{:S(2)}) collective-permute-start(bf16[256,384]{1,0:T(8,128)(2,1)S(1)} %slice.21), channel_id=1, source_target_pairs={{0,192},{64,0},{128,64},{192,128},{1,193},{65,1},{129,65},{193,129... | collective-permute-start | bytes 589832 | tf_op jit(solution)/shard_map/ppermute | solution.py:173
  36.3 4.1 %collective-permute-start.4 = (bf16[4,128,384]{2,1,0:T(8,128)(2,1)S(1)}, bf16[4,128,384]{2,1,0:T(8,128)(2,1)S(1)}, u32[]{:S(2)}, u32[]{:S(2)}) collective-permute-start(bf16[4,128,384]{2,1,0:T(8,128)(2,1)S(1)} %get-tuple-element.37.low_ref), channel_id=1, source_target_pairs={{0,4},{4,0},{1,5},{5,1},{2,6},{6,2},{3,7},{7,3},{8,12},{12,8},{9,1... | collective-permute-start | bytes 1179656 | tf_op jit(solution)/shard_map/ppermute | solution.py:177
  36.8 3.5 %collective-permute-start.5 = (bf16[4,128,384]{2,1,0:T(8,128)(2,1)S(1)}, bf16[4,128,384]{2,1,0:T(8,128)(2,1)S(1)}, u32[]{:S(2)}, u32[]{:S(2)}) collective-permute-start(bf16[4,128,384]{2,1,0:T(8,128)(2,1)S(1)} %get-tuple-element.36.high_ref), channel_id=1, source_target_pairs={{0,4},{4,0},{1,5},{5,1},{2,6},{6,2},{3,7},{7,3},{8,12},{12,8},{9,1... | collective-permute-start | bytes 1179656 | tf_op jit(solution)/shard_map/ppermute | solution.py:177
  44.0 2.1 %collective-permute-start.9 = (f32[9,128,128]{2,1,0:T(8,128)S(1)}, f32[9,128,128]{2,1,0:T(8,128)S(1)}, u32[]{:S(2)}, u32[]{:S(2)}) collective-permute-start(f32[9,128,128]{2,1,0:T(8,128)S(1)} %get-tuple-element.27.sent_ref), channel_id=1, source_target_pairs={{0,4},{4,0},{1,5},{5,1},{2,6},{6,2},{3,7},{7,3},{8,12},{12,8},{9,1... | collective-permute-start | bytes 1769480 | tf_op jit(solution)/shard_map/ppermute | solution.py:205
  46.9 18.5 %all-to-all-start.1 = ((bf16[8,192,128]{2,1,0:T(8,128)(2,1)}), bf16[8,192,128]{2,1,0:T(8,128)(2,1)S(1)}, u32[]{:S(2)}, u32[]{:S(2)}) async-start(bf16[8,192,128]{2,1,0:T(8,128)(2,1)} %join.1), calls=%async_computation.1 | async-start | bytes 786432 | tf_op jit(solution)/shard_map/all_to_all | solution.py:215
  50.4 15.1 %collective-permute-start.6 = (bf16[4,128,128]{2,1,0:T(8,128)(2,1)S(1)}, bf16[4,128,128]{2,1,0:T(8,128)(2,1)S(1)}, u32[]{:S(2)}, u32[]{:S(2)}) collective-permute-start(bf16[4,128,128]{2,1,0:T(8,128)(2,1)S(1)} %get-tuple-element.23), channel_id=1, source_target_pairs={{0,1},{1,2},{2,3},{3,0},{4,5},{5,6},{6,7},{7,4},{8,9},{9,10},{10,1... | collective-permute-start | bytes 393224 | tf_op jit(solution)/shard_map/ppermute | solution.py:206
  51.8 13.7 %collective-permute-start.7 = (bf16[4,128,128]{2,1,0:T(8,128)(2,1)S(1)}, bf16[4,128,128]{2,1,0:T(8,128)(2,1)S(1)}, u32[]{:S(2)}, u32[]{:S(2)}) collective-permute-start(bf16[4,128,128]{2,1,0:T(8,128)(2,1)S(1)} %get-tuple-element.24), channel_id=1, source_target_pairs={{0,2},{1,3},{2,0},{3,1},{4,6},{5,7},{6,4},{7,5},{8,10},{9,11},{10,... | collective-permute-start | bytes 393224 | tf_op jit(solution)/shard_map/ppermute | solution.py:206
  54.3 11.2 %collective-permute-start.8 = (bf16[4,128,128]{2,1,0:T(8,128)(2,1)S(1)}, bf16[4,128,128]{2,1,0:T(8,128)(2,1)S(1)}, u32[]{:S(2)}, u32[]{:S(2)}) collective-permute-start(bf16[4,128,128]{2,1,0:T(8,128)(2,1)S(1)} %get-tuple-element.25), channel_id=1, source_target_pairs={{0,3},{1,0},{2,1},{3,2},{4,7},{5,4},{6,5},{7,6},{8,11},{9,8},{10,9... | collective-permute-start | bytes 393224 | tf_op jit(solution)/shard_map/ppermute | solution.py:206
  66.4 17.6 %all-to-all-start.2 = ((f32[16,64,128]{2,1,0:T(8,128)}), f32[16,64,128]{2,1,0:T(8,128)S(1)}, u32[]{:S(2)}, u32[]{:S(2)}) async-start(f32[16,64,128]{2,1,0:T(8,128)} %get-tuple-element.32), calls=%async_computation.2 | async-start | bytes 1048576 | tf_op jit(solution)/shard_map/all_to_all | solution.py:231
  73.2 12.7 %collective-permute-start.10 = (f32[128,128]{1,0:T(8,128)S(1)}, f32[128,128]{1,0:T(8,128)S(1)}, u32[]{:S(2)}, u32[]{:S(2)}) collective-permute-start(f32[128,128]{1,0:T(8,128)S(1)} %get-tuple-element.29), channel_id=1, source_target_pairs={{0,192},{64,0},{128,64},{192,128},{1,193},{65,1},{129,65},{193,129... | collective-permute-start | bytes 196616 | tf_op jit(solution)/shard_map/ppermute | solution.py:228
  75.7 10.1 %collective-permute-start.11 = (f32[128,128]{1,0:T(8,128)S(1)}, f32[128,128]{1,0:T(8,128)S(1)}, u32[]{:S(2)}, u32[]{:S(2)}) collective-permute-start(f32[128,128]{1,0:T(8,128)S(1)} %get-tuple-element.30), channel_id=1, source_target_pairs={{0,128},{64,192},{128,0},{192,64},{1,129},{65,193},{129,1},{193,65... | collective-permute-start | bytes 196616 | tf_op jit(solution)/shard_map/ppermute | solution.py:228
  76.3 10.1 %collective-permute-start.12 = (f32[128,128]{1,0:T(8,128)S(1)}, f32[128,128]{1,0:T(8,128)S(1)}, u32[]{:S(2)}, u32[]{:S(2)}) collective-permute-start(f32[128,128]{1,0:T(8,128)S(1)} %get-tuple-element.31), channel_id=1, source_target_pairs={{0,64},{64,128},{128,192},{192,0},{1,65},{65,129},{129,193},{193,1... | collective-permute-start | bytes 196616 | tf_op jit(solution)/shard_map/ppermute | solution.py:228
  84.0 3.0 %collective-permute-start.13 = (f32[64,128]{1,0:T(8,128)S(1)}, f32[64,128]{1,0:T(8,128)S(1)}, u32[]{:S(2)}, u32[]{:S(2)}) collective-permute-start(f32[64,128]{1,0:T(8,128)S(1)} %broadcast_multiply_fusion), channel_id=1, source_target_pairs={{0,4},{4,0},{1,5},{5,1},{2,6},{6,2},{3,7},{7,3},{8,12},{12,8},{9,1... | collective-permute-start | bytes 98312 | tf_op jit(solution)/shard_map/ppermute | solution.py:233

commit v7 on v6

--- a/solution.py
+++ b/solution.py
@@ -41,24 +41,27 @@
 
 
 def pack_kernel(
-    count_hbm, factor_hbm, side_hbm, cols_hbm, probe_hbm, pairs_hbm, rows_out, cols_out, count_ref, pairs_ref, sems
+    count_hbm, factor_hbm, side_hbm, cols_hbm, probe_hbm, pairs_hbm,
+    rows_out, cols_out, count_ref, pairs_ref, cols_ref, rows_ref, sems, out_sems
 ):
-    copies = [
-        pltpu.make_async_copy(source, target, sems.at[k])
-        for k, (source, target) in enumerate(
-            (
-                (count_hbm, count_ref),
-                (pairs_hbm, pairs_ref),
-                (cols_hbm, cols_out.at[0, :, 0:RANK]),
-                (probe_hbm, cols_out.at[0, :, RANK:WIDTH]),
-                (factor_hbm, rows_out.at[0:BLOCK, 0:RANK]),
-                (side_hbm, rows_out.at[0:BLOCK, RANK:WIDTH]),
-            )
-        )
-    ]
+    pairs = (
+        (cols_hbm, cols_ref.at[:, 0:RANK]),
+        (probe_hbm, cols_ref.at[:, RANK:WIDTH]),
+        (count_hbm, count_ref),
+        (pairs_hbm, pairs_ref),
+        (factor_hbm, rows_ref.at[0:BLOCK, 0:RANK]),
+        (side_hbm, rows_ref.at[0:BLOCK, RANK:WIDTH]),
+    )
+    copies = [pltpu.make_async_copy(source, target, sems.at[k]) for k, (source, target) in enumerate(pairs)]
+    outs = [pltpu.make_async_copy(cols_ref, cols_out.at[s], out_sems.at[s]) for s in range(Z)]
+    outs.append(pltpu.make_async_copy(rows_ref, rows_out, out_sems.at[Z]))
     for copy in copies:
         copy.start()
     for copy in copies[:2]:
+        copy.wait()
+    for out in outs[:Z]:
+        out.start()
+    for copy in copies[2:4]:
         copy.wait()
     slots = pairs_ref.shape[1]
     used = lax.broadcasted_iota(jnp.int32, (BLOCKS, slots), 1) < count_ref[0]
@@ -67,13 +70,12 @@
     ones = jnp.ones((MASK_ROWS, slots), BF16)
     flags = lax.dot_general(ones, hits, (((1,), (1,)), ((), ())), preferred_element_type=F32)
     flags = jnp.concatenate([flags, jnp.zeros((MASK_ROWS, WIDTH - BLOCKS), F32)], 1)
-    rows_out[BLOCK:LOAD_ROWS, :] = flags.astype(BF16)
-    for copy in copies[2:4]:
-        copy.wait()
-    for s in range(1, Z):
-        cols_out[s] = cols_out[0]
+    rows_ref[BLOCK:LOAD_ROWS, :] = flags.astype(BF16)
     for copy in copies[4:]:
         copy.wait()
+    outs[Z].start()
+    for out in outs:
+        out.wait()
 
 
 def tiles(shift, rows_refs, cols_refs, row_acc, first, col_acc):
@@ -160,11 +162,14 @@
         pack_kernel,
         out_shape=[shape((LOAD_ROWS, WIDTH), BF16), shape((Z, SUB, WIDTH), BF16)],
         in_specs=[hbm] * 6,
-        out_specs=[vmem, vmem],
+        out_specs=[hbm, hbm],
         scratch_shapes=[
             pltpu.SMEM((1,), jnp.int32),
             pltpu.VMEM(pair_blocks.shape, jnp.int32),
+            pltpu.VMEM((SUB, WIDTH), BF16),
+            pltpu.VMEM((LOAD_ROWS, WIDTH), BF16),
             pltpu.SemaphoreType.DMA((6,)),
+            pltpu.SemaphoreType.DMA((Z + 1,)),
         ],
         compiler_params=pltpu.CompilerParams(vmem_limit_bytes=WHOLE),
         name="pack",

time: 88.1 us -> 87.9 us (level)
  no operation moved by 1% of the time
where the time goes in v7:
time: 87.9 us; the launch traced here: 87.6 us
  starting transfers between devices  36.9 us (42%)
  waiting for transfers between devices  36.3 us (41%)
  Pallas kernels  10.7 us (12%)
  between operations  1.43 us (2%)
  other arithmetic  1.39 us (2%)
    all_to_all x2, waiting for transfers between devices, shards(): lax.all_to_all(col_load, 'z', split_axis=0, concat_axis=0, tiled=True)  19.3 us
    all_to_all x2, starting transfers between devices, shards(): lax.all_to_all(col_load, 'z', split_axis=0, concat_axis=0, tiled=True)  12.6 us
    ppermute x2, waiting for transfers between devices, shards(): near = [lax.ppermute(row_load, 'y', ring(Y, s)) for s in (1, 3)]  8.45 us
    all_to_all x1, starting transfers between devices, shards(): lax.all_to_all(gram, ('y', 'x'), split_axis=0, concat_axis=0, tiled=True)  6.75 us
    all_to_all x1, waiting for transfers between devices, shards(): lax.all_to_all(gram, ('y', 'x'), split_axis=0, concat_axis=0, tiled=True)  6.32 us
    ppermute x3, starting transfers between devices, shards(): got_pieces = [lax.ppermute(pieces[s], 'x', ring(X, s)) for s in range(1, X)]  5.07 us
    ppermute x3, starting transfers between devices, shards(): lax.ppermute(sums[back], 'y', ring(Y, Y - back))  3.73 us
    pallas_call x1, Pallas kernels, shards(): pl.pallas_call(other_kernel, out_shape=[shape((Y, SUB, PROBES), F32)] + [...  3.59 us
  transfers between devices with their start and end apart: 17, of which 6 were waited for; matrix products, arithmetic and copies ran while one was open for 2% of the time, Pallas kernels for 4%

profile of v7, /device:TPU:1, one launch (start us, length us, event | category | flops | bytes accessed | tf_op | source)
XLA Modules:
  0.0 87.6 jit_solution(3481297610529937002)
XLA Ops:
  1.3 2.0 %pack.1 = (bf16[528,384]{1,0:T(8,128)(2,1)}, bf16[8,128,384]{2,1,0:T(8,128)(2,1)}) custom-call(s32[1]{0:T(128)S(6)} %copy.10.count_hbm, bf16[512,256]{1,0:T(8,128)(2,1)} %factor_hbm.1, bf16[512,128]{1,0:T(8,128)(2,1)} %side_hbm.1, bf16[128,256]{1,0:T(8,128)(2,1)} %cols_hbm.1, bf16[128,128]{1,0:T(8,128)(2,1)} %probe_hbm.1, s32[1,64]{1,0:T(1,128)} %pairs_hbm.1), custom_call_target="tpu_custom_call" | custom-call | tf_op jit(solution)/shard_map/pack/pallas_call | solution.py:161
  3.3 9.2 %all-to-all-start = ((bf16[8,128,384]{2,1,0:T(8,128)(2,1)}), bf16[8,128,384]{2,1,0:T(8,128)(2,1)S(1)}, u32[]{:S(2)}, u32[]{:S(2)}) async-start(bf16[8,128,384]{2,1,0:T(8,128)(2,1)} %get-tuple-element.19), calls=%async_computation | async-start | bytes 1572864 | tf_op jit(solution)/shard_map/all_to_all | solution.py:180
  12.5 1.4 %collective-permute-start = (bf16[528,384]{1,0:T(8,128)(2,1)S(1)}, bf16[528,384]{1,0:T(8,128)(2,1)S(1)}, u32[]{:S(2)}, u32[]{:S(2)}) collective-permute-start(bf16[528,384]{1,0:T(8,128)(2,1)S(1)} %copy-done), channel_id=1, source_target_pairs={{0,64},{64,128},{128,192},{192,0},{1,65},{65,129},{129,193},{193,1... | collective-permute-start | bytes 1216520 | tf_op jit(solution)/shard_map/ppermute | solution.py:177
  13.9 1.5 %collective-permute-start.2 = (bf16[528,384]{1,0:T(8,128)(2,1)S(1)}, bf16[528,384]{1,0:T(8,128)(2,1)S(1)}, u32[]{:S(2)}, u32[]{:S(2)}) collective-permute-start(bf16[528,384]{1,0:T(8,128)(2,1)S(1)} %copy-done), channel_id=1, source_target_pairs={{0,192},{64,0},{128,64},{192,128},{1,193},{65,1},{129,65},{193,129... | collective-permute-start | bytes 1216520 | tf_op jit(solution)/shard_map/ppermute | solution.py:177
  15.4 8.4 %collective-permute-done.rows1 = bf16[528,384]{1,0:T(8,128)(2,1)S(1)} collective-permute-done((bf16[528,384]{1,0:T(8,128)(2,1)S(1)}, bf16[528,384]{1,0:T(8,128)(2,1)S(1)}, u32[]{:S(2)}, u32[]{:S(2)}) %collective-permute-start) | collective-permute-done | bytes 405536 | tf_op jit(solution)/shard_map/ppermute | solution.py:177
  24.0 2.7 %collective-permute-start.3 = (bf16[256,384]{1,0:T(8,128)(2,1)S(1)}, bf16[256,384]{1,0:T(8,128)(2,1)S(1)}, u32[]{:S(2)}, u32[]{:S(2)}) collective-permute-start(bf16[256,384]{1,0:T(8,128)(2,1)S(1)} %slice.21), channel_id=1, source_target_pairs={{0,192},{64,0},{128,64},{192,128},{1,193},{65,1},{129,65},{193,129... | collective-permute-start | bytes 589832 | tf_op jit(solution)/shard_map/ppermute | solution.py:178
  26.7 9.3 %all-to-all-done = bf16[8,128,384]{2,1,0:T(8,128)(2,1)S(1)} async-done(((bf16[8,128,384]{2,1,0:T(8,128)(2,1)}), bf16[8,128,384]{2,1,0:T(8,128)(2,1)S(1)}, u32[]{:S(2)}, u32[]{:S(2)}) %all-to-all-start) | async-done | bytes 786464 | tf_op jit(solution)/shard_map/all_to_all | solution.py:180
  36.8 3.4 %own_tiles.1 = (f32[4,512,128]{2,1,0:T(8,128)S(1)}, f32[8,128,128]{2,1,0:T(8,128)S(1)}, f32[128,128]{1,0:T(8,128)S(1)}) custom-call(bf16[528,384]{1,0:T(8,128)(2,1)S(1)} %copy-done, bf16[528,384]{1,0:T(8,128)(2,1)S(1)} %collective-permute-done.rows1, bf16[272,384]{1,0:T(8,128)(2,1)S(1)} %collective-permute-done.1.far_low, ...), custom_call_target="tpu_custom_call" | custom-call | flops 2147483648 | bytes 4194304 | tf_op jit(solution)/shard_map/own_tiles/pallas_call | solution.py:187
  40.2 3.6 %other_tiles.1 = (f32[4,128,128]{2,1,0:T(8,128)S(1)}, bf16[4,128,128]{2,1,0:T(8,128)(2,1)S(1)}, bf16[4,128,128]{2,1,0:T(8,128)(2,1)S(1)}, bf16[4,128,128]{2,1,0:T(8,128)(2,1)S(1)}, f32[9,128,128]{2,1,0:T(8,128)S(1)}) custom-call(bf16[528,384]{1,0:T(8,128)(2,1)S(1)} %copy-done, bf16[528,384]{1,0:T(8,128)(2,1)S(1)} %collective-permute-done.rows1, ...), custom_call_target="tpu_custom_call" | custom-call | flops 2147483648 | bytes 4194304 | tf_op jit(solution)/shard_map/other_tiles/pallas_call | solution.py:197
  44.3 1.6 %collective-permute-done.9.got_ref = f32[9,128,128]{2,1,0:T(8,128)S(1)} collective-permute-done((f32[9,128,128]{2,1,0:T(8,128)S(1)}, f32[9,128,128]{2,1,0:T(8,128)S(1)}, u32[]{:S(2)}, u32[]{:S(2)}) %collective-permute-start.9) | collective-permute-done | bytes 589856 | tf_op jit(solution)/shard_map/ppermute | solution.py:210
  46.0 0.8 join.1
  46.8 3.5 %all-to-all-start.1 = ((bf16[8,192,128]{2,1,0:T(8,128)(2,1)}), bf16[8,192,128]{2,1,0:T(8,128)(2,1)S(1)}, u32[]{:S(2)}, u32[]{:S(2)}) async-start(bf16[8,192,128]{2,1,0:T(8,128)(2,1)} %join.1), calls=%async_computation.1 | async-start | bytes 786432 | tf_op jit(solution)/shard_map/all_to_all | solution.py:220
  50.2 1.5 %collective-permute-start.6 = (bf16[4,128,128]{2,1,0:T(8,128)(2,1)S(1)}, bf16[4,128,128]{2,1,0:T(8,128)(2,1)S(1)}, u32[]{:S(2)}, u32[]{:S(2)}) collective-permute-start(bf16[4,128,128]{2,1,0:T(8,128)(2,1)S(1)} %get-tuple-element.23), channel_id=1, source_target_pairs={{0,1},{1,2},{2,3},{3,0},{4,5},{5,6},{6,7},{7,4},{8,9},{9,10},{10,1... | collective-permute-start | bytes 393224 | tf_op jit(solution)/shard_map/ppermute | solution.py:211
  51.7 2.5 %collective-permute-start.7 = (bf16[4,128,128]{2,1,0:T(8,128)(2,1)S(1)}, bf16[4,128,128]{2,1,0:T(8,128)(2,1)S(1)}, u32[]{:S(2)}, u32[]{:S(2)}) collective-permute-start(bf16[4,128,128]{2,1,0:T(8,128)(2,1)S(1)} %get-tuple-element.24), channel_id=1, source_target_pairs={{0,2},{1,3},{2,0},{3,1},{4,6},{5,7},{6,4},{7,5},{8,10},{9,11},{10,... | collective-permute-start | bytes 393224 | tf_op jit(solution)/shard_map/ppermute | solution.py:211
  54.2 1.1 %collective-permute-start.8 = (bf16[4,128,128]{2,1,0:T(8,128)(2,1)S(1)}, bf16[4,128,128]{2,1,0:T(8,128)(2,1)S(1)}, u32[]{:S(2)}, u32[]{:S(2)}) collective-permute-start(bf16[4,128,128]{2,1,0:T(8,128)(2,1)S(1)} %get-tuple-element.25), channel_id=1, source_target_pairs={{0,3},{1,0},{2,1},{3,2},{4,7},{5,4},{6,5},{7,6},{8,11},{9,8},{10,9... | collective-permute-start | bytes 393224 | tf_op jit(solution)/shard_map/ppermute | solution.py:211
  55.3 10.0 %all-to-all-done.1 = bf16[8,192,128]{2,1,0:T(8,128)(2,1)S(1)} async-done(((bf16[8,192,128]{2,1,0:T(8,128)(2,1)}), bf16[8,192,128]{2,1,0:T(8,128)(2,1)S(1)}, u32[]{:S(2)}, u32[]{:S(2)}) %all-to-all-start.1) | async-done | bytes 393248 | tf_op jit(solution)/shard_map/all_to_all | solution.py:220
  65.4 0.9 %pieces.1 = (f32[128,128]{1,0:T(8,128)S(1)}, f32[128,128]{1,0:T(8,128)S(1)}, f32[128,128]{1,0:T(8,128)S(1)}, f32[128,128]{1,0:T(8,128)S(1)}, f32[16,64,128]{2,1,0:T(8,128)}) custom-call(f32[4,128,128]{2,1,0:T(8,128)S(1)} %get-tuple-element.22.kept_ref, bf16[4,128,128]{2,1,0:T(8,128)(2,1)S(1)} %collective-permute-done.6.got1, ...), custom_call_target="tpu_custom_call" | custom-call | tf_op jit(solution)/shard_map/pieces/pallas_call | solution.py:225
  66.3 6.7 %all-to-all-start.2 = ((f32[16,64,128]{2,1,0:T(8,128)}), f32[16,64,128]{2,1,0:T(8,128)S(1)}, u32[]{:S(2)}, u32[]{:S(2)}) async-start(f32[16,64,128]{2,1,0:T(8,128)} %get-tuple-element.32), calls=%async_computation.2 | async-start | bytes 1048576 | tf_op jit(solution)/shard_map/all_to_all | solution.py:236
  73.0 2.6 %collective-permute-start.10 = (f32[128,128]{1,0:T(8,128)S(1)}, f32[128,128]{1,0:T(8,128)S(1)}, u32[]{:S(2)}, u32[]{:S(2)}) collective-permute-start(f32[128,128]{1,0:T(8,128)S(1)} %get-tuple-element.29), channel_id=1, source_target_pairs={{0,192},{64,0},{128,64},{192,128},{1,193},{65,1},{129,65},{193,129... | collective-permute-start | bytes 196616 | tf_op jit(solution)/shard_map/ppermute | solution.py:233
  76.8 0.7 copy.9
  77.5 6.3 %all-to-all-done.2 = f32[16,64,128]{2,1,0:T(8,128)S(1)} async-done(((f32[16,64,128]{2,1,0:T(8,128)}), f32[16,64,128]{2,1,0:T(8,128)S(1)}, u32[]{:S(2)}, u32[]{:S(2)}) %all-to-all-start.2) | async-done | bytes 524320 | tf_op jit(solution)/shard_map/all_to_all | solution.py:236
  83.9 1.8 %collective-permute-start.13 = (f32[64,128]{1,0:T(8,128)S(1)}, f32[64,128]{1,0:T(8,128)S(1)}, u32[]{:S(2)}, u32[]{:S(2)}) collective-permute-start(f32[64,128]{1,0:T(8,128)S(1)} %broadcast_multiply_fusion), channel_id=1, source_target_pairs={{0,4},{4,0},{1,5},{5,1},{2,6},{6,2},{3,7},{7,3},{8,12},{12,8},{9,1... | collective-permute-start | bytes 98312 | tf_op jit(solution)/shard_map/ppermute | solution.py:238
  86.3 0.6 add_multiply_fusion
  86.9 0.6 pad_maximum_fusion
  (28 shorter events, 3.2 us)
Async XLA Ops:
  3.3 9.2 %copy-start = (bf16[528,384]{1,0:T(8,128)(2,1)S(1)}, bf16[528,384]{1,0:T(8,128)(2,1)}, u32[]{:S(2)}) copy-start(bf16[528,384]{1,0:T(8,128)(2,1)} %get-tuple-element.18.rows0) | copy-start | bytes 1216516
  3.3 32.7 %all-to-all-start = ((bf16[8,128,384]{2,1,0:T(8,128)(2,1)}), bf16[8,128,384]{2,1,0:T(8,128)(2,1)S(1)}, u32[]{:S(2)}, u32[]{:S(2)}) async-start(bf16[8,128,384]{2,1,0:T(8,128)(2,1)} %get-tuple-element.19), calls=%async_computation | async-start | bytes 1572864 | tf_op jit(solution)/shard_map/all_to_all | solution.py:180
  12.5 11.3 %collective-permute-start = (bf16[528,384]{1,0:T(8,128)(2,1)S(1)}, bf16[528,384]{1,0:T(8,128)(2,1)S(1)}, u32[]{:S(2)}, u32[]{:S(2)}) collective-permute-start(bf16[528,384]{1,0:T(8,128)(2,1)S(1)} %copy-done), channel_id=1, source_target_pairs={{0,64},{64,128},{128,192},{192,0},{1,65},{65,129},{129,193},{193,1... | collective-permute-start | bytes 1216520 | tf_op jit(solution)/shard_map/ppermute | solution.py:177
  13.9 10.1 %collective-permute-start.2 = (bf16[528,384]{1,0:T(8,128)(2,1)S(1)}, bf16[528,384]{1,0:T(8,128)(2,1)S(1)}, u32[]{:S(2)}, u32[]{:S(2)}) collective-permute-start(bf16[528,384]{1,0:T(8,128)(2,1)S(1)} %copy-done), channel_id=1, source_target_pairs={{0,192},{64,0},{128,64},{192,128},{1,193},{65,1},{129,65},{193,129... | collective-permute-start | bytes 1216520 | tf_op jit(solution)/shard_map/ppermute | solution.py:177
  23.8 13.0 %collective-permute-start.1 = (bf16[272,384]{1,0:T(8,128)(2,1)S(1)}, bf16[272,384]{1,0:T(8,128)(2,1)S(1)}, u32[]{:S(2)}, u32[]{:S(2)}) collective-permute-start(bf16[272,384]{1,0:T(8,128)(2,1)S(1)} %slice.20), channel_id=1, source_target_pairs={{0,64},{64,128},{128,192},{192,0},{1,65},{65,129},{129,193},{193,1... | collective-permute-start | bytes 626696 | tf_op jit(solution)/shard_map/ppermute | solution.py:178
  24.0 12.8 %collective-permute-start.3 = (bf16[256,384]{1,0:T(8,128)(2,1)S(1)}, bf16[256,384]{1,0:T(8,128)(2,1)S(1)}, u32[]{:S(2)}, u32[]{:S(2)}) collective-permute-start(bf16[256,384]{1,0:T(8,128)(2,1)S(1)} %slice.21), channel_id=1, source_target_pairs={{0,192},{64,0},{128,64},{192,128},{1,193},{65,1},{129,65},{193,129... | collective-permute-start | bytes 589832 | tf_op jit(solution)/shard_map/ppermute | solution.py:178
  36.1 4.1 %collective-permute-start.4 = (bf16[4,128,384]{2,1,0:T(8,128)(2,1)S(1)}, bf16[4,128,384]{2,1,0:T(8,128)(2,1)S(1)}, u32[]{:S(2)}, u32[]{:S(2)}) collective-permute-start(bf16[4,128,384]{2,1,0:T(8,128)(2,1)S(1)} %get-tuple-element.37.low_ref), channel_id=1, source_target_pairs={{0,4},{4,0},{1,5},{5,1},{2,6},{6,2},{3,7},{7,3},{8,12},{12,8},{9,1... | collective-permute-start | bytes 1179656 | tf_op jit(solution)/shard_map/ppermute | solution.py:182
  36.7 3.5 %collective-permute-start.5 = (bf16[4,128,384]{2,1,0:T(8,128)(2,1)S(1)}, bf16[4,128,384]{2,1,0:T(8,128)(2,1)S(1)}, u32[]{:S(2)}, u32[]{:S(2)}) collective-permute-start(bf16[4,128,384]{2,1,0:T(8,128)(2,1)S(1)} %get-tuple-element.36.high_ref), channel_id=1, source_target_pairs={{0,4},{4,0},{1,5},{5,1},{2,6},{6,2},{3,7},{7,3},{8,12},{12,8},{9,1... | collective-permute-start | bytes 1179656 | tf_op jit(solution)/shard_map/ppermute | solution.py:182
  43.8 2.1 %collective-permute-start.9 = (f32[9,128,128]{2,1,0:T(8,128)S(1)}, f32[9,128,128]{2,1,0:T(8,128)S(1)}, u32[]{:S(2)}, u32[]{:S(2)}) collective-permute-start(f32[9,128,128]{2,1,0:T(8,128)S(1)} %get-tuple-element.27.sent_ref), channel_id=1, source_target_pairs={{0,4},{4,0},{1,5},{5,1},{2,6},{6,2},{3,7},{7,3},{8,12},{12,8},{9,1... | collective-permute-start | bytes 1769480 | tf_op jit(solution)/shard_map/ppermute | solution.py:210
  46.8 18.5 %all-to-all-start.1 = ((bf16[8,192,128]{2,1,0:T(8,128)(2,1)}), bf16[8,192,128]{2,1,0:T(8,128)(2,1)S(1)}, u32[]{:S(2)}, u32[]{:S(2)}) async-start(bf16[8,192,128]{2,1,0:T(8,128)(2,1)} %join.1), calls=%async_computation.1 | async-start | bytes 786432 | tf_op jit(solution)/shard_map/all_to_all | solution.py:220
  50.2 15.1 %collective-permute-start.6 = (bf16[4,128,128]{2,1,0:T(8,128)(2,1)S(1)}, bf16[4,128,128]{2,1,0:T(8,128)(2,1)S(1)}, u32[]{:S(2)}, u32[]{:S(2)}) collective-permute-start(bf16[4,128,128]{2,1,0:T(8,128)(2,1)S(1)} %get-tuple-element.23), channel_id=1, source_target_pairs={{0,1},{1,2},{2,3},{3,0},{4,5},{5,6},{6,7},{7,4},{8,9},{9,10},{10,1... | collective-permute-start | bytes 393224 | tf_op jit(solution)/shard_map/ppermute | solution.py:211
  51.7 13.7 %collective-permute-start.7 = (bf16[4,128,128]{2,1,0:T(8,128)(2,1)S(1)}, bf16[4,128,128]{2,1,0:T(8,128)(2,1)S(1)}, u32[]{:S(2)}, u32[]{:S(2)}) collective-permute-start(bf16[4,128,128]{2,1,0:T(8,128)(2,1)S(1)} %get-tuple-element.24), channel_id=1, source_target_pairs={{0,2},{1,3},{2,0},{3,1},{4,6},{5,7},{6,4},{7,5},{8,10},{9,11},{10,... | collective-permute-start | bytes 393224 | tf_op jit(solution)/shard_map/ppermute | solution.py:211
  54.2 11.2 %collective-permute-start.8 = (bf16[4,128,128]{2,1,0:T(8,128)(2,1)S(1)}, bf16[4,128,128]{2,1,0:T(8,128)(2,1)S(1)}, u32[]{:S(2)}, u32[]{:S(2)}) collective-permute-start(bf16[4,128,128]{2,1,0:T(8,128)(2,1)S(1)} %get-tuple-element.25), channel_id=1, source_target_pairs={{0,3},{1,0},{2,1},{3,2},{4,7},{5,4},{6,5},{7,6},{8,11},{9,8},{10,9... | collective-permute-start | bytes 393224 | tf_op jit(solution)/shard_map/ppermute | solution.py:211
  66.3 17.6 %all-to-all-start.2 = ((f32[16,64,128]{2,1,0:T(8,128)}), f32[16,64,128]{2,1,0:T(8,128)S(1)}, u32[]{:S(2)}, u32[]{:S(2)}) async-start(f32[16,64,128]{2,1,0:T(8,128)} %get-tuple-element.32), calls=%async_computation.2 | async-start | bytes 1048576 | tf_op jit(solution)/shard_map/all_to_all | solution.py:236
  73.0 12.7 %collective-permute-start.10 = (f32[128,128]{1,0:T(8,128)S(1)}, f32[128,128]{1,0:T(8,128)S(1)}, u32[]{:S(2)}, u32[]{:S(2)}) collective-permute-start(f32[128,128]{1,0:T(8,128)S(1)} %get-tuple-element.29), channel_id=1, source_target_pairs={{0,192},{64,0},{128,64},{192,128},{1,193},{65,1},{129,65},{193,129... | collective-permute-start | bytes 196616 | tf_op jit(solution)/shard_map/ppermute | solution.py:233
  75.6 10.1 %collective-permute-start.11 = (f32[128,128]{1,0:T(8,128)S(1)}, f32[128,128]{1,0:T(8,128)S(1)}, u32[]{:S(2)}, u32[]{:S(2)}) collective-permute-start(f32[128,128]{1,0:T(8,128)S(1)} %get-tuple-element.30), channel_id=1, source_target_pairs={{0,128},{64,192},{128,0},{192,64},{1,129},{65,193},{129,1},{193,65... | collective-permute-start | bytes 196616 | tf_op jit(solution)/shard_map/ppermute | solution.py:233
  76.2 10.1 %collective-permute-start.12 = (f32[128,128]{1,0:T(8,128)S(1)}, f32[128,128]{1,0:T(8,128)S(1)}, u32[]{:S(2)}, u32[]{:S(2)}) collective-permute-start(f32[128,128]{1,0:T(8,128)S(1)} %get-tuple-element.31), channel_id=1, source_target_pairs={{0,64},{64,128},{128,192},{192,0},{1,65},{65,129},{129,193},{193,1... | collective-permute-start | bytes 196616 | tf_op jit(solution)/shard_map/ppermute | solution.py:233
  83.9 3.0 %collective-permute-start.13 = (f32[64,128]{1,0:T(8,128)S(1)}, f32[64,128]{1,0:T(8,128)S(1)}, u32[]{:S(2)}, u32[]{:S(2)}) collective-permute-start(f32[64,128]{1,0:T(8,128)S(1)} %broadcast_multiply_fusion), channel_id=1, source_target_pairs={{0,4},{4,0},{1,5},{5,1},{2,6},{6,2},{3,7},{7,3},{8,12},{12,8},{9,1... | collective-permute-start | bytes 98312 | tf_op jit(solution)/shard_map/ppermute | solution.py:238

commit v8 on v7

--- a/solution.py
+++ b/solution.py
@@ -21,7 +21,7 @@
 TERMS = 1
 SENT = SUB + TERMS * PROBES // C
 SCALE = 1.0 / math.sqrt(NODES)
-LIMIT = 40 * 2**20
+LIMIT = 24 * 2**20
 WHOLE = 60 * 2**20
 SWAP = [(0, 1), (1, 0)]
 

time: 87.9 us -> 87.9 us (level)
  no operation moved by 1% of the time
where the time goes in v8:
time: 87.9 us; the launch traced here: 87.6 us
  starting transfers between devices  36.9 us (42%)
  waiting for transfers between devices  36.3 us (41%)
  Pallas kernels  10.7 us (12%)
  between operations  1.43 us (2%)
  other arithmetic  1.39 us (2%)
    all_to_all x2, waiting for transfers between devices, shards(): lax.all_to_all(col_load, 'z', split_axis=0, concat_axis=0, tiled=True)  19.3 us
    all_to_all x2, starting transfers between devices, shards(): lax.all_to_all(col_load, 'z', split_axis=0, concat_axis=0, tiled=True)  12.6 us
    ppermute x2, waiting for transfers between devices, shards(): near = [lax.ppermute(row_load, 'y', ring(Y, s)) for s in (1, 3)]  8.45 us
    all_to_all x1, starting transfers between devices, shards(): lax.all_to_all(gram, ('y', 'x'), split_axis=0, concat_axis=0, tiled=True)  6.75 us
    all_to_all x1, waiting for transfers between devices, shards(): lax.all_to_all(gram, ('y', 'x'), split_axis=0, concat_axis=0, tiled=True)  6.32 us
    ppermute x3, starting transfers between devices, shards(): got_pieces = [lax.ppermute(pieces[s], 'x', ring(X, s)) for s in range(1, X)]  5.07 us
    ppermute x3, starting transfers between devices, shards(): lax.ppermute(sums[back], 'y', ring(Y, Y - back))  3.73 us
    pallas_call x1, Pallas kernels, shards(): pl.pallas_call(other_kernel, out_shape=[shape((Y, SUB, PROBES), F32)] + [...  3.59 us
  transfers between devices with their start and end apart: 17, of which 6 were waited for; matrix products, arithmetic and copies ran while one was open for 2% of the time, Pallas kernels for 4%

profile of v8, /device:TPU:1, one launch (start us, length us, event | category | flops | bytes accessed | tf_op | source)
XLA Modules:
  0.0 87.6 jit_solution(7748279987727312114)
XLA Ops:
  1.3 2.0 %pack.1 = (bf16[528,384]{1,0:T(8,128)(2,1)}, bf16[8,128,384]{2,1,0:T(8,128)(2,1)}) custom-call(s32[1]{0:T(128)S(6)} %copy.10.count_hbm, bf16[512,256]{1,0:T(8,128)(2,1)} %factor_hbm.1, bf16[512,128]{1,0:T(8,128)(2,1)} %side_hbm.1, bf16[128,256]{1,0:T(8,128)(2,1)} %cols_hbm.1, bf16[128,128]{1,0:T(8,128)(2,1)} %probe_hbm.1, s32[1,64]{1,0:T(1,128)} %pairs_hbm.1), custom_call_target="tpu_custom_call" | custom-call | tf_op jit(solution)/shard_map/pack/pallas_call | solution.py:161
  3.3 9.2 %all-to-all-start = ((bf16[8,128,384]{2,1,0:T(8,128)(2,1)}), bf16[8,128,384]{2,1,0:T(8,128)(2,1)S(1)}, u32[]{:S(2)}, u32[]{:S(2)}) async-start(bf16[8,128,384]{2,1,0:T(8,128)(2,1)} %get-tuple-element.19), calls=%async_computation | async-start | bytes 1572864 | tf_op jit(solution)/shard_map/all_to_all | solution.py:180
  12.5 1.4 %collective-permute-start = (bf16[528,384]{1,0:T(8,128)(2,1)S(1)}, bf16[528,384]{1,0:T(8,128)(2,1)S(1)}, u32[]{:S(2)}, u32[]{:S(2)}) collective-permute-start(bf16[528,384]{1,0:T(8,128)(2,1)S(1)} %copy-done), channel_id=1, source_target_pairs={{0,64},{64,128},{128,192},{192,0},{1,65},{65,129},{129,193},{193,1... | collective-permute-start | bytes 1216520 | tf_op jit(solution)/shard_map/ppermute | solution.py:177
  13.9 1.5 %collective-permute-start.2 = (bf16[528,384]{1,0:T(8,128)(2,1)S(1)}, bf16[528,384]{1,0:T(8,128)(2,1)S(1)}, u32[]{:S(2)}, u32[]{:S(2)}) collective-permute-start(bf16[528,384]{1,0:T(8,128)(2,1)S(1)} %copy-done), channel_id=1, source_target_pairs={{0,192},{64,0},{128,64},{192,128},{1,193},{65,1},{129,65},{193,129... | collective-permute-start | bytes 1216520 | tf_op jit(solution)/shard_map/ppermute | solution.py:177
  15.4 8.4 %collective-permute-done.rows1 = bf16[528,384]{1,0:T(8,128)(2,1)S(1)} collective-permute-done((bf16[528,384]{1,0:T(8,128)(2,1)S(1)}, bf16[528,384]{1,0:T(8,128)(2,1)S(1)}, u32[]{:S(2)}, u32[]{:S(2)}) %collective-permute-start) | collective-permute-done | bytes 405536 | tf_op jit(solution)/shard_map/ppermute | solution.py:177
  24.0 2.7 %collective-permute-start.3 = (bf16[256,384]{1,0:T(8,128)(2,1)S(1)}, bf16[256,384]{1,0:T(8,128)(2,1)S(1)}, u32[]{:S(2)}, u32[]{:S(2)}) collective-permute-start(bf16[256,384]{1,0:T(8,128)(2,1)S(1)} %slice.21), channel_id=1, source_target_pairs={{0,192},{64,0},{128,64},{192,128},{1,193},{65,1},{129,65},{193,129... | collective-permute-start | bytes 589832 | tf_op jit(solution)/shard_map/ppermute | solution.py:178
  26.7 9.3 %all-to-all-done = bf16[8,128,384]{2,1,0:T(8,128)(2,1)S(1)} async-done(((bf16[8,128,384]{2,1,0:T(8,128)(2,1)}), bf16[8,128,384]{2,1,0:T(8,128)(2,1)S(1)}, u32[]{:S(2)}, u32[]{:S(2)}) %all-to-all-start) | async-done | bytes 786464 | tf_op jit(solution)/shard_map/all_to_all | solution.py:180
  36.8 3.4 %own_tiles.1 = (f32[4,512,128]{2,1,0:T(8,128)S(1)}, f32[8,128,128]{2,1,0:T(8,128)S(1)}, f32[128,128]{1,0:T(8,128)S(1)}) custom-call(bf16[528,384]{1,0:T(8,128)(2,1)S(1)} %copy-done, bf16[528,384]{1,0:T(8,128)(2,1)S(1)} %collective-permute-done.rows1, bf16[272,384]{1,0:T(8,128)(2,1)S(1)} %collective-permute-done.1.far_low, ...), custom_call_target="tpu_custom_call" | custom-call | flops 2147483648 | bytes 4194304 | tf_op jit(solution)/shard_map/own_tiles/pallas_call | solution.py:187
  40.2 3.6 %other_tiles.1 = (f32[4,128,128]{2,1,0:T(8,128)S(1)}, bf16[4,128,128]{2,1,0:T(8,128)(2,1)S(1)}, bf16[4,128,128]{2,1,0:T(8,128)(2,1)S(1)}, bf16[4,128,128]{2,1,0:T(8,128)(2,1)S(1)}, f32[9,128,128]{2,1,0:T(8,128)S(1)}) custom-call(bf16[528,384]{1,0:T(8,128)(2,1)S(1)} %copy-done, bf16[528,384]{1,0:T(8,128)(2,1)S(1)} %collective-permute-done.rows1, ...), custom_call_target="tpu_custom_call" | custom-call | flops 2147483648 | bytes 4194304 | tf_op jit(solution)/shard_map/other_tiles/pallas_call | solution.py:197
  44.3 1.6 %collective-permute-done.9.got_ref = f32[9,128,128]{2,1,0:T(8,128)S(1)} collective-permute-done((f32[9,128,128]{2,1,0:T(8,128)S(1)}, f32[9,128,128]{2,1,0:T(8,128)S(1)}, u32[]{:S(2)}, u32[]{:S(2)}) %collective-permute-start.9) | collective-permute-done | bytes 589856 | tf_op jit(solution)/shard_map/ppermute | solution.py:210
  46.0 0.8 join.1
  46.8 3.5 %all-to-all-start.1 = ((bf16[8,192,128]{2,1,0:T(8,128)(2,1)}), bf16[8,192,128]{2,1,0:T(8,128)(2,1)S(1)}, u32[]{:S(2)}, u32[]{:S(2)}) async-start(bf16[8,192,128]{2,1,0:T(8,128)(2,1)} %join.1), calls=%async_computation.1 | async-start | bytes 786432 | tf_op jit(solution)/shard_map/all_to_all | solution.py:220
  50.2 1.5 %collective-permute-start.6 = (bf16[4,128,128]{2,1,0:T(8,128)(2,1)S(1)}, bf16[4,128,128]{2,1,0:T(8,128)(2,1)S(1)}, u32[]{:S(2)}, u32[]{:S(2)}) collective-permute-start(bf16[4,128,128]{2,1,0:T(8,128)(2,1)S(1)} %get-tuple-element.23), channel_id=1, source_target_pairs={{0,1},{1,2},{2,3},{3,0},{4,5},{5,6},{6,7},{7,4},{8,9},{9,10},{10,1... | collective-permute-start | bytes 393224 | tf_op jit(solution)/shard_map/ppermute | solution.py:211
  51.7 2.5 %collective-permute-start.7 = (bf16[4,128,128]{2,1,0:T(8,128)(2,1)S(1)}, bf16[4,128,128]{2,1,0:T(8,128)(2,1)S(1)}, u32[]{:S(2)}, u32[]{:S(2)}) collective-permute-start(bf16[4,128,128]{2,1,0:T(8,128)(2,1)S(1)} %get-tuple-element.24), channel_id=1, source_target_pairs={{0,2},{1,3},{2,0},{3,1},{4,6},{5,7},{6,4},{7,5},{8,10},{9,11},{10,... | collective-permute-start | bytes 393224 | tf_op jit(solution)/shard_map/ppermute | solution.py:211
  54.2 1.1 %collective-permute-start.8 = (bf16[4,128,128]{2,1,0:T(8,128)(2,1)S(1)}, bf16[4,128,128]{2,1,0:T(8,128)(2,1)S(1)}, u32[]{:S(2)}, u32[]{:S(2)}) collective-permute-start(bf16[4,128,128]{2,1,0:T(8,128)(2,1)S(1)} %get-tuple-element.25), channel_id=1, source_target_pairs={{0,3},{1,0},{2,1},{3,2},{4,7},{5,4},{6,5},{7,6},{8,11},{9,8},{10,9... | collective-permute-start | bytes 393224 | tf_op jit(solution)/shard_map/ppermute | solution.py:211
  55.3 10.0 %all-to-all-done.1 = bf16[8,192,128]{2,1,0:T(8,128)(2,1)S(1)} async-done(((bf16[8,192,128]{2,1,0:T(8,128)(2,1)}), bf16[8,192,128]{2,1,0:T(8,128)(2,1)S(1)}, u32[]{:S(2)}, u32[]{:S(2)}) %all-to-all-start.1) | async-done | bytes 393248 | tf_op jit(solution)/shard_map/all_to_all | solution.py:220
  65.4 0.9 %pieces.1 = (f32[128,128]{1,0:T(8,128)S(1)}, f32[128,128]{1,0:T(8,128)S(1)}, f32[128,128]{1,0:T(8,128)S(1)}, f32[128,128]{1,0:T(8,128)S(1)}, f32[16,64,128]{2,1,0:T(8,128)}) custom-call(f32[4,128,128]{2,1,0:T(8,128)S(1)} %get-tuple-element.22.kept_ref, bf16[4,128,128]{2,1,0:T(8,128)(2,1)S(1)} %collective-permute-done.6.got1, ...), custom_call_target="tpu_custom_call" | custom-call | tf_op jit(solution)/shard_map/pieces/pallas_call | solution.py:225
  66.3 6.7 %all-to-all-start.2 = ((f32[16,64,128]{2,1,0:T(8,128)}), f32[16,64,128]{2,1,0:T(8,128)S(1)}, u32[]{:S(2)}, u32[]{:S(2)}) async-start(f32[16,64,128]{2,1,0:T(8,128)} %get-tuple-element.32), calls=%async_computation.2 | async-start | bytes 1048576 | tf_op jit(solution)/shard_map/all_to_all | solution.py:236
  73.0 2.6 %collective-permute-start.10 = (f32[128,128]{1,0:T(8,128)S(1)}, f32[128,128]{1,0:T(8,128)S(1)}, u32[]{:S(2)}, u32[]{:S(2)}) collective-permute-start(f32[128,128]{1,0:T(8,128)S(1)} %get-tuple-element.29), channel_id=1, source_target_pairs={{0,192},{64,0},{128,64},{192,128},{1,193},{65,1},{129,65},{193,129... | collective-permute-start | bytes 196616 | tf_op jit(solution)/shard_map/ppermute | solution.py:233
  76.8 0.7 copy.9
  77.5 6.3 %all-to-all-done.2 = f32[16,64,128]{2,1,0:T(8,128)S(1)} async-done(((f32[16,64,128]{2,1,0:T(8,128)}), f32[16,64,128]{2,1,0:T(8,128)S(1)}, u32[]{:S(2)}, u32[]{:S(2)}) %all-to-all-start.2) | async-done | bytes 524320 | tf_op jit(solution)/shard_map/all_to_all | solution.py:236
  83.9 1.8 %collective-permute-start.13 = (f32[64,128]{1,0:T(8,128)S(1)}, f32[64,128]{1,0:T(8,128)S(1)}, u32[]{:S(2)}, u32[]{:S(2)}) collective-permute-start(f32[64,128]{1,0:T(8,128)S(1)} %broadcast_multiply_fusion), channel_id=1, source_target_pairs={{0,4},{4,0},{1,5},{5,1},{2,6},{6,2},{3,7},{7,3},{8,12},{12,8},{9,1... | collective-permute-start | bytes 98312 | tf_op jit(solution)/shard_map/ppermute | solution.py:238
  86.3 0.6 add_multiply_fusion
  86.9 0.6 pad_maximum_fusion
  (28 shorter events, 3.2 us)
Async XLA Ops:
  3.3 9.2 %copy-start = (bf16[528,384]{1,0:T(8,128)(2,1)S(1)}, bf16[528,384]{1,0:T(8,128)(2,1)}, u32[]{:S(2)}) copy-start(bf16[528,384]{1,0:T(8,128)(2,1)} %get-tuple-element.18.rows0) | copy-start | bytes 1216516
  3.3 32.7 %all-to-all-start = ((bf16[8,128,384]{2,1,0:T(8,128)(2,1)}), bf16[8,128,384]{2,1,0:T(8,128)(2,1)S(1)}, u32[]{:S(2)}, u32[]{:S(2)}) async-start(bf16[8,128,384]{2,1,0:T(8,128)(2,1)} %get-tuple-element.19), calls=%async_computation | async-start | bytes 1572864 | tf_op jit(solution)/shard_map/all_to_all | solution.py:180
  12.5 11.3 %collective-permute-start = (bf16[528,384]{1,0:T(8,128)(2,1)S(1)}, bf16[528,384]{1,0:T(8,128)(2,1)S(1)}, u32[]{:S(2)}, u32[]{:S(2)}) collective-permute-start(bf16[528,384]{1,0:T(8,128)(2,1)S(1)} %copy-done), channel_id=1, source_target_pairs={{0,64},{64,128},{128,192},{192,0},{1,65},{65,129},{129,193},{193,1... | collective-permute-start | bytes 1216520 | tf_op jit(solution)/shard_map/ppermute | solution.py:177
  13.9 10.1 %collective-permute-start.2 = (bf16[528,384]{1,0:T(8,128)(2,1)S(1)}, bf16[528,384]{1,0:T(8,128)(2,1)S(1)}, u32[]{:S(2)}, u32[]{:S(2)}) collective-permute-start(bf16[528,384]{1,0:T(8,128)(2,1)S(1)} %copy-done), channel_id=1, source_target_pairs={{0,192},{64,0},{128,64},{192,128},{1,193},{65,1},{129,65},{193,129... | collective-permute-start | bytes 1216520 | tf_op jit(solution)/shard_map/ppermute | solution.py:177
  23.8 13.0 %collective-permute-start.1 = (bf16[272,384]{1,0:T(8,128)(2,1)S(1)}, bf16[272,384]{1,0:T(8,128)(2,1)S(1)}, u32[]{:S(2)}, u32[]{:S(2)}) collective-permute-start(bf16[272,384]{1,0:T(8,128)(2,1)S(1)} %slice.20), channel_id=1, source_target_pairs={{0,64},{64,128},{128,192},{192,0},{1,65},{65,129},{129,193},{193,1... | collective-permute-start | bytes 626696 | tf_op jit(solution)/shard_map/ppermute | solution.py:178
  24.0 12.8 %collective-permute-start.3 = (bf16[256,384]{1,0:T(8,128)(2,1)S(1)}, bf16[256,384]{1,0:T(8,128)(2,1)S(1)}, u32[]{:S(2)}, u32[]{:S(2)}) collective-permute-start(bf16[256,384]{1,0:T(8,128)(2,1)S(1)} %slice.21), channel_id=1, source_target_pairs={{0,192},{64,0},{128,64},{192,128},{1,193},{65,1},{129,65},{193,129... | collective-permute-start | bytes 589832 | tf_op jit(solution)/shard_map/ppermute | solution.py:178
  36.1 4.1 %collective-permute-start.4 = (bf16[4,128,384]{2,1,0:T(8,128)(2,1)S(1)}, bf16[4,128,384]{2,1,0:T(8,128)(2,1)S(1)}, u32[]{:S(2)}, u32[]{:S(2)}) collective-permute-start(bf16[4,128,384]{2,1,0:T(8,128)(2,1)S(1)} %get-tuple-element.37.low_ref), channel_id=1, source_target_pairs={{0,4},{4,0},{1,5},{5,1},{2,6},{6,2},{3,7},{7,3},{8,12},{12,8},{9,1... | collective-permute-start | bytes 1179656 | tf_op jit(solution)/shard_map/ppermute | solution.py:182
  36.7 3.5 %collective-permute-start.5 = (bf16[4,128,384]{2,1,0:T(8,128)(2,1)S(1)}, bf16[4,128,384]{2,1,0:T(8,128)(2,1)S(1)}, u32[]{:S(2)}, u32[]{:S(2)}) collective-permute-start(bf16[4,128,384]{2,1,0:T(8,128)(2,1)S(1)} %get-tuple-element.36.high_ref), channel_id=1, source_target_pairs={{0,4},{4,0},{1,5},{5,1},{2,6},{6,2},{3,7},{7,3},{8,12},{12,8},{9,1... | collective-permute-start | bytes 1179656 | tf_op jit(solution)/shard_map/ppermute | solution.py:182
  43.8 2.1 %collective-permute-start.9 = (f32[9,128,128]{2,1,0:T(8,128)S(1)}, f32[9,128,128]{2,1,0:T(8,128)S(1)}, u32[]{:S(2)}, u32[]{:S(2)}) collective-permute-start(f32[9,128,128]{2,1,0:T(8,128)S(1)} %get-tuple-element.27.sent_ref), channel_id=1, source_target_pairs={{0,4},{4,0},{1,5},{5,1},{2,6},{6,2},{3,7},{7,3},{8,12},{12,8},{9,1... | collective-permute-start | bytes 1769480 | tf_op jit(solution)/shard_map/ppermute | solution.py:210
  46.8 18.5 %all-to-all-start.1 = ((bf16[8,192,128]{2,1,0:T(8,128)(2,1)}), bf16[8,192,128]{2,1,0:T(8,128)(2,1)S(1)}, u32[]{:S(2)}, u32[]{:S(2)}) async-start(bf16[8,192,128]{2,1,0:T(8,128)(2,1)} %join.1), calls=%async_computation.1 | async-start | bytes 786432 | tf_op jit(solution)/shard_map/all_to_all | solution.py:220
  50.2 15.1 %collective-permute-start.6 = (bf16[4,128,128]{2,1,0:T(8,128)(2,1)S(1)}, bf16[4,128,128]{2,1,0:T(8,128)(2,1)S(1)}, u32[]{:S(2)}, u32[]{:S(2)}) collective-permute-start(bf16[4,128,128]{2,1,0:T(8,128)(2,1)S(1)} %get-tuple-element.23), channel_id=1, source_target_pairs={{0,1},{1,2},{2,3},{3,0},{4,5},{5,6},{6,7},{7,4},{8,9},{9,10},{10,1... | collective-permute-start | bytes 393224 | tf_op jit(solution)/shard_map/ppermute | solution.py:211
  51.7 13.7 %collective-permute-start.7 = (bf16[4,128,128]{2,1,0:T(8,128)(2,1)S(1)}, bf16[4,128,128]{2,1,0:T(8,128)(2,1)S(1)}, u32[]{:S(2)}, u32[]{:S(2)}) collective-permute-start(bf16[4,128,128]{2,1,0:T(8,128)(2,1)S(1)} %get-tuple-element.24), channel_id=1, source_target_pairs={{0,2},{1,3},{2,0},{3,1},{4,6},{5,7},{6,4},{7,5},{8,10},{9,11},{10,... | collective-permute-start | bytes 393224 | tf_op jit(solution)/shard_map/ppermute | solution.py:211
  54.2 11.2 %collective-permute-start.8 = (bf16[4,128,128]{2,1,0:T(8,128)(2,1)S(1)}, bf16[4,128,128]{2,1,0:T(8,128)(2,1)S(1)}, u32[]{:S(2)}, u32[]{:S(2)}) collective-permute-start(bf16[4,128,128]{2,1,0:T(8,128)(2,1)S(1)} %get-tuple-element.25), channel_id=1, source_target_pairs={{0,3},{1,0},{2,1},{3,2},{4,7},{5,4},{6,5},{7,6},{8,11},{9,8},{10,9... | collective-permute-start | bytes 393224 | tf_op jit(solution)/shard_map/ppermute | solution.py:211
  66.3 17.6 %all-to-all-start.2 = ((f32[16,64,128]{2,1,0:T(8,128)}), f32[16,64,128]{2,1,0:T(8,128)S(1)}, u32[]{:S(2)}, u32[]{:S(2)}) async-start(f32[16,64,128]{2,1,0:T(8,128)} %get-tuple-element.32), calls=%async_computation.2 | async-start | bytes 1048576 | tf_op jit(solution)/shard_map/all_to_all | solution.py:236
  73.0 12.7 %collective-permute-start.10 = (f32[128,128]{1,0:T(8,128)S(1)}, f32[128,128]{1,0:T(8,128)S(1)}, u32[]{:S(2)}, u32[]{:S(2)}) collective-permute-start(f32[128,128]{1,0:T(8,128)S(1)} %get-tuple-element.29), channel_id=1, source_target_pairs={{0,192},{64,0},{128,64},{192,128},{1,193},{65,1},{129,65},{193,129... | collective-permute-start | bytes 196616 | tf_op jit(solution)/shard_map/ppermute | solution.py:233
  75.6 10.1 %collective-permute-start.11 = (f32[128,128]{1,0:T(8,128)S(1)}, f32[128,128]{1,0:T(8,128)S(1)}, u32[]{:S(2)}, u32[]{:S(2)}) collective-permute-start(f32[128,128]{1,0:T(8,128)S(1)} %get-tuple-element.30), channel_id=1, source_target_pairs={{0,128},{64,192},{128,0},{192,64},{1,129},{65,193},{129,1},{193,65... | collective-permute-start | bytes 196616 | tf_op jit(solution)/shard_map/ppermute | solution.py:233
  76.2 10.1 %collective-permute-start.12 = (f32[128,128]{1,0:T(8,128)S(1)}, f32[128,128]{1,0:T(8,128)S(1)}, u32[]{:S(2)}, u32[]{:S(2)}) collective-permute-start(f32[128,128]{1,0:T(8,128)S(1)} %get-tuple-element.31), channel_id=1, source_target_pairs={{0,64},{64,128},{128,192},{192,0},{1,65},{65,129},{129,193},{193,1... | collective-permute-start | bytes 196616 | tf_op jit(solution)/shard_map/ppermute | solution.py:233
  83.9 3.0 %collective-permute-start.13 = (f32[64,128]{1,0:T(8,128)S(1)}, f32[64,128]{1,0:T(8,128)S(1)}, u32[]{:S(2)}, u32[]{:S(2)}) collective-permute-start(f32[64,128]{1,0:T(8,128)S(1)} %broadcast_multiply_fusion), channel_id=1, source_target_pairs={{0,4},{4,0},{1,5},{5,1},{2,6},{6,2},{3,7},{7,3},{8,12},{12,8},{9,1... | collective-permute-start | bytes 98312 | tf_op jit(solution)/shard_map/ppermute | solution.py:238
